TPU v7x, 32 devices: a whole 2x2x4 slice. The times are simulated.
32 devices in a mesh: blk: 8 (over y, x, core), head: 4 (over z).
Axes of the slice: x: 2, y: 2, z: 4, core: 2. Of those that a mesh axis runs over, the one named last changes fastest.
Arguments:
- tokens: bfloat16 [3072, 1024], P(('blk', 'head')), may hold values from -18 to 18
- block_order: int32 [16], replicated, may hold values from 0 to 15, as said below
- request_lengths: int32 [9], replicated, may hold values from 1 to 2304, 3072 in all
- enc_lengths: int32 [9], replicated, may hold values from 1 to 512, 2048 in all
- w_qkv: bfloat16 [3, 1024, 1024], P(None, None, 'head'), may hold values from -0.1875 to 0.1875
- w_out: bfloat16 [1024, 1024], P('head'), may hold values from -0.1875 to 0.1875
- enc_kv: bfloat16 [2, 2048, 1024], P(None, 'blk', 'head'), may hold values from -18 to 18
- w_cq: bfloat16 [1024, 1024], replicated, may hold values from -0.1875 to 0.1875
- w_co: bfloat16 [1024, 1024], replicated, may hold values from -0.1875 to 0.1875
- w_up: bfloat16 [1024, 4096], replicated, may hold values from -0.1875 to 0.1875
- w_down: bfloat16 [4096, 1024], replicated, may hold values from -0.09375 to 0.09375
- w_next: bfloat16 [3, 1024, 1024], P(None, None, 'head'), may hold values from -0.1875 to 0.1875
Outputs:
- output: float32 [3072, 1024], P(('blk', 'head'))
- cache: bfloat16 [2, 3072, 1024], P(None, 'blk', 'head')
- next_qkv: float32 [3, 3072, 1024], P(None, 'blk', 'head')
Inputs may be any that keep to these rules, and one draw needn't show every extreme that they name: `block_order`: each half-block index appears once, and stored half-blocks 2i and 2i + 1 hold position blocks that add up to 15. `request_lengths`: the lengths sum to 3072. `enc_lengths`: the lengths sum to 2048.
All inputs are finite; a program needn't handle non-finite values.
Results may differ from a plain program's by a relative error of at most 0.024.
Values may be sent and summed in bfloat16 or wider, within the bound.
No kernel may reach another device: no remote copies, remote signals or barrier semaphores. Data moves between devices by JAX's collectives and lax.ppermute only.
A program may use at most 128 MiB of HBM per device.

v0:
```python
import math

import jax
import jax.numpy as jnp
from jax import lax
from jax.sharding import PartitionSpec as P

HEADS = 16


NEGATIVE = -1e30
SCALING = 0.125
EPSILON = 1e-05


def normalize(matrix):
    center = matrix - jnp.mean(matrix, axis=-1, keepdims=True)
    return center * lax.rsqrt(jnp.mean(center * center, axis=-1, keepdims=True) + EPSILON)


def position_of(order_table, indices, halfway):
    slots = jnp.arange(order_table.shape[0], dtype=jnp.int32)
    picked = jnp.sum(
        jnp.where((indices // halfway)[:, None] == slots[None, :], order_table[None, :], 0), axis=1
    )
    return picked * halfway + indices % halfway


def group_of(places, lengths):
    ends = jnp.cumsum(lengths)
    return jnp.sum((places[:, None] >= ends[None, :]).astype(jnp.int32), axis=1)


def online_update(carried, queries, key_rows, value_rows, visible):
    maxima, totals, running = carried
    heads_here = queries.shape[1]
    key_split = key_rows.reshape(key_rows.shape[0], heads_here, -1)
    value_split = value_rows.reshape(value_rows.shape[0], heads_here, -1)
    scores = (
        jnp.einsum("qhd,khd->qhk", queries, key_split, preferred_element_type=jnp.float32) * SCALING
    )
    scores = jnp.where(visible[:, None, :], scores, NEGATIVE)
    updated = jnp.maximum(maxima, jnp.max(scores, axis=2))
    factor = jnp.exp(maxima - updated)
    weights = jnp.exp(scores - updated[:, :, None])
    totals = totals * factor + jnp.sum(weights, axis=2)
    running = running * factor[:, :, None] + jnp.einsum(
        "qhk,khd->qhd",
        weights.astype(jnp.bfloat16),
        value_split,
        preferred_element_type=jnp.float32,
    )
    return (updated, totals, running)


def sweep(
    carried, queries, key_rows, value_rows, key_places, key_groups, query_places, query_groups
):
    length = key_rows.shape[0]
    block_size = math.gcd(length, 2048)
    blocks_count = length // block_size
    key_blocks = key_rows.reshape(blocks_count, block_size, key_rows.shape[1])
    value_blocks = value_rows.reshape(blocks_count, block_size, value_rows.shape[1])
    group_blocks = key_groups.reshape(blocks_count, block_size)
    if key_places is None:
        place_blocks = group_blocks
    else:
        place_blocks = key_places.reshape(blocks_count, block_size)

    def advance(status, element):
        key_block, value_block, place_block, group_block = element
        visible = group_block[None, :] == query_groups[:, None]
        if key_places is None:
            return (online_update(status, queries, key_block, value_block, visible), None)
        visible = visible & (place_block[None, :] <= query_places[:, None])
        updated = online_update(status, queries, key_block, value_block, visible)
        return (updated, None)

    carried, unused = lax.scan(
        advance, carried, (key_blocks, value_blocks, place_blocks, group_blocks)
    )
    return carried


def empty_state(count_q, heads_here, head_width):
    return (
        jnp.full((count_q, heads_here), NEGATIVE, jnp.float32),
        jnp.zeros((count_q, heads_here), jnp.float32),
        jnp.zeros((count_q, heads_here, head_width), jnp.float32),
    )


def finish(carried):
    maxima, totals, running = carried
    return (running / totals[:, :, None]).reshape(running.shape[0], -1).astype(jnp.bfloat16)


def on_device(
    tokens,
    block_order,
    request_lengths,
    enc_lengths,
    w_qkv,
    w_out,
    enc_kv,
    w_cq,
    w_co,
    w_up,
    w_down,
    w_next,
):
    rows_here = tokens.shape[0]
    model_width = tokens.shape[1]
    group_size = lax.axis_size("head")
    cycle_size = lax.axis_size("blk")
    block_rows = rows_here * group_size
    halfway = block_rows // 2
    group_width = w_qkv.shape[2]
    head_width = model_width // HEADS
    group_heads = group_width // head_width
    gathered = lax.all_gather(tokens, "head", axis=0, tiled=True)
    projected = jnp.einsum(
        "td,cde->cte", gathered, w_qkv, preferred_element_type=jnp.float32
    ).astype(jnp.bfloat16)
    cycle_index = lax.axis_index("blk")
    block_start = cycle_index * block_rows
    query_places = position_of(
        block_order, block_start + jnp.arange(block_rows, dtype=jnp.int32), halfway
    )
    query_groups = group_of(query_places, request_lengths)
    queries = projected[0].reshape(block_rows, group_heads, head_width)
    start_state = empty_state(block_rows, group_heads, head_width)
    slots = jnp.arange(2 * cycle_size, dtype=jnp.int32)
    holders = jnp.sum(jnp.where(block_order[:, None] == slots[None, :], slots[:, None], 0), axis=0)
    start_carry = (start_state, jnp.zeros((1,), jnp.bfloat16))
    shards = (
        lax.all_gather(projected[1], "blk", axis=0, tiled=True),
        lax.all_gather(projected[2], "blk", axis=0, tiled=True),
    )
    shard_length = shards[0].shape[0]
    key_places = position_of(block_order, jnp.arange(shard_length, dtype=jnp.int32), halfway)
    key_groups = group_of(key_places, request_lengths)
    final_state = sweep(
        start_carry[0],
        queries,
        shards[0],
        shards[1],
        key_places,
        key_groups,
        query_places,
        query_groups,
    )
    attended = finish(final_state)
    pair = lax.dynamic_slice_in_dim(block_order, 2 * cycle_index, 2, 0)
    targets = pair // 2
    halves = projected[1:].reshape(2, 2, halfway, group_width)
    cycle_slots = jnp.arange(cycle_size, dtype=jnp.int32)
    outgoing = jnp.where(
        (cycle_slots == targets[0])[None, :, None, None],
        halves[:, 0][:, None],
        jnp.where(
            (cycle_slots == targets[1])[None, :, None, None],
            halves[:, 1][:, None],
            jnp.zeros((), jnp.bfloat16),
        ),
    )
    incoming = lax.all_to_all(outgoing, "blk", split_axis=1, concat_axis=1, tiled=True)
    first_source = lax.dynamic_index_in_dim(holders, 2 * cycle_index, 0, keepdims=False) // 2
    second_source = lax.dynamic_index_in_dim(holders, 2 * cycle_index + 1, 0, keepdims=False) // 2
    cache = jnp.concatenate(
        [
            lax.dynamic_index_in_dim(incoming, first_source, 1, keepdims=False),
            lax.dynamic_index_in_dim(incoming, second_source, 1, keepdims=False),
        ],
        axis=1,
    )
    mixed = lax.psum_scatter(
        jnp.dot(attended, w_out, preferred_element_type=jnp.float32),
        "head",
        scatter_dimension=0,
        tiled=True,
    )
    hidden = normalize(mixed + tokens.astype(jnp.float32))
    hidden_b = hidden.astype(jnp.bfloat16)
    member = lax.axis_index("head")
    own_places = lax.dynamic_slice_in_dim(query_places, member * rows_here, rows_here, 0)
    own_groups = group_of(own_places, request_lengths)
    cross_query = jnp.dot(hidden_b, w_cq, preferred_element_type=jnp.float32).astype(jnp.bfloat16)
    cross_split = cross_query.reshape(rows_here, HEADS, head_width)
    widened = lax.all_gather(enc_kv, "head", axis=2, tiled=True)
    shards = lax.all_gather(widened, "blk", axis=1, tiled=True)
    shard_length = shards.shape[1]
    encoder_groups = group_of(jnp.arange(shard_length, dtype=jnp.int32), enc_lengths)
    crossed = finish(
        sweep(
            empty_state(rows_here, HEADS, head_width),
            cross_split,
            shards[0],
            shards[1],
            None,
            encoder_groups,
            None,
            own_groups,
        )
    )
    summed = jnp.dot(crossed, w_co, preferred_element_type=jnp.float32)
    second = normalize(summed + hidden)
    second_b = second.astype(jnp.bfloat16)
    inner = jax.nn.gelu(
        jnp.dot(second_b, w_up, preferred_element_type=jnp.float32), approximate=False
    ).astype(jnp.bfloat16)
    output = normalize(jnp.dot(inner, w_down, preferred_element_type=jnp.float32) + second)
    output_b = output.astype(jnp.bfloat16)
    block_output = lax.all_gather(output_b, "head", axis=0, tiled=True)
    next_qkv = jnp.einsum("td,cde->cte", block_output, w_next, preferred_element_type=jnp.float32)
    return (output, cache, next_qkv)


def solution(mesh):
    in_specs = (
        P(("blk", "head"), None),
        P(),
        P(),
        P(),
        P(None, None, "head"),
        P("head", None),
        P(None, "blk", "head"),
        P(),
        P(),
        P(),
        P(),
        P(None, None, "head"),
    )
    out_specs = (P(("blk", "head"), None), P(None, "blk", "head"), P(None, "blk", "head"))
    return jax.shard_map(
        on_device, mesh=mesh, in_specs=in_specs, out_specs=out_specs, check_vma=False
    )
```

profile of v0, /device:TPU:0, one launch (start us, length us, event | category | flops | bytes accessed | tf_op | source)
XLA Modules:
  0.0 299.0 jit_solution(6979450326983845441)
XLA Ops:
  7.2 21.6 %all_gather.18 = bf16[384,1024]{1,0:T(8,128)(2,1)S(1)} all-gather(bf16[96,1024]{1,0:T(8,128)(2,1)} %param.14), channel_id=1, replica_groups=mesh['blk'=8,'head'=4] {'head'}, dimensions={0}, use_global_device_ids=true | all-gather | bytes 983040 | tf_op jit(solution)/shard_map/all_gather | solution.py:121
  28.9 2.4 fusion.31
  36.2 1.3 convert_reduce_fusion.2
  38.3 20.1 %all-gather.13.cloned.1.call-done = bf16[1,3072,256]{1,2,0:T(8,128)(2,1)} async-done(((bf16[1,384,256]{1,2,0:T(8,128)(2,1)}), bf16[1,3072,256]{1,2,0:T(8,128)(2,1)}) %all-gather.13.cloned.1.call-update) | async-done | bytes 1572880 | tf_op jit(solution)/shard_map/all_gather | solution.py:138
  58.4 2.6 copy.37
  61.0 25.2 %all-gather.11.cloned.1.call-done = bf16[1,3072,256]{1,2,0:T(8,128)(2,1)} async-done(((bf16[1,384,256]{1,2,0:T(8,128)(2,1)}), bf16[1,3072,256]{1,2,0:T(8,128)(2,1)}) %all-gather.11.cloned.1.call-update) | async-done | bytes 1572880 | tf_op jit(solution)/shard_map/all_gather | solution.py:137
  86.1 2.6 copy.36
  88.7 38.4 %while.3 = (s32[]{:T(128)}, f32[384,4]{0,1:T(4,128)S(1)}, f32[384,4]{0,1:T(4,128)S(1)}, f32[384,4,64]{0,2,1:T(8,128)}, s32[3,1024]{1,0:T(4,128)}, /*index=5*/s32...) while((s32[]{:T(128)}, f32[384,4]{0,1:T(4,128)S(1)}, ...), condition=%wide.region_11.12_spmd.clone, body=%wide.region_8.11_spmd.clone.sunk | while | flops 421436928 | bytes 32042220 | solution.py:79
  89.5 1.5 compare_and_fusion.2
  91.0 2.1 constant_dynamic-slice_fusion.7
  93.1 1.3 copy.50
  95.3 2.2 fusion.171
  97.5 1.4 fusion.172
  98.9 1.9 fusion.174
  102.3 1.5 compare_and_fusion.2
  103.8 2.1 constant_dynamic-slice_fusion.7
  105.8 1.3 copy.50
  108.1 2.1 fusion.171
  110.3 1.4 fusion.172
  111.7 1.9 fusion.174
  115.1 1.5 compare_and_fusion.2
  116.6 2.1 constant_dynamic-slice_fusion.7
  118.6 1.2 copy.50
  120.9 2.1 fusion.171
  123.1 1.4 fusion.172
  124.5 1.9 fusion.174
  127.1 1.0 divide_convert_fusion
  128.1 2.7 fusion.143
  132.7 1.3 iota_compare_fusion.4
  134.0 1.4 select_select_fusion
  135.4 4.6 %all-to-all-start = ((bf16[2,8,192,256]{3,2,0,1:T(8,128)(2,1)}), bf16[2,8,192,256]{3,2,0,1:T(8,128)(2,1)}, u32[]{:S(2)}, u32[]{:S(2)}) async-start(bf16[2,8,192,256]{3,2,0,1:T(8,128)(2,1)} %select_select_fusion), calls=%async_computation.1 | async-start | bytes 3145728 | tf_op jit(solution)/shard_map/all_to_all | solution.py:167
  147.3 13.6 %all-to-all-done = bf16[2,8,192,256]{3,2,0,1:T(8,128)(2,1)} async-done(((bf16[2,8,192,256]{3,2,0,1:T(8,128)(2,1)}), bf16[2,8,192,256]{3,2,0,1:T(8,128)(2,1)}, u32[]{:S(2)}, u32[]{:S(2)}) %all-to-all-start) | async-done | bytes 1572896 | tf_op jit(solution)/shard_map/all_to_all | solution.py:167
  160.9 1.0 dynamic-slice_bitcast_fusion.1
  162.7 3.5 %reduce-scatter.2.cloned.1.call-done = f32[96,1024]{1,0:T(8,128)} async-done(((f32[384,1024]{1,0:T(8,128)}), f32[96,1024]{1,0:T(8,128)}) %reduce-scatter.2.cloned.1.call-update) | async-done | bytes 393232 | tf_op jit(solution)/shard_map/reduce_scatter | solution.py:177
  166.3 1.1 fusion.84
  167.4 1.2 multiply_reduce_fusion.2
  168.6 2.3 convolution_convert_fusion.1
  171.1 50.3 %all-gather.9.cloned.1.call-done = bf16[2,2048,1024]{2,1,0:T(8,128)(2,1)} async-done(((bf16[2,256,1024]{2,1,0:T(8,128)(2,1)}), bf16[2,2048,1024]{2,1,0:T(8,128)(2,1)}) %all-gather.9.cloned.1.call-update) | async-done | bytes 8388624 | tf_op jit(solution)/shard_map/all_gather | solution.py:191
  221.4 5.9 %fusion.137 = (bf16[1,2048,1024]{2,1,0:T(8,128)(2,1)}, bf16[1,2048,1024]{2,1,0:T(8,128)(2,1)}) fusion(bf16[2,2048,1024]{2,1,0:T(8,128)(2,1)} %all-gather.9.cloned.1.call-done), kind=kLoop, calls=%fused_computation.199 | loop fusion | bytes 16777216 | tf_op jit(solution)/shard_map/slice | solution.py:198
  227.3 6.5 %copy.41 = bf16[1,2048,1024]{1,2,0:T(8,128)(2,1)} copy(bf16[1,2048,1024]{2,1,0:T(8,128)(2,1)} %get-tuple-element.191) | data formatting | bytes 8388608 | tf_op jit(solution)/shard_map/slice | solution.py:198
  233.8 6.5 %copy.42 = bf16[1,2048,1024]{1,2,0:T(8,128)(2,1)} copy(bf16[1,2048,1024]{2,1,0:T(8,128)(2,1)} %get-tuple-element.192) | data formatting | bytes 8388608 | tf_op jit(solution)/shard_map/slice | solution.py:199
  240.3 4.6 %bitcast_reduce_fusion = (f32[96,16]{0,1:T(8,128)S(1)}, f32[16,96,2048]{2,1,0:T(8,128)S(1)}) fusion(pred[96,2048]{1,0:T(8,128)(4,1)S(1)} %broadcast_compare_fusion, bf16[96,16,64]{0,2,1:T(8,128)(2,1)S(1)} %bitcast.127, bf16[2048,16,64]{0,2,1:T(8,128)(2,1)} %bitcast.120), kind=kOutput, calls=%fused_computation.22 | convolution fusion | flops 412088832 | bytes 17176576 | tf_op jit(solution)/shard_map/while/body/eval_jaxpr/qhd,khd->qhk/dot_general | solution.py:40
  244.9 3.1 %fusion.16 = f32[96,16]{0,1:T(8,128)S(1)} fusion(f32[16,96,2048]{2,1,0:T(8,128)S(1)} %get-tuple-element.209, f32[96,16]{0,1:T(8,128)S(1)} %broadcast_maximum_fusion, pred[96,2048]{1,0:T(8,128)(4,1)S(1)} %broadcast_compare_fusion), kind=kLoop, calls=%fused_computation.25 | loop fusion | flops 12581376 | bytes 12791808 | tf_op jit(solution)/shard_map/while/body/eval_jaxpr/reduce_sum | solution.py:46
  248.0 1.5 copy-done.1
  249.5 9.5 %fusion.41 = bf16[96,16,64]{0,2,1:T(8,128)(2,1)S(1)} fusion(bf16[2048,16,64]{0,2,1:T(8,128)(2,1)} %bitcast.125, f32[16,96,2048]{2,1,0:T(8,128)} %copy-done.1, f32[96,16]{0,1:T(8,128)S(1)} %broadcast_maximum_fusion, pred[96,2048]{1,0:T(8,128)(4,1)S(1)} %broadcast_compare_fusion, f32[96,16]{0,1:T(8,128)S(1)} %get-tuple-element.203, ...), kind=kOutput, calls=%fused_computation.58 | convolution fusion | flops 415531008 | bytes 17188864 | tf_op jit(solution)/shard_map/while/body/eval_jaxpr/qhk,khd->qhd/dot_general | solution.py:47
  259.9 10.2 %fusion.142 = (f32[96]{0:T(128)S(1)}, f32[96,1024]{1,0:T(8,128)S(1)}) fusion(f32[96]{0:T(128)S(1)} %add_rsqrt_fusion.1, f32[96,1024]{1,0:T(8,128)S(1)} %get-tuple-element.211, f32[96]{0:T(128)S(1)} %broadcast_multiply_fusion.2, bf16[4096,1024]{1,0:T(8,128)(2,1)} %param.24, bf16[1024,4096]{1,0:T(8,128)(2,1)} %param.23), kind=kOutput, calls=%fused_computation.204 | convolution fusion | flops 1636859776 | bytes 17564800 | tf_op jit(solution)/shard_map/dot_general | solution.py:212
  271.2 19.5 %all_gather.23 = bf16[384,1024]{1,0:T(8,128)(2,1)S(1)} all-gather(bf16[96,1024]{1,0:T(8,128)(2,1)S(1)} %get-tuple-element.183), channel_id=1, replica_groups=mesh['blk'=8,'head'=4] {'head'}, dimensions={0}, use_global_device_ids=true | all-gather | bytes 983040 | tf_op jit(solution)/shard_map/all_gather | solution.py:214
  290.7 1.8 convolution_bitcast_fusion
  (109 shorter events, 19.8 us)
Async XLA Ops:
  7.2 251.9 %copy-start = (bf16[1024,1024]{1,0:T(8,128)(2,1)S(1)}, bf16[1024,1024]{1,0:T(8,128)(2,1)}, u32[]{:S(2)}) copy-start(bf16[1024,1024]{1,0:T(8,128)(2,1)} %param.22) | copy-start | bytes 6291460
  7.2 51.2 %all-gather.13.cloned.1.call-start = ((), (), s32[]{:S(2)}) async-start(), calls=%async_computation.6 | async-start | bytes 1769472 | tf_op jit(solution)/shard_map/all_gather | solution.py:138
  31.3 0.8 copy-start.5
  32.1 2.5 copy-start.13
  32.1 2.7 copy-start.8
  33.0 53.2 %all-gather.11.cloned.1.call-start = ((), (), s32[]{:S(2)}) async-start(), calls=%async_computation.5 | async-start | bytes 1769472 | tf_op jit(solution)/shard_map/all_gather | solution.py:137
  33.7 97.2 %all-gather.7.cloned.1.call-start = ((), (), s32[]{:S(2)}) async-start(), calls=%async_computation.3 | async-start | bytes 1310720 | tf_op jit(solution)/shard_map/all_gather | solution.py:190
  34.5 131.8 %reduce-scatter.2.cloned.1.call-start = ((), (), s32[]{:S(2)}) async-start(), calls=%async_computation.2 | async-start | bytes 1966080 | tf_op jit(solution)/shard_map/reduce_scatter | solution.py:177
  34.8 26.2 %copy-start.10 = (s32[9,1]{0,1:T(1,128)}, s32[9,1]{0,1:T(1,128)S(1)}, u32[]{:S(2)}) copy-start(s32[9,1]{0,1:T(1,128)S(1)} %reduce-window.17) | copy-start | bytes 112
  97.5 1.4 copy-start.2
  97.5 1.4 copy-start.6
  100.8 0.7 copy-start.7
  110.3 1.4 copy-start.2
  110.3 1.4 copy-start.6
  113.6 0.7 copy-start.7
  123.1 1.4 copy-start.2
  123.1 1.4 copy-start.6
  126.3 0.7 copy-start.7
  130.8 1.0 slice-start
  130.8 1.2 copy-start.9
  130.8 90.6 %all-gather.9.cloned.1.call-start = ((), (), s32[]{:S(2)}) async-start(), calls=%async_computation.4 | async-start | bytes 9437184 | tf_op jit(solution)/shard_map/all_gather | solution.py:191
  135.4 10.5 %copy-start.14 = (s32[9]{0:T(128)S(1)}, s32[9]{0:T(128)}, u32[]{:S(2)}) copy-start(s32[9]{0:T(128)} %param.17) | copy-start | bytes 112
  135.4 11.5 %copy-start.11 = (s32[9,1]{0,1:T(1,128)S(1)}, s32[9,1]{0,1:T(1,128)}, u32[]{:S(2)}) copy-start(s32[9,1]{0,1:T(1,128)} %copy-done.10) | copy-start | bytes 112
  135.4 25.5 %all-to-all-start = ((bf16[2,8,192,256]{3,2,0,1:T(8,128)(2,1)}), bf16[2,8,192,256]{3,2,0,1:T(8,128)(2,1)}, u32[]{:S(2)}, u32[]{:S(2)}) async-start(bf16[2,8,192,256]{3,2,0,1:T(8,128)(2,1)} %select_select_fusion), calls=%async_computation.1 | async-start | bytes 3145728 | tf_op jit(solution)/shard_map/all_to_all | solution.py:167
  140.0 26.2 %copy-start.4 = (bf16[96,1024]{1,0:T(8,128)(2,1)S(1)}, bf16[96,1024]{1,0:T(8,128)(2,1)}, u32[]{:S(2)}) copy-start(bf16[96,1024]{1,0:T(8,128)(2,1)} %param.14) | copy-start | bytes 589828
  244.9 4.6 %copy-start.1 = (f32[16,96,2048]{2,1,0:T(8,128)}, f32[16,96,2048]{2,1,0:T(8,128)S(1)}, u32[]{:S(2)}) copy-start(f32[16,96,2048]{2,1,0:T(8,128)S(1)} %get-tuple-element.209) | copy-start | bytes 37748740
  249.5 9.5 %copy-start.3 = (f32[96,1024]{1,0:T(8,128)S(1)}, f32[96,1024]{1,0:T(8,128)}, u32[]{:S(2)}) copy-start(f32[96,1024]{1,0:T(8,128)} %reduce-scatter.2.cloned.1.call-done) | copy-start | bytes 1179652
  270.1 20.6 %copy-start.12 = (bf16[3,1024,256]{2,1,0:T(8,128)(2,1)S(1)}, bf16[3,1024,256]{2,1,0:T(8,128)(2,1)}, u32[]{:S(2)}) copy-start(bf16[3,1024,256]{2,1,0:T(8,128)(2,1)} %param.25) | copy-start | bytes 4718596
Sparse Core Ops, SparseCore 0:
  33.1 25.2 all-gather.12
  60.2 25.8 all-gather.10
  87.7 30.1 all-gather.6
  130.9 35.2 reduce-scatter.1
  168.0 53.3 all-gather.8
where the time goes:
time: 300 us; the launch traced here: 299 us
  waiting for transfers between devices  115 us (38%)
  local copies, waits for them, and re-layouts  49 us (16%)
  matrix products  46.1 us (15%)
  blocking collectives  41.1 us (14%)
  other arithmetic  23.7 us (8%)
  between operations  19.3 us (6%)
  starting transfers between devices  4.8 us (2%)
    all_gather x1, waiting for transfers between devices, on_device(): shards = lax.all_gather(widened, 'blk', axis=1, tiled=True)  50.3 us
    all_gather x1, waiting for transfers between devices, on_device(): lax.all_gather(projected[1], 'blk', axis=0, tiled=True)  25.2 us
    all_gather x1, blocking collectives, on_device(): gathered = lax.all_gather(tokens, 'head', axis=0, tiled=True)  21.6 us
    all_gather x1, waiting for transfers between devices, on_device(): lax.all_gather(projected[2], 'blk', axis=0, tiled=True)  20.1 us
    all_gather x1, blocking collectives, on_device(): block_output = lax.all_gather(output_b, 'head', axis=0, tiled=True)  19.5 us
    dynamic_slice x12, local copies, waits for them, and re-layouts, sweep(): lax.scan(advance, carried, (key_blocks, value_blocks, place_blocks, group...  15.2 us
    dot_general x4, matrix products, online_update(): jnp.einsum('qhk,khd->qhd', weights.astype(jnp.bfloat16), value_split, pre...  15.1 us
    all_to_all x1, waiting for transfers between devices, on_device(): lax.all_to_all(outgoing, 'blk', split_axis=1, concat_axis=1, tiled=True)  13.6 us
  transfers between devices with their start and end apart: 6, of which 5 were waited for; matrix products, arithmetic and copies ran while one was open for 20% of the time, Pallas kernels for 0%

commit v1 on v0

v1 whole, which is shorter than its diff:
```python
import functools

import jax
import jax.numpy as jnp
from jax import lax
from jax.experimental import pallas as pl
from jax.experimental.pallas import tpu as pltpu
from jax.sharding import PartitionSpec as P

HEADS = 16
NEGATIVE = -1e30
SCALING = 0.125
EPSILON = 1e-05
TILE = 256
MIB = 1024 * 1024


def whole(count):
    return [pl.BlockSpec(memory_space=pltpu.VMEM)] * count


def smem(count):
    return [pl.BlockSpec(memory_space=pltpu.SMEM)] * count


def params(mib):
    return pltpu.CompilerParams(vmem_limit_bytes=mib * MIB)


def xor(size, bits):
    return [(i, i ^ bits) for i in range(size)]


def normalize(matrix):
    center = matrix - jnp.mean(matrix, axis=-1, keepdims=True)
    return center * lax.rsqrt(jnp.mean(center * center, axis=-1, keepdims=True) + EPSILON)


def project_kernel(spots_ref, x0, x1, w_ref, x_ref, q_ref, kv_ref):
    quarter = x0.shape[0]
    for i, piece in enumerate((x0, x1)):
        x_ref[pl.ds(pl.multiple_of(spots_ref[i] % 2 * quarter, quarter), quarter), :] = piece[...]
    x = x_ref[...]
    q_ref[...] = jnp.dot(x, w_ref[0], preferred_element_type=jnp.float32).astype(jnp.bfloat16)
    for c in range(2):
        kv_ref[c] = jnp.dot(x, w_ref[1 + c], preferred_element_type=jnp.float32).astype(
            jnp.bfloat16
        )


def project(spots, x0, x1, w_qkv):
    rows, width, model = 2 * x0.shape[0], w_qkv.shape[2], x0.shape[1]
    return pl.pallas_call(
        project_kernel,
        out_shape=(
            jax.ShapeDtypeStruct((rows, model), jnp.bfloat16),
            jax.ShapeDtypeStruct((rows, width), jnp.bfloat16),
            jax.ShapeDtypeStruct((2, rows, width), jnp.bfloat16),
        ),
        in_specs=smem(1) + whole(3),
        out_specs=tuple(whole(3)),
        compiler_params=params(8),
        name="project",
    )(spots, x0, x1, w_qkv)


def place_kernel(count, dest_ref, *refs):
    out_ref = refs[count]
    for i in range(count):
        rows = refs[i].shape[0]
        out_ref[pl.ds(pl.multiple_of(dest_ref[i] * rows, rows), rows), :] = refs[i][...]


def place(chunks, dest):
    count = len(chunks)
    rows, columns = chunks[0].shape
    return pl.pallas_call(
        functools.partial(place_kernel, count),
        out_shape=jax.ShapeDtypeStruct((rows * count, columns), chunks[0].dtype),
        in_specs=smem(1) + whole(count),
        out_specs=whole(1)[0],
        compiler_params=params(8),
        name="place",
    )(dest, *chunks)


def order_kernel(count, cached, dest_ref, *refs):
    k_ref, v_ref = refs[count], refs[count + 1]
    held_ref, sem = refs[-2], refs[-1]
    copies, index = [], 0
    for i in range(count):
        pieces, rows = refs[i].shape[0], refs[i].shape[2]
        for piece in range(pieces):
            at = pl.ds(pl.multiple_of(dest_ref[index] * rows, rows), rows)
            for c, to in enumerate((k_ref, held_ref)):
                copy = pltpu.make_async_copy(refs[i].at[piece, c], to.at[at, :], sem)
                copy.start()
                copies.append(copy)
            index += 1
    for copy in copies:
        copy.wait()
    lane = lax.broadcasted_iota(jnp.int32, (TILE, 128), 1) // 64

    def step(tile, carry):
        at = pl.ds(pl.multiple_of(tile * TILE, TILE), TILE)
        for head in range(v_ref.shape[0]):
            pair = held_ref[at, (head // 2) * 128 : (head // 2 + 1) * 128]
            v_ref[head, at, :] = jnp.where(lane == head % 2, pair, jnp.ones_like(pair))
        return carry

    lax.fori_loop(0, held_ref.shape[0] // TILE, step, 0)
    if cached:
        cache_ref = refs[count + 2]
        length = cache_ref.shape[1]
        at = pl.ds(pl.multiple_of(dest_ref[index] * length, length), length)
        cache_ref[0] = k_ref[at, :]
        cache_ref[1] = held_ref[at, :]


def order(chunks, dest, cached):
    rows, width = chunks[0].shape[2:]
    total = rows * sum(c.shape[0] for c in chunks)
    heads = width // 64
    outs = [
        jax.ShapeDtypeStruct((total, width), jnp.bfloat16),
        jax.ShapeDtypeStruct((heads, total, 128), jnp.bfloat16),
    ]
    if cached:
        outs.append(jax.ShapeDtypeStruct((2, cached, width), jnp.bfloat16))
    return pl.pallas_call(
        functools.partial(order_kernel, len(chunks), bool(cached)),
        out_shape=tuple(outs),
        in_specs=smem(1) + [pl.BlockSpec(memory_space=pltpu.HBM)] * len(chunks),
        out_specs=tuple(whole(len(outs))),
        scratch_shapes=[pltpu.VMEM((total, width), jnp.bfloat16), pltpu.SemaphoreType.DMA],
        compiler_params=params(4 + 2 * total * width * 2 // MIB),
        name="order",
    )(dest, *chunks)


def flash(queries, k_ref, v_ref, low, high, first, last):
    rows, width = queries.shape
    heads = width // 64
    lane = lax.broadcasted_iota(jnp.int32, (rows, 128), 1) // 64
    masked = []
    for head in range(heads):
        pair = queries[:, (head // 2) * 128 : (head // 2 + 1) * 128]
        pair = (pair.astype(jnp.float32) * SCALING).astype(jnp.bfloat16)
        masked.append(jnp.where(lane == head % 2, pair, jnp.zeros_like(pair)))

    def step(tile, carry):
        start = pl.multiple_of(tile * TILE, TILE)
        keys = start + lax.broadcasted_iota(jnp.int32, (rows, TILE), 1)
        seen = (keys >= low) & (keys < high)
        bias = jnp.where(seen, 0.0, NEGATIVE)
        after = []
        for head in range(heads):
            peak, total = carry[head]
            at = slice((head // 2) * 128, (head // 2 + 1) * 128)
            scores = lax.dot_general(
                masked[head],
                k_ref[pl.ds(start, TILE), at],
                (((1,), (1,)), ((), ())),
                preferred_element_type=jnp.float32,
            )
            scores = scores + bias
            top = jnp.maximum(peak, jnp.max(scores, axis=1, keepdims=True))
            weights = jnp.exp(scores - top)
            total = total * jnp.exp(peak - top) + jnp.dot(
                weights.astype(jnp.bfloat16),
                v_ref[head, pl.ds(start, TILE), :],
                preferred_element_type=jnp.float32,
            )
            after.append((top, total))
        return tuple(after)

    begin = tuple(
        (jnp.full((rows, 1), NEGATIVE, jnp.float32), jnp.zeros((rows, 128), jnp.float32))
        for _ in range(heads)
    )
    carry = lax.fori_loop(first, last + 1, step, begin)
    outs = []
    for pair in range(heads // 2):
        even, odd = carry[2 * pair][1], carry[2 * pair + 1][1]
        sums = pltpu.roll(jnp.where(lane == 0, odd, even), 64, 1)
        outs.append(jnp.where(lane == 0, even, odd) / sums)
    return jnp.concatenate(outs, axis=1)


def self_kernel(half, order_ref, ends_ref, spots_ref, near_ref, far_ref, k_ref, v_ref, out_ref):
    rows = near_ref.shape[0]
    queries = jnp.where(spots_ref[0] // 2 == half, near_ref[...], far_ref[...])
    base = order_ref[half] * rows
    places = base + lax.broadcasted_iota(jnp.int32, (rows, 1), 0)
    low = jnp.zeros((rows, 1), jnp.int32)
    least = jnp.int32(0)
    for j in range(ends_ref.shape[0]):
        end = ends_ref[j]
        low = jnp.where(places >= end, end, low)
        least = jnp.where(base >= end, end, least)
    result = flash(
        queries,
        k_ref,
        v_ref,
        low,
        places + 1,
        least // TILE,
        (base + rows - 1) // TILE,
    )
    out_ref[...] = result.astype(jnp.bfloat16)


def self_attention(half, pair, ends, spots, near, far, keys, values):
    return pl.pallas_call(
        functools.partial(self_kernel, half),
        out_shape=jax.ShapeDtypeStruct(near.shape, jnp.bfloat16),
        in_specs=smem(3) + whole(4),
        out_specs=whole(1)[0],
        compiler_params=params(8),
        name="self_attention",
    )(pair, ends, spots, near, far, keys, values)


def cross_kernel(
    half, order_ref, ends_ref, encs_ref, spots_ref,
    a0, a1, a2, a3, near_ref, far_ref, wo_ref, wq_ref, k_ref, v_ref, hidden_ref, out_ref,
):
    rows, width = a0.shape
    mixed = jnp.where(spots_ref[0] // 2 == half, near_ref[...], far_ref[...]).astype(jnp.float32)
    for i, piece in enumerate((a0, a1, a2, a3)):
        at = pl.ds(pl.multiple_of(spots_ref[i] * width, width), width)
        mixed = mixed + jnp.dot(piece[...], wo_ref[at, :], preferred_element_type=jnp.float32)
    hidden = normalize(mixed)
    hidden_ref[...] = hidden
    queries = jnp.dot(
        hidden.astype(jnp.bfloat16), wq_ref[...], preferred_element_type=jnp.float32
    ).astype(jnp.bfloat16)
    base = order_ref[half] * rows
    places = base + lax.broadcasted_iota(jnp.int32, (rows, 1), 0)
    count = ends_ref.shape[0]
    low = jnp.zeros((rows, 1), jnp.int32)
    least = jnp.int32(0)
    for j in range(count):
        low = jnp.where(places >= ends_ref[j], encs_ref[j], low)
        least = jnp.where(base >= ends_ref[j], encs_ref[j], least)
    high = jnp.full((rows, 1), encs_ref[count - 1], jnp.int32)
    most = encs_ref[count - 1]
    for j in reversed(range(count)):
        high = jnp.where(places < ends_ref[j], encs_ref[j], high)
        most = jnp.where(base + rows - 1 < ends_ref[j], encs_ref[j], most)
    result = flash(queries, k_ref, v_ref, low, high, least // TILE, (most - 1) // TILE)
    out_ref[...] = result.astype(jnp.bfloat16)


def cross_attention(
    half, pair, ends, encs, spots, pieces, near, far, w_out, w_cq, keys, values
):
    rows, width = pieces[0].shape
    return pl.pallas_call(
        functools.partial(cross_kernel, half),
        out_shape=(
            jax.ShapeDtypeStruct(near.shape, jnp.float32),
            jax.ShapeDtypeStruct((rows, width), jnp.bfloat16),
        ),
        in_specs=smem(4) + whole(10),
        out_specs=tuple(whole(2)),
        compiler_params=params(12),
        name="cross_attention",
    )(pair, ends, encs, spots, *pieces, near, far, w_out, w_cq, keys, values)


def fetch_kernel(count, *refs):
    sem = refs[-1]
    copies = []
    for i in range(count):
        copy = pltpu.make_async_copy(refs[i], refs[count + i], sem)
        copy.start()
        copies.append(copy)
    for copy in copies:
        copy.wait()


def fetch(arrays):
    return pl.pallas_call(
        functools.partial(fetch_kernel, len(arrays)),
        out_shape=tuple(jax.ShapeDtypeStruct(a.shape, a.dtype) for a in arrays),
        in_specs=[pl.BlockSpec(memory_space=pltpu.HBM)] * len(arrays),
        out_specs=tuple(whole(len(arrays))),
        scratch_shapes=[pltpu.SemaphoreType.DMA],
        compiler_params=params(1),
        name="fetch",
    )(*arrays)


def mlp_kernel(
    spots_ref, c0, c1, c2, c3, hidden_ref, wco_ref, up_ref, down_ref, wn_ref,
    out_ref, next_ref, bf_ref, sum_ref,
):
    width = c0.shape[1]
    mixed = hidden_ref[...]
    for i, piece in enumerate((c0, c1, c2, c3)):
        at = pl.ds(pl.multiple_of(spots_ref[i] * width, width), width)
        mixed = mixed + jnp.dot(piece[...], wco_ref[at, :], preferred_element_type=jnp.float32)
    second = normalize(mixed)
    bf_ref[...] = second.astype(jnp.bfloat16)
    sum_ref[...] = second
    part = 1024

    def step(i, carry):
        at = pl.ds(pl.multiple_of(i * part, part), part)
        raised = jnp.dot(bf_ref[...], up_ref[:, at], preferred_element_type=jnp.float32)
        inner = (raised * (1.0 + lax.erf(raised * (0.5**0.5))) * 0.5).astype(jnp.bfloat16)
        sum_ref[...] += jnp.dot(inner, down_ref[at, :], preferred_element_type=jnp.float32)
        return carry

    lax.fori_loop(0, up_ref.shape[1] // part, step, 0)
    output = normalize(sum_ref[...])
    out_ref[...] = output
    output_b = output.astype(jnp.bfloat16)
    for c in range(3):
        next_ref[c] = jnp.dot(output_b, wn_ref[c], preferred_element_type=jnp.float32)


def mlp(spots, pieces, hidden, w_co, w_up, w_down, w_next):
    rows, width = pieces[0].shape
    model = w_up.shape[0]
    return pl.pallas_call(
        mlp_kernel,
        out_shape=(
            jax.ShapeDtypeStruct((rows, model), jnp.float32),
            jax.ShapeDtypeStruct((3, rows, width), jnp.float32),
        ),
        in_specs=smem(1) + whole(9),
        out_specs=tuple(whole(2)),
        scratch_shapes=[
            pltpu.VMEM((rows, model), jnp.bfloat16),
            pltpu.VMEM((rows, model), jnp.float32),
        ],
        compiler_params=params(12),
        name="mlp",
    )(spots, *pieces, hidden, w_co, w_up, w_down, w_next)


def over_head(x, size):
    return [x] + [lax.ppermute(x, "head", xor(size, j)) for j in range(1, size)]


def over_plane(x, size):
    me = lax.axis_index("blk")
    if size != 8:
        return [lax.all_gather(x, "blk", axis=0)], [jnp.int32(s) for s in range(size)]
    near = [(s, x if s == 0 else lax.ppermute(x, "blk", xor(size, s))) for s in (0, 2, 4, 6)]
    far = [(s + 1, lax.ppermute(y, "blk", xor(size, 1))) for s, y in near]
    return [y[None] for _, y in near + far], [me ^ s for s, _ in near + far]


def on_device(
    tokens, block_order, request_lengths, enc_lengths, w_qkv, w_out, enc_kv, w_cq, w_co, w_up,
    w_down, w_next,
):
    quarter = tokens.shape[0]
    group = lax.axis_size("head")
    cycle = lax.axis_size("blk")
    me = lax.axis_index("blk")
    member = lax.axis_index("head")
    width = w_qkv.shape[2]
    ends = jnp.cumsum(request_lengths).astype(jnp.int32)
    encs = jnp.cumsum(enc_lengths).astype(jnp.int32)
    pair = lax.dynamic_slice_in_dim(block_order, 2 * me, 2, 0)
    spots = member ^ jnp.arange(group, dtype=jnp.int32)

    rows = over_head(tokens, group)
    w_co, w_up, w_down, w_next = fetch((w_co, w_up, w_down, w_next))
    queries, xs, shards, dest = [], [], [], []
    for far in range(2):
        x, q, kv = project(spots[2 * far : 2 * far + 2], rows[2 * far], rows[2 * far + 1], w_qkv)
        queries.append(q)
        xs.append(x)
        arrays, sources = over_plane(kv, cycle)
        shards += arrays
        dest += [block_order[2 * source + (member // 2 ^ far)] for source in sources]
    dest.append(me)
    keys, values, cache = order(shards, jnp.stack(dest), 4 * quarter)

    enc_shards, enc_dest = over_plane(enc_kv, cycle)
    enc_keys, enc_values = order(enc_shards, jnp.stack(enc_dest), 0)
    out_rows = place(over_head(w_out, group), spots)
    cq_columns = lax.dynamic_slice_in_dim(w_cq, member * width, width, 1)

    outs, nexts = [], []
    for half in range(2):
        attended = self_attention(half, pair, ends, spots, *queries, keys, values)
        hidden, crossed = cross_attention(
            half, pair, ends, encs, spots, over_head(attended, group), *xs, out_rows, cq_columns,
            enc_keys, enc_values,
        )
        output, next_half = mlp(
            spots, over_head(crossed, group), hidden, w_co, w_up, w_down, w_next
        )
        outs.append(output)
        nexts.append(next_half)
    output = lax.dynamic_slice_in_dim(
        jnp.concatenate(outs, axis=0), member * quarter, quarter, 0
    )
    return (output, cache, jnp.concatenate(nexts, axis=1))


def solution(mesh):
    in_specs = (
        P(("blk", "head"), None),
        P(),
        P(),
        P(),
        P(None, None, "head"),
        P("head", None),
        P(None, "blk", "head"),
        P(),
        P(),
        P(),
        P(),
        P(None, None, "head"),
    )
    out_specs = (P(("blk", "head"), None), P(None, "blk", "head"), P(None, "blk", "head"))
    return jax.shard_map(
        on_device, mesh=mesh, in_specs=in_specs, out_specs=out_specs, check_vma=False
    )
```

time: 300 us -> 166 us (0.55)
  the two profiles are of different devices: /device:TPU:0 before, /device:TPU:2 now
where the time goes in v1:
time: 166 us; the launch traced here: 164 us
  local copies, waits for them, and re-layouts  53.6 us (32%)
  Pallas kernels  48.2 us (29%)
  starting transfers between devices  39.6 us (24%)
  waiting for transfers between devices  18.9 us (11%)
  other arithmetic  2.27 us (1%)
    unnamed x120, local copies, waits for them, and re-layouts  42.5 us
    ppermute x18, starting transfers between devices, over_head(): return [x] + [lax.ppermute(x, 'head', xor(size, j)) for j in range(1, size)]  26.6 us
    ppermute x18, waiting for transfers between devices, over_head(): return [x] + [lax.ppermute(x, 'head', xor(size, j)) for j in range(1, size)]  13.4 us
    pallas_call x2, Pallas kernels, mlp(): pl.pallas_call(mlp_kernel, out_shape=(jax.ShapeDtypeStruct((rows, model),...  12.3 us
    pallas_call x2, Pallas kernels, self_attention(): pl.pallas_call(functools.partial(self_kernel, half), out_shape=jax.ShapeD...  11.8 us
    ppermute x9, starting transfers between devices, over_plane(): lax.ppermute(x, 'blk', xor(size, s))  10.9 us
    another operation x1, local copies, waits for them, and re-layouts, on_device(): keys, values, cache = order(shards, jnp.stack(dest), 4 * quarter)  10.1 us
    pallas_call x2, Pallas kernels, order(): pl.pallas_call(functools.partial(order_kernel, len(chunks), bool(cached))...  9.55 us
  transfers between devices with their start and end apart: 39, of which 5 were waited for; matrix products, arithmetic and copies ran while one was open for 7% of the time, Pallas kernels for 26%

profile of v1, /device:TPU:2, one launch (start us, length us, event | category | flops | bytes accessed | tf_op | source)
XLA Modules:
  0.0 163.6 jit_solution(758111752809123818)
XLA Ops:
  0.7 3.7 %collective-permute-start.2 = (bf16[96,1024]{1,0:T(8,128)(2,1)}, bf16[96,1024]{1,0:T(8,128)(2,1)S(1)}, u32[]{:S(2)}, u32[]{:S(2)}) collective-permute-start(bf16[96,1024]{1,0:T(8,128)(2,1)} %x0.1), channel_id=1, source_target_pairs={{0,3},{1,2},{2,1},{3,0},{4,7},{5,6},{6,5},{7,4},{8,11},{9,10},{10,... | collective-permute-start | bytes 589832 | tf_op jit(solution)/shard_map/ppermute | solution.py:345
  5.1 1.5 collective-permute-start.24
  7.2 3.4 %collective-permute-done.2.x1 = bf16[96,1024]{1,0:T(8,128)(2,1)S(1)} collective-permute-done((bf16[96,1024]{1,0:T(8,128)(2,1)}, bf16[96,1024]{1,0:T(8,128)(2,1)S(1)}, u32[]{:S(2)}, u32[]{:S(2)}) %collective-permute-start.2) | collective-permute-done | bytes 196640 | tf_op jit(solution)/shard_map/ppermute | solution.py:345
  11.3 9.9 %collective-permute-done.1.x0 = bf16[96,1024]{1,0:T(8,128)(2,1)S(1)} collective-permute-done((bf16[96,1024]{1,0:T(8,128)(2,1)}, bf16[96,1024]{1,0:T(8,128)(2,1)S(1)}, u32[]{:S(2)}, u32[]{:S(2)}) %collective-permute-start.1) | collective-permute-done | bytes 196640 | tf_op jit(solution)/shard_map/ppermute | solution.py:345
  21.9 1.5 collective-permute-start.25
  23.5 1.4 copy-done.4
  24.9 0.9 copy-done.22
  26.8 1.0 project.3
  27.9 1.5 collective-permute-start.12
  29.4 1.5 collective-permute-start.11
  32.8 0.9 copy-done.20
  33.8 1.4 project.2
  36.5 1.4 collective-permute-start.5
  38.0 1.5 collective-permute-start.4
  43.7 1.5 collective-permute-done.5
  45.8 3.1 %collective-permute-done.4 = bf16[2,192,256]{2,1,0:T(8,128)(2,1)S(1)} collective-permute-done((bf16[2,192,256]{2,1,0:T(8,128)(2,1)S(1)}, bf16[2,192,256]{2,1,0:T(8,128)(2,1)S(1)}, u32[]{:S(2)}, u32[]{:S(2)}) %collective-permute-start.4) | collective-permute-done | bytes 196640 | tf_op jit(solution)/shard_map/ppermute | solution.py:352
  55.5 3.0 %collective-permute-start.20 = (bf16[256,1024]{1,0:T(8,128)(2,1)S(1)}, bf16[256,1024]{1,0:T(8,128)(2,1)}, u32[]{:S(2)}, u32[]{:S(2)}) collective-permute-start(bf16[256,1024]{1,0:T(8,128)(2,1)S(1)} %copy-done.12), channel_id=1, source_target_pairs={{0,1},{1,0},{2,3},{3,2},{4,5},{5,4},{6,7},{7,6},{8,9},{9,8},{10,11... | collective-permute-start | bytes 1572872 | tf_op jit(solution)/shard_map/ppermute | solution.py:345
  59.2 1.3 collective-permute-start.22
  63.7 10.1 %stack.32.dest_ref = s32[17]{0:T(128)S(1)} concatenate(s32[1]{0:T(128)} %get-tuple-element.63, s32[1]{0:T(128)} %get-tuple-element.62, s32[1]{0:T(128)} %get-tuple-element.61, s32[1]{0:T(128)} %get-tuple-element.60, s32[1]{0:T(128)} %get-tuple-element.59, s32[1]{0:T(128)} %get-tuple-element.58, s32[1]{0:T(128)} %get-tuple-element.57, s32[1]{0:T(128)} %get-tuple-element.56, ...), dimensions={0} | concatenate | bytes 136 | tf_op jit(solution)/shard_map/stack | solution.py:383
  73.8 1.0 copy-done.26
  74.8 0.9 copy-done.28
  76.7 0.9 copy-done.32
  77.6 0.9 copy-done.34
  78.5 0.9 copy-done.36
  79.4 0.9 copy-done.38
  81.3 0.9 copy-done.42
  88.7 6.4 %order.2 = (bf16[3072,256]{1,0:T(8,128)(2,1)S(1)}, bf16[4,3072,128]{2,1,0:T(8,128)(2,1)S(1)}, bf16[2,384,256]{2,1,0:T(8,128)(2,1)}) custom-call(s32[17]{0:T(128)S(1)} %stack.32.dest_ref, bf16[1,2,192,256]{3,2,1,0:T(8,128)(2,1)S(1)} %bitcast.44, bf16[1,2,192,256]{3,2,1,0:T(8,128)(2,1)S(1)} %bitcast.48, bf16[1,2,192,256]{3,2,1,0:T(8,128)(2,1)S(1)} %bitcast.47, ...), custom_call_target="tpu_custom_call" | custom-call | tf_op jit(solution)/shard_map/order/pallas_call | solution.py:130
  95.2 4.2 %self_attention.3.a0 = bf16[192,256]{1,0:T(8,128)(2,1)S(1)} custom-call(s32[2]{0:T(128)S(1)} %dynamic_slice.57.order_ref, s32[9]{0:T(128)S(1)} %bitcast.55, s32[4]{0:T(128)S(1)} %iota_xor_fusion.spots_ref.dest_ref, bf16[192,256]{1,0:T(8,128)(2,1)S(1)} %copy-done.14, bf16[192,256]{1,0:T(8,128)(2,1)S(1)} %get-tuple-element.27.far_ref, ...), custom_call_target="tpu_custom_call" | custom-call | tf_op jit(solution)/shard_map/self_attention/pallas_call | solution.py:214
  99.4 2.5 %collective-permute-start.35 = (bf16[192,256]{1,0:T(8,128)(2,1)S(1)}, bf16[192,256]{1,0:T(8,128)(2,1)S(1)}, u32[]{:S(2)}, u32[]{:S(2)}) collective-permute-start(bf16[192,256]{1,0:T(8,128)(2,1)S(1)} %self_attention.3.a0), channel_id=1, source_target_pairs={{0,3},{1,2},{2,1},{3,0},{4,7},{5,6},{6,5},{7,4},{8,11},{9,10},{10,... | collective-permute-start | bytes 294920 | tf_op jit(solution)/shard_map/ppermute | solution.py:345
  102.0 1.9 %collective-permute-start.33 = (bf16[192,256]{1,0:T(8,128)(2,1)S(1)}, bf16[192,256]{1,0:T(8,128)(2,1)S(1)}, u32[]{:S(2)}, u32[]{:S(2)}) collective-permute-start(bf16[192,256]{1,0:T(8,128)(2,1)S(1)} %self_attention.3.a0), channel_id=1, source_target_pairs={{0,1},{1,0},{2,3},{3,2},{4,5},{5,4},{6,7},{7,6},{8,9},{9,8},{10,11... | collective-permute-start | bytes 294920 | tf_op jit(solution)/shard_map/ppermute | solution.py:345
  104.0 3.1 %order.3 = (bf16[2048,256]{1,0:T(8,128)(2,1)S(1)}, bf16[4,2048,128]{2,1,0:T(8,128)(2,1)S(1)}) custom-call(s32[8]{0:T(128)S(1)} %stack.40.dest_ref, bf16[1,2,256,256]{3,2,1,0:T(8,128)(2,1)S(1)} %bitcast.36, bf16[1,2,256,256]{3,2,1,0:T(8,128)(2,1)} %bitcast.29.refs_1_, bf16[1,2,256,256]{3,2,1,0:T(8,128)(2,1)} %bitcast.30.refs_2_, ...), custom_call_target="tpu_custom_call" | custom-call | tf_op jit(solution)/shard_map/order/pallas_call | solution.py:130
  107.1 1.5 place.1.wo_ref
  108.6 7.6 %self_attention.2.a0 = bf16[192,256]{1,0:T(8,128)(2,1)S(1)} custom-call(s32[2]{0:T(128)S(1)} %dynamic_slice.57.order_ref, s32[9]{0:T(128)S(1)} %bitcast.56, s32[4]{0:T(128)S(1)} %iota_xor_fusion.spots_ref.dest_ref, bf16[192,256]{1,0:T(8,128)(2,1)S(1)} %copy-done.14, bf16[192,256]{1,0:T(8,128)(2,1)S(1)} %get-tuple-element.27.far_ref, ...), custom_call_target="tpu_custom_call" | custom-call | tf_op jit(solution)/shard_map/self_attention/pallas_call | solution.py:214
  116.2 2.5 %collective-permute-start.19 = (bf16[192,256]{1,0:T(8,128)(2,1)S(1)}, bf16[192,256]{1,0:T(8,128)(2,1)S(1)}, u32[]{:S(2)}, u32[]{:S(2)}) collective-permute-start(bf16[192,256]{1,0:T(8,128)(2,1)S(1)} %self_attention.2.a0), channel_id=1, source_target_pairs={{0,3},{1,2},{2,1},{3,0},{4,7},{5,6},{6,5},{7,4},{8,11},{9,10},{10,... | collective-permute-start | bytes 294920 | tf_op jit(solution)/shard_map/ppermute | solution.py:345
  118.8 1.9 %collective-permute-start.17 = (bf16[192,256]{1,0:T(8,128)(2,1)S(1)}, bf16[192,256]{1,0:T(8,128)(2,1)S(1)}, u32[]{:S(2)}, u32[]{:S(2)}) collective-permute-start(bf16[192,256]{1,0:T(8,128)(2,1)S(1)} %self_attention.2.a0), channel_id=1, source_target_pairs={{0,1},{1,0},{2,3},{3,2},{4,5},{5,4},{6,7},{7,6},{8,9},{9,8},{10,11... | collective-permute-start | bytes 294920 | tf_op jit(solution)/shard_map/ppermute | solution.py:345
  120.7 4.5 %cross_attention.3 = (f32[192,1024]{1,0:T(8,128)S(1)}, bf16[192,256]{1,0:T(8,128)(2,1)S(1)}) custom-call(s32[2]{0:T(128)S(1)} %dynamic_slice.57.order_ref, s32[9]{0:T(128)S(1)} %bitcast.57, s32[9]{0:T(128)S(1)} %bitcast.59, s32[4]{0:T(128)S(1)} %iota_xor_fusion.spots_ref.dest_ref, bf16[192,256]{1,0:T(8,128)(2,1)S(1)} %self_attention.3.a0, ...), custom_call_target="tpu_custom_call" | custom-call | tf_op jit(solution)/shard_map/cross_attention/pallas_call | solution.py:259
  125.2 2.5 %collective-permute-start.38 = (bf16[192,256]{1,0:T(8,128)(2,1)S(1)}, bf16[192,256]{1,0:T(8,128)(2,1)S(1)}, u32[]{:S(2)}, u32[]{:S(2)}) collective-permute-start(bf16[192,256]{1,0:T(8,128)(2,1)S(1)} %get-tuple-element.43.c0), channel_id=1, source_target_pairs={{0,3},{1,2},{2,1},{3,0},{4,7},{5,6},{6,5},{7,4},{8,11},{9,10},{10,... | collective-permute-start | bytes 294920 | tf_op jit(solution)/shard_map/ppermute | solution.py:345
  127.8 1.9 %collective-permute-start.36 = (bf16[192,256]{1,0:T(8,128)(2,1)S(1)}, bf16[192,256]{1,0:T(8,128)(2,1)S(1)}, u32[]{:S(2)}, u32[]{:S(2)}) collective-permute-start(bf16[192,256]{1,0:T(8,128)(2,1)S(1)} %get-tuple-element.43.c0), channel_id=1, source_target_pairs={{0,1},{1,0},{2,3},{3,2},{4,5},{5,4},{6,7},{7,6},{8,9},{9,8},{10,11... | collective-permute-start | bytes 294920 | tf_op jit(solution)/shard_map/ppermute | solution.py:345
  129.7 4.7 %cross_attention.2 = (f32[192,1024]{1,0:T(8,128)S(1)}, bf16[192,256]{1,0:T(8,128)(2,1)S(1)}) custom-call(s32[2]{0:T(128)S(1)} %dynamic_slice.57.order_ref, s32[9]{0:T(128)S(1)} %bitcast.58, s32[9]{0:T(128)S(1)} %bitcast.60, s32[4]{0:T(128)S(1)} %iota_xor_fusion.spots_ref.dest_ref, bf16[192,256]{1,0:T(8,128)(2,1)S(1)} %self_attention.2.a0, ...), custom_call_target="tpu_custom_call" | custom-call | tf_op jit(solution)/shard_map/cross_attention/pallas_call | solution.py:259
  135.3 2.5 %collective-permute-start.32 = (bf16[192,256]{1,0:T(8,128)(2,1)S(1)}, bf16[192,256]{1,0:T(8,128)(2,1)S(1)}, u32[]{:S(2)}, u32[]{:S(2)}) collective-permute-start(bf16[192,256]{1,0:T(8,128)(2,1)S(1)} %get-tuple-element.36.c0), channel_id=1, source_target_pairs={{0,3},{1,2},{2,1},{3,0},{4,7},{5,6},{6,5},{7,4},{8,11},{9,10},{10,... | collective-permute-start | bytes 294920 | tf_op jit(solution)/shard_map/ppermute | solution.py:345
  137.8 1.9 %collective-permute-start.30 = (bf16[192,256]{1,0:T(8,128)(2,1)S(1)}, bf16[192,256]{1,0:T(8,128)(2,1)S(1)}, u32[]{:S(2)}, u32[]{:S(2)}) collective-permute-start(bf16[192,256]{1,0:T(8,128)(2,1)S(1)} %get-tuple-element.36.c0), channel_id=1, source_target_pairs={{0,1},{1,0},{2,3},{3,2},{4,5},{5,4},{6,7},{7,6},{8,9},{9,8},{10,11... | collective-permute-start | bytes 294920 | tf_op jit(solution)/shard_map/ppermute | solution.py:345
  139.7 3.4 %copy-done.2 = bf16[1024,4096]{1,0:T(8,128)(2,1)S(1)} copy-done((bf16[1024,4096]{1,0:T(8,128)(2,1)S(1)}, bf16[1024,4096]{1,0:T(8,128)(2,1)}, u32[]{:S(2)}) %copy-start.2) | copy-done | bytes 8388632
  143.1 3.4 %copy-done.3 = bf16[4096,1024]{1,0:T(8,128)(2,1)S(1)} copy-done((bf16[4096,1024]{1,0:T(8,128)(2,1)S(1)}, bf16[4096,1024]{1,0:T(8,128)(2,1)}, u32[]{:S(2)}) %copy-start.3) | copy-done | bytes 8388632
  146.5 1.4 copy-done.7
  147.9 1.4 fetch.1
  149.3 6.1 %mlp.3 = (f32[192,1024]{1,0:T(8,128)S(1)}, f32[3,192,256]{2,1,0:T(8,128)S(1)}) custom-call(s32[4]{0:T(128)S(1)} %iota_xor_fusion.spots_ref.dest_ref, bf16[192,256]{1,0:T(8,128)(2,1)S(1)} %get-tuple-element.43.c0, bf16[192,256]{1,0:T(8,128)(2,1)S(1)} %collective-permute-done.36.c1, bf16[192,256]{1,0:T(8,128)(2,1)S(1)} %collective-permute-done.37.c2, ...), custom_call_target="tpu_custom_call" | custom-call | tf_op jit(solution)/shard_map/mlp/pallas_call | solution.py:327
  155.5 6.1 %mlp.2 = (f32[192,1024]{1,0:T(8,128)S(1)}, f32[3,192,256]{2,1,0:T(8,128)S(1)}) custom-call(s32[4]{0:T(128)S(1)} %iota_xor_fusion.spots_ref.dest_ref, bf16[192,256]{1,0:T(8,128)(2,1)S(1)} %get-tuple-element.36.c0, bf16[192,256]{1,0:T(8,128)(2,1)S(1)} %collective-permute-done.30.c1, bf16[192,256]{1,0:T(8,128)(2,1)S(1)} %collective-permute-done.31.c2, ...), custom_call_target="tpu_custom_call" | custom-call | tf_op jit(solution)/shard_map/mlp/pallas_call | solution.py:327
  161.6 1.1 pad_maximum_fusion
  (173 shorter events, 32.5 us)
Async XLA Ops:
  0.6 103.3 %copy-start = (bf16[1024,1024]{1,0:T(8,128)(2,1)S(1)}, bf16[1024,1024]{1,0:T(8,128)(2,1)}, u32[]{:S(2)}) copy-start(bf16[1024,1024]{1,0:T(8,128)(2,1)} %param.19) | copy-start | bytes 6291460
  0.6 61.8 %copy-start.58 = (s32[9]{0:T(128)S(1)}, s32[9]{0:T(128)}, u32[]{:S(2)}) copy-start(s32[9]{0:T(128)} %param.14) | copy-start | bytes 112
  0.7 62.0 %copy-start.59 = (s32[9]{0:T(128)S(1)}, s32[9]{0:T(128)}, u32[]{:S(2)}) copy-start(s32[9]{0:T(128)} %param.15) | copy-start | bytes 112
  0.7 62.2 %copy-start.57 = (s32[16]{0:T(128)S(1)}, s32[16]{0:T(128)}, u32[]{:S(2)}) copy-start(s32[16]{0:T(128)} %param.13) | copy-start | bytes 196
  0.7 9.9 %collective-permute-start.2 = (bf16[96,1024]{1,0:T(8,128)(2,1)}, bf16[96,1024]{1,0:T(8,128)(2,1)S(1)}, u32[]{:S(2)}, u32[]{:S(2)}) collective-permute-start(bf16[96,1024]{1,0:T(8,128)(2,1)} %x0.1), channel_id=1, source_target_pairs={{0,3},{1,2},{2,1},{3,0},{4,7},{5,6},{6,5},{7,4},{8,11},{9,10},{10,... | collective-permute-start | bytes 589832 | tf_op jit(solution)/shard_map/ppermute | solution.py:345
  4.3 16.9 %collective-permute-start.1 = (bf16[96,1024]{1,0:T(8,128)(2,1)}, bf16[96,1024]{1,0:T(8,128)(2,1)S(1)}, u32[]{:S(2)}, u32[]{:S(2)}) collective-permute-start(bf16[96,1024]{1,0:T(8,128)(2,1)} %x0.1), channel_id=1, source_target_pairs={{0,2},{1,3},{2,0},{3,1},{4,6},{5,7},{6,4},{7,5},{8,10},{9,11},{10,... | collective-permute-start | bytes 589832 | tf_op jit(solution)/shard_map/ppermute | solution.py:345
  4.3 23.5 %collective-permute-start = (bf16[96,1024]{1,0:T(8,128)(2,1)}, bf16[96,1024]{1,0:T(8,128)(2,1)}, u32[]{:S(2)}, u32[]{:S(2)}) collective-permute-start(bf16[96,1024]{1,0:T(8,128)(2,1)} %x0.1), channel_id=1, source_target_pairs={{0,1},{1,0},{2,3},{3,2},{4,5},{5,4},{6,7},{7,6},{8,9},{9,8},{10,11... | collective-permute-start | bytes 589832 | tf_op jit(solution)/shard_map/ppermute | solution.py:345
  5.1 22.8 %collective-permute-start.24 = (bf16[2,256,256]{2,1,0:T(8,128)(2,1)}, bf16[2,256,256]{2,1,0:T(8,128)(2,1)}, u32[]{:S(2)}, u32[]{:S(2)}) collective-permute-start(bf16[2,256,256]{2,1,0:T(8,128)(2,1)} %param.18), channel_id=1, source_target_pairs={{0,16},{4,20},{8,24},{12,28},{16,0},{20,4},{24,8},{28,12},{1,17},{... | collective-permute-start | bytes 786440 | tf_op jit(solution)/shard_map/ppermute | solution.py:352
  6.7 22.8 %collective-permute-start.23 = (bf16[2,256,256]{2,1,0:T(8,128)(2,1)}, bf16[2,256,256]{2,1,0:T(8,128)(2,1)}, u32[]{:S(2)}, u32[]{:S(2)}) collective-permute-start(bf16[2,256,256]{2,1,0:T(8,128)(2,1)} %param.18), channel_id=1, source_target_pairs={{0,8},{4,12},{8,0},{12,4},{16,24},{20,28},{24,16},{28,20},{1,9},{5... | collective-permute-start | bytes 786440 | tf_op jit(solution)/shard_map/ppermute | solution.py:352
  11.3 19.6 %collective-permute-start.26 = (bf16[2,256,256]{2,1,0:T(8,128)(2,1)}, bf16[2,256,256]{2,1,0:T(8,128)(2,1)S(1)}, u32[]{:S(2)}, u32[]{:S(2)}) collective-permute-start(bf16[2,256,256]{2,1,0:T(8,128)(2,1)} %param.18), channel_id=1, source_target_pairs={{0,4},{4,0},{8,12},{12,8},{16,20},{20,16},{24,28},{28,24},{1,5},{5... | collective-permute-start | bytes 786440 | tf_op jit(solution)/shard_map/ppermute | solution.py:353
  21.9 13.9 %collective-permute-start.25 = (bf16[2,256,256]{2,1,0:T(8,128)(2,1)}, bf16[2,256,256]{2,1,0:T(8,128)(2,1)}, u32[]{:S(2)}, u32[]{:S(2)}) collective-permute-start(bf16[2,256,256]{2,1,0:T(8,128)(2,1)} %param.18), channel_id=1, source_target_pairs={{0,24},{4,28},{8,16},{12,20},{16,8},{20,12},{24,0},{28,4},{1,25},{... | collective-permute-start | bytes 786440 | tf_op jit(solution)/shard_map/ppermute | solution.py:352
  26.8 24.8 %copy-start.12 = (bf16[256,1024]{1,0:T(8,128)(2,1)S(1)}, bf16[256,1024]{1,0:T(8,128)(2,1)}, u32[]{:S(2)}) copy-start(bf16[256,1024]{1,0:T(8,128)(2,1)} %refs_0_.2) | copy-start | bytes 1572868
  27.8 8.0 %collective-permute-start.13 = (bf16[2,192,256]{2,1,0:T(8,128)(2,1)S(1)}, bf16[2,192,256]{2,1,0:T(8,128)(2,1)S(1)}, u32[]{:S(2)}, u32[]{:S(2)}) collective-permute-start(bf16[2,192,256]{2,1,0:T(8,128)(2,1)S(1)} %get-tuple-element.29), channel_id=1, source_target_pairs={{0,4},{4,0},{8,12},{12,8},{16,20},{20,16},{24,28},{28,24},{1,5},{5... | collective-permute-start | bytes 589832 | tf_op jit(solution)/shard_map/ppermute | solution.py:353
  27.9 10.1 %collective-permute-start.12 = (bf16[2,192,256]{2,1,0:T(8,128)(2,1)S(1)}, bf16[2,192,256]{2,1,0:T(8,128)(2,1)S(1)}, u32[]{:S(2)}, u32[]{:S(2)}) collective-permute-start(bf16[2,192,256]{2,1,0:T(8,128)(2,1)S(1)} %get-tuple-element.29), channel_id=1, source_target_pairs={{0,24},{4,28},{8,16},{12,20},{16,8},{20,12},{24,0},{28,4},{1,25},{... | collective-permute-start | bytes 589832 | tf_op jit(solution)/shard_map/ppermute | solution.py:352
  29.4 10.9 %collective-permute-start.11 = (bf16[2,192,256]{2,1,0:T(8,128)(2,1)S(1)}, bf16[2,192,256]{2,1,0:T(8,128)(2,1)S(1)}, u32[]{:S(2)}, u32[]{:S(2)}) collective-permute-start(bf16[2,192,256]{2,1,0:T(8,128)(2,1)S(1)} %get-tuple-element.29), channel_id=1, source_target_pairs={{0,16},{4,20},{8,24},{12,28},{16,0},{20,4},{24,8},{28,12},{1,17},{... | collective-permute-start | bytes 589832 | tf_op jit(solution)/shard_map/ppermute | solution.py:352
  31.6 10.2 %collective-permute-start.10 = (bf16[2,192,256]{2,1,0:T(8,128)(2,1)S(1)}, bf16[2,192,256]{2,1,0:T(8,128)(2,1)S(1)}, u32[]{:S(2)}, u32[]{:S(2)}) collective-permute-start(bf16[2,192,256]{2,1,0:T(8,128)(2,1)S(1)} %get-tuple-element.29), channel_id=1, source_target_pairs={{0,8},{4,12},{8,0},{12,4},{16,24},{20,28},{24,16},{28,20},{1,9},{5... | collective-permute-start | bytes 589832 | tf_op jit(solution)/shard_map/ppermute | solution.py:352
  35.9 5.9 %collective-permute-start.6 = (bf16[2,192,256]{2,1,0:T(8,128)(2,1)S(1)}, bf16[2,192,256]{2,1,0:T(8,128)(2,1)S(1)}, u32[]{:S(2)}, u32[]{:S(2)}) collective-permute-start(bf16[2,192,256]{2,1,0:T(8,128)(2,1)S(1)} %get-tuple-element.28), channel_id=1, source_target_pairs={{0,4},{4,0},{8,12},{12,8},{16,20},{20,16},{24,28},{28,24},{1,5},{5... | collective-permute-start | bytes 589832 | tf_op jit(solution)/shard_map/ppermute | solution.py:353
  36.5 8.6 %collective-permute-start.5 = (bf16[2,192,256]{2,1,0:T(8,128)(2,1)S(1)}, bf16[2,192,256]{2,1,0:T(8,128)(2,1)S(1)}, u32[]{:S(2)}, u32[]{:S(2)}) collective-permute-start(bf16[2,192,256]{2,1,0:T(8,128)(2,1)S(1)} %get-tuple-element.28), channel_id=1, source_target_pairs={{0,24},{4,28},{8,16},{12,20},{16,8},{20,12},{24,0},{28,4},{1,25},{... | collective-permute-start | bytes 589832 | tf_op jit(solution)/shard_map/ppermute | solution.py:352
  38.0 11.0 %collective-permute-start.4 = (bf16[2,192,256]{2,1,0:T(8,128)(2,1)S(1)}, bf16[2,192,256]{2,1,0:T(8,128)(2,1)S(1)}, u32[]{:S(2)}, u32[]{:S(2)}) collective-permute-start(bf16[2,192,256]{2,1,0:T(8,128)(2,1)S(1)} %get-tuple-element.28), channel_id=1, source_target_pairs={{0,16},{4,20},{8,24},{12,28},{16,0},{20,4},{24,8},{28,12},{1,17},{... | collective-permute-start | bytes 589832 | tf_op jit(solution)/shard_map/ppermute | solution.py:352
  40.3 9.4 %collective-permute-start.3 = (bf16[2,192,256]{2,1,0:T(8,128)(2,1)S(1)}, bf16[2,192,256]{2,1,0:T(8,128)(2,1)S(1)}, u32[]{:S(2)}, u32[]{:S(2)}) collective-permute-start(bf16[2,192,256]{2,1,0:T(8,128)(2,1)S(1)} %get-tuple-element.28), channel_id=1, source_target_pairs={{0,8},{4,12},{8,0},{12,4},{16,24},{20,28},{24,16},{28,20},{1,9},{5... | collective-permute-start | bytes 589832 | tf_op jit(solution)/shard_map/ppermute | solution.py:352
  41.8 9.1 %collective-permute-start.28 = (bf16[2,256,256]{2,1,0:T(8,128)(2,1)}, bf16[2,256,256]{2,1,0:T(8,128)(2,1)S(1)}, u32[]{:S(2)}, u32[]{:S(2)}) collective-permute-start(bf16[2,256,256]{2,1,0:T(8,128)(2,1)} %collective-permute-done.24), channel_id=1, source_target_pairs={{0,4},{4,0},{8,12},{12,8},{16,20},{20,16},{24,28},{28,24},{1,5},{5... | collective-permute-start | bytes 786440 | tf_op jit(solution)/shard_map/ppermute | solution.py:353
  42.5 9.1 %collective-permute-start.16 = (bf16[2,192,256]{2,1,0:T(8,128)(2,1)S(1)}, bf16[2,192,256]{2,1,0:T(8,128)(2,1)S(1)}, u32[]{:S(2)}, u32[]{:S(2)}) collective-permute-start(bf16[2,192,256]{2,1,0:T(8,128)(2,1)S(1)} %collective-permute-done.12), channel_id=1, source_target_pairs={{0,4},{4,0},{8,12},{12,8},{16,20},{20,16},{24,28},{28,24},{1,5},{5... | collective-permute-start | bytes 589832 | tf_op jit(solution)/shard_map/ppermute | solution.py:353
  45.2 7.8 %collective-permute-start.15 = (bf16[2,192,256]{2,1,0:T(8,128)(2,1)S(1)}, bf16[2,192,256]{2,1,0:T(8,128)(2,1)S(1)}, u32[]{:S(2)}, u32[]{:S(2)}) collective-permute-start(bf16[2,192,256]{2,1,0:T(8,128)(2,1)S(1)} %collective-permute-done.11), channel_id=1, source_target_pairs={{0,4},{4,0},{8,12},{12,8},{16,20},{20,16},{24,28},{28,24},{1,5},{5... | collective-permute-start | bytes 589832 | tf_op jit(solution)/shard_map/ppermute | solution.py:353
  49.0 5.9 %collective-permute-start.14 = (bf16[2,192,256]{2,1,0:T(8,128)(2,1)S(1)}, bf16[2,192,256]{2,1,0:T(8,128)(2,1)S(1)}, u32[]{:S(2)}, u32[]{:S(2)}) collective-permute-start(bf16[2,192,256]{2,1,0:T(8,128)(2,1)S(1)} %collective-permute-done.10), channel_id=1, source_target_pairs={{0,4},{4,0},{8,12},{12,8},{16,20},{20,16},{24,28},{28,24},{1,5},{5... | collective-permute-start | bytes 589832 | tf_op jit(solution)/shard_map/ppermute | solution.py:353
  49.7 8.8 %collective-permute-start.9 = (bf16[2,192,256]{2,1,0:T(8,128)(2,1)S(1)}, bf16[2,192,256]{2,1,0:T(8,128)(2,1)S(1)}, u32[]{:S(2)}, u32[]{:S(2)}) collective-permute-start(bf16[2,192,256]{2,1,0:T(8,128)(2,1)S(1)} %collective-permute-done.5), channel_id=1, source_target_pairs={{0,4},{4,0},{8,12},{12,8},{16,20},{20,16},{24,28},{28,24},{1,5},{5... | collective-permute-start | bytes 589832 | tf_op jit(solution)/shard_map/ppermute | solution.py:353
  51.6 50.4 %collective-permute-start.21 = (bf16[256,1024]{1,0:T(8,128)(2,1)S(1)}, bf16[256,1024]{1,0:T(8,128)(2,1)}, u32[]{:S(2)}, u32[]{:S(2)}) collective-permute-start(bf16[256,1024]{1,0:T(8,128)(2,1)S(1)} %copy-done.12), channel_id=1, source_target_pairs={{0,2},{1,3},{2,0},{3,1},{4,6},{5,7},{6,4},{7,5},{8,10},{9,11},{10,... | collective-permute-start | bytes 1572872 | tf_op jit(solution)/shard_map/ppermute | solution.py:345
  52.3 8.3 %collective-permute-start.8 = (bf16[2,192,256]{2,1,0:T(8,128)(2,1)S(1)}, bf16[2,192,256]{2,1,0:T(8,128)(2,1)S(1)}, u32[]{:S(2)}, u32[]{:S(2)}) collective-permute-start(bf16[2,192,256]{2,1,0:T(8,128)(2,1)S(1)} %collective-permute-done.4), channel_id=1, source_target_pairs={{0,4},{4,0},{8,12},{12,8},{16,20},{20,16},{24,28},{28,24},{1,5},{5... | collective-permute-start | bytes 589832 | tf_op jit(solution)/shard_map/ppermute | solution.py:353
  53.7 7.6 %collective-permute-start.7 = (bf16[2,192,256]{2,1,0:T(8,128)(2,1)S(1)}, bf16[2,192,256]{2,1,0:T(8,128)(2,1)S(1)}, u32[]{:S(2)}, u32[]{:S(2)}) collective-permute-start(bf16[2,192,256]{2,1,0:T(8,128)(2,1)S(1)} %collective-permute-done.3), channel_id=1, source_target_pairs={{0,4},{4,0},{8,12},{12,8},{16,20},{20,16},{24,28},{28,24},{1,5},{5... | collective-permute-start | bytes 589832 | tf_op jit(solution)/shard_map/ppermute | solution.py:353
  55.5 51.6 %collective-permute-start.20 = (bf16[256,1024]{1,0:T(8,128)(2,1)S(1)}, bf16[256,1024]{1,0:T(8,128)(2,1)}, u32[]{:S(2)}, u32[]{:S(2)}) collective-permute-start(bf16[256,1024]{1,0:T(8,128)(2,1)S(1)} %copy-done.12), channel_id=1, source_target_pairs={{0,1},{1,0},{2,3},{3,2},{4,5},{5,4},{6,7},{7,6},{8,9},{9,8},{10,11... | collective-permute-start | bytes 1572872 | tf_op jit(solution)/shard_map/ppermute | solution.py:345
  59.2 47.9 %collective-permute-start.22 = (bf16[256,1024]{1,0:T(8,128)(2,1)S(1)}, bf16[256,1024]{1,0:T(8,128)(2,1)}, u32[]{:S(2)}, u32[]{:S(2)}) collective-permute-start(bf16[256,1024]{1,0:T(8,128)(2,1)S(1)} %copy-done.12), channel_id=1, source_target_pairs={{0,3},{1,2},{2,1},{3,0},{4,7},{5,6},{6,5},{7,4},{8,11},{9,10},{10,... | collective-permute-start | bytes 1572872 | tf_op jit(solution)/shard_map/ppermute | solution.py:345
  61.3 38.2 %collective-permute-start.27 = (bf16[2,256,256]{2,1,0:T(8,128)(2,1)}, bf16[2,256,256]{2,1,0:T(8,128)(2,1)}, u32[]{:S(2)}, u32[]{:S(2)}) collective-permute-start(bf16[2,256,256]{2,1,0:T(8,128)(2,1)} %collective-permute-done.23), channel_id=1, source_target_pairs={{0,4},{4,0},{8,12},{12,8},{16,20},{20,16},{24,28},{28,24},{1,5},{5... | collective-permute-start | bytes 786440 | tf_op jit(solution)/shard_map/ppermute | solution.py:353
  61.9 40.0 %collective-permute-start.29 = (bf16[2,256,256]{2,1,0:T(8,128)(2,1)}, bf16[2,256,256]{2,1,0:T(8,128)(2,1)}, u32[]{:S(2)}, u32[]{:S(2)}) collective-permute-start(bf16[2,256,256]{2,1,0:T(8,128)(2,1)} %collective-permute-done.25), channel_id=1, source_target_pairs={{0,4},{4,0},{8,12},{12,8},{16,20},{20,16},{24,28},{28,24},{1,5},{5... | collective-permute-start | bytes 786440 | tf_op jit(solution)/shard_map/ppermute | solution.py:353
  73.8 21.3 %copy-start.14 = (bf16[192,256]{1,0:T(8,128)(2,1)S(1)}, bf16[192,256]{1,0:T(8,128)(2,1)}, u32[]{:S(2)}) copy-start(bf16[192,256]{1,0:T(8,128)(2,1)} %copy-done.13) | copy-start | bytes 294916
  95.2 8.8 %copy-start.15 = (bf16[2,256,256]{2,1,0:T(8,128)(2,1)S(1)}, bf16[2,256,256]{2,1,0:T(8,128)(2,1)}, u32[]{:S(2)}) copy-start(bf16[2,256,256]{2,1,0:T(8,128)(2,1)} %param.18) | copy-start | bytes 786436
  99.4 19.3 %collective-permute-start.35 = (bf16[192,256]{1,0:T(8,128)(2,1)S(1)}, bf16[192,256]{1,0:T(8,128)(2,1)S(1)}, u32[]{:S(2)}, u32[]{:S(2)}) collective-permute-start(bf16[192,256]{1,0:T(8,128)(2,1)S(1)} %self_attention.3.a0), channel_id=1, source_target_pairs={{0,3},{1,2},{2,1},{3,0},{4,7},{5,6},{6,5},{7,4},{8,11},{9,10},{10,... | collective-permute-start | bytes 294920 | tf_op jit(solution)/shard_map/ppermute | solution.py:345
  102.0 18.7 %collective-permute-start.34 = (bf16[192,256]{1,0:T(8,128)(2,1)S(1)}, bf16[192,256]{1,0:T(8,128)(2,1)S(1)}, u32[]{:S(2)}, u32[]{:S(2)}) collective-permute-start(bf16[192,256]{1,0:T(8,128)(2,1)S(1)} %self_attention.3.a0), channel_id=1, source_target_pairs={{0,2},{1,3},{2,0},{3,1},{4,6},{5,7},{6,4},{7,5},{8,10},{9,11},{10,... | collective-permute-start | bytes 294920 | tf_op jit(solution)/shard_map/ppermute | solution.py:345
  102.0 18.7 %collective-permute-start.33 = (bf16[192,256]{1,0:T(8,128)(2,1)S(1)}, bf16[192,256]{1,0:T(8,128)(2,1)S(1)}, u32[]{:S(2)}, u32[]{:S(2)}) collective-permute-start(bf16[192,256]{1,0:T(8,128)(2,1)S(1)} %self_attention.3.a0), channel_id=1, source_target_pairs={{0,1},{1,0},{2,3},{3,2},{4,5},{5,4},{6,7},{7,6},{8,9},{9,8},{10,11... | collective-permute-start | bytes 294920 | tf_op jit(solution)/shard_map/ppermute | solution.py:345
  116.2 11.6 %collective-permute-start.19 = (bf16[192,256]{1,0:T(8,128)(2,1)S(1)}, bf16[192,256]{1,0:T(8,128)(2,1)S(1)}, u32[]{:S(2)}, u32[]{:S(2)}) collective-permute-start(bf16[192,256]{1,0:T(8,128)(2,1)S(1)} %self_attention.2.a0), channel_id=1, source_target_pairs={{0,3},{1,2},{2,1},{3,0},{4,7},{5,6},{6,5},{7,4},{8,11},{9,10},{10,... | collective-permute-start | bytes 294920 | tf_op jit(solution)/shard_map/ppermute | solution.py:345
  118.8 10.9 %collective-permute-start.18 = (bf16[192,256]{1,0:T(8,128)(2,1)S(1)}, bf16[192,256]{1,0:T(8,128)(2,1)S(1)}, u32[]{:S(2)}, u32[]{:S(2)}) collective-permute-start(bf16[192,256]{1,0:T(8,128)(2,1)S(1)} %self_attention.2.a0), channel_id=1, source_target_pairs={{0,2},{1,3},{2,0},{3,1},{4,6},{5,7},{6,4},{7,5},{8,10},{9,11},{10,... | collective-permute-start | bytes 294920 | tf_op jit(solution)/shard_map/ppermute | solution.py:345
  118.8 10.9 %collective-permute-start.17 = (bf16[192,256]{1,0:T(8,128)(2,1)S(1)}, bf16[192,256]{1,0:T(8,128)(2,1)S(1)}, u32[]{:S(2)}, u32[]{:S(2)}) collective-permute-start(bf16[192,256]{1,0:T(8,128)(2,1)S(1)} %self_attention.2.a0), channel_id=1, source_target_pairs={{0,1},{1,0},{2,3},{3,2},{4,5},{5,4},{6,7},{7,6},{8,9},{9,8},{10,11... | collective-permute-start | bytes 294920 | tf_op jit(solution)/shard_map/ppermute | solution.py:345
  125.2 9.2 %copy-start.8 = (f32[192,1024]{1,0:T(8,128)}, f32[192,1024]{1,0:T(8,128)S(1)}, u32[]{:S(2)}) copy-start(f32[192,1024]{1,0:T(8,128)S(1)} %get-tuple-element.44.hidden_ref) | copy-start | bytes 2359300
  125.2 14.5 %copy-start.6 = (bf16[1024,1024]{1,0:T(8,128)(2,1)S(1)}, bf16[1024,1024]{1,0:T(8,128)(2,1)}, u32[]{:S(2)}) copy-start(bf16[1024,1024]{1,0:T(8,128)(2,1)} %refs_0_.3) | copy-start | bytes 6291460
  125.2 12.6 %collective-permute-start.38 = (bf16[192,256]{1,0:T(8,128)(2,1)S(1)}, bf16[192,256]{1,0:T(8,128)(2,1)S(1)}, u32[]{:S(2)}, u32[]{:S(2)}) collective-permute-start(bf16[192,256]{1,0:T(8,128)(2,1)S(1)} %get-tuple-element.43.c0), channel_id=1, source_target_pairs={{0,3},{1,2},{2,1},{3,0},{4,7},{5,6},{6,5},{7,4},{8,11},{9,10},{10,... | collective-permute-start | bytes 294920 | tf_op jit(solution)/shard_map/ppermute | solution.py:345
  127.8 21.5 %collective-permute-start.37 = (bf16[192,256]{1,0:T(8,128)(2,1)S(1)}, bf16[192,256]{1,0:T(8,128)(2,1)S(1)}, u32[]{:S(2)}, u32[]{:S(2)}) collective-permute-start(bf16[192,256]{1,0:T(8,128)(2,1)S(1)} %get-tuple-element.43.c0), channel_id=1, source_target_pairs={{0,2},{1,3},{2,0},{3,1},{4,6},{5,7},{6,4},{7,5},{8,10},{9,11},{10,... | collective-permute-start | bytes 294920 | tf_op jit(solution)/shard_map/ppermute | solution.py:345
  127.8 21.5 %collective-permute-start.36 = (bf16[192,256]{1,0:T(8,128)(2,1)S(1)}, bf16[192,256]{1,0:T(8,128)(2,1)S(1)}, u32[]{:S(2)}, u32[]{:S(2)}) collective-permute-start(bf16[192,256]{1,0:T(8,128)(2,1)S(1)} %get-tuple-element.43.c0), channel_id=1, source_target_pairs={{0,1},{1,0},{2,3},{3,2},{4,5},{5,4},{6,7},{7,6},{8,9},{9,8},{10,11... | collective-permute-start | bytes 294920 | tf_op jit(solution)/shard_map/ppermute | solution.py:345
  135.3 20.1 %collective-permute-start.32 = (bf16[192,256]{1,0:T(8,128)(2,1)S(1)}, bf16[192,256]{1,0:T(8,128)(2,1)S(1)}, u32[]{:S(2)}, u32[]{:S(2)}) collective-permute-start(bf16[192,256]{1,0:T(8,128)(2,1)S(1)} %get-tuple-element.36.c0), channel_id=1, source_target_pairs={{0,3},{1,2},{2,1},{3,0},{4,7},{5,6},{6,5},{7,4},{8,11},{9,10},{10,... | collective-permute-start | bytes 294920 | tf_op jit(solution)/shard_map/ppermute | solution.py:345
  137.8 17.7 %collective-permute-start.31 = (bf16[192,256]{1,0:T(8,128)(2,1)S(1)}, bf16[192,256]{1,0:T(8,128)(2,1)S(1)}, u32[]{:S(2)}, u32[]{:S(2)}) collective-permute-start(bf16[192,256]{1,0:T(8,128)(2,1)S(1)} %get-tuple-element.36.c0), channel_id=1, source_target_pairs={{0,2},{1,3},{2,0},{3,1},{4,6},{5,7},{6,4},{7,5},{8,10},{9,11},{10,... | collective-permute-start | bytes 294920 | tf_op jit(solution)/shard_map/ppermute | solution.py:345
  137.8 17.7 %collective-permute-start.30 = (bf16[192,256]{1,0:T(8,128)(2,1)S(1)}, bf16[192,256]{1,0:T(8,128)(2,1)S(1)}, u32[]{:S(2)}, u32[]{:S(2)}) collective-permute-start(bf16[192,256]{1,0:T(8,128)(2,1)S(1)} %get-tuple-element.36.c0), channel_id=1, source_target_pairs={{0,1},{1,0},{2,3},{3,2},{4,5},{5,4},{6,7},{7,6},{8,9},{9,8},{10,11... | collective-permute-start | bytes 294920 | tf_op jit(solution)/shard_map/ppermute | solution.py:345
  (51 other events, 75.7 us)

commit v2 on v1

v2 whole, which is shorter than its diff:
```python
import functools
import math

import jax
import jax.numpy as jnp
from jax import lax
from jax.experimental import pallas as pl
from jax.experimental.pallas import tpu as pltpu
from jax.sharding import PartitionSpec as P

HEADS = 16
NEGATIVE = -1e30
SCALING = 0.125
EPSILON = 1e-05
TILE = 256
MIB = 1024 * 1024


def whole(count):
    return [pl.BlockSpec(memory_space=pltpu.VMEM)] * count


def anywhere(count):
    return [pl.BlockSpec(memory_space=pl.ANY)] * count


def smem(count):
    return [pl.BlockSpec(memory_space=pltpu.SMEM)] * count


def params(mib):
    return pltpu.CompilerParams(vmem_limit_bytes=mib * MIB)


def xor(size, bits):
    return [(i, i ^ bits) for i in range(size)]


def normalize(matrix):
    center = matrix - jnp.mean(matrix, axis=-1, keepdims=True)
    return center * lax.rsqrt(jnp.mean(center * center, axis=-1, keepdims=True) + EPSILON)


def cost(flops, moved):
    return pl.CostEstimate(flops=int(flops) // 20, bytes_accessed=int(moved) // 20, transcendentals=0)


def skipping(kernel, at, count):
    def body(*refs):
        kernel(*refs[:at], *refs[at + count :])

    return body


def rows_at(index, rows):
    return pl.ds(pl.multiple_of(index * rows, rows), rows)


def sums_of(lengths_ref):
    sums, total = [], jnp.int32(0)
    for j in range(lengths_ref.shape[0]):
        total = total + lengths_ref[j]
        sums.append(total)
    return sums


def project_kernel(ids_ref, x0, x1, x2, x3, w_ref, wo_ref, x_ref, q_ref, kv_ref, part_ref):
    part_ref[...] = wo_ref[rows_at(ids_ref[0] % 2, part_ref.shape[0]), :]
    for i, piece in enumerate((x0, x1, x2, x3)):
        x_ref[rows_at(ids_ref[1] ^ i, x0.shape[0]), :] = piece[...]
    x = x_ref[...]
    for c in range(2):
        kv_ref[c] = jnp.dot(x, w_ref[1 + c], preferred_element_type=jnp.float32).astype(
            jnp.bfloat16
        )
    q_ref[...] = jnp.dot(x, w_ref[0], preferred_element_type=jnp.float32).astype(jnp.bfloat16)


def project(ids, pieces, w_qkv, w_out):
    rows, width, model = 4 * pieces[0].shape[0], w_qkv.shape[2], pieces[0].shape[1]
    return pl.pallas_call(
        project_kernel,
        out_shape=(
            jax.ShapeDtypeStruct((rows, model), jnp.bfloat16),
            jax.ShapeDtypeStruct((rows, width), jnp.bfloat16),
            jax.ShapeDtypeStruct((2, rows, width), jnp.bfloat16),
            jax.ShapeDtypeStruct((width // 2, w_out.shape[1]), jnp.bfloat16),
        ),
        in_specs=smem(1) + whole(6),
        out_specs=tuple(whole(4)),
        compiler_params=params(4),
        cost_estimate=cost(2 * rows * model * 3 * width, 2 * 3 * model * width),
        name="project",
    )(ids, *pieces, w_qkv, w_out)


def fetch_kernel(count, columns, ids_ref, *refs):
    sem = refs[-1]
    copies = []
    for i in range(count):
        source, target = refs[i], refs[count + i]
        if i in columns:
            width = target.shape[1]
            source = source.at[:, pl.ds(pl.multiple_of(ids_ref[1] * width, width), width)]
        copy = pltpu.make_async_copy(source, target, sem)
        copy.start()
        copies.append(copy)
    for copy in copies:
        copy.wait()


def fetch(ids, arrays, columns, room, after):
    count = len(arrays)
    shapes = [(a.shape[0], columns[i]) if i in columns else a.shape for i, a in enumerate(arrays)]
    return pl.pallas_call(
        skipping(functools.partial(fetch_kernel, count, columns), 1 + count, len(after)),
        out_shape=tuple(jax.ShapeDtypeStruct(s, a.dtype) for s, a in zip(shapes, arrays)),
        in_specs=smem(1) + anywhere(count + len(after)),
        out_specs=tuple(whole(count)),
        scratch_shapes=[pltpu.SemaphoreType.DMA],
        compiler_params=params(room),
        cost_estimate=cost(0, 2 * sum(math.prod(s) for s in shapes)),
        name="fetch",
    )(ids, *arrays, *after)


def bundle_kernel(groups, *refs):
    at = sum(groups)
    for i, count in enumerate(groups):
        for j in range(count):
            refs[at + i][j] = refs[sum(groups[:i]) + j][...]


def bundle(groups, after):
    counts = [len(g) for g in groups]
    total = sum(counts)
    return pl.pallas_call(
        skipping(functools.partial(bundle_kernel, counts), total, len(after)),
        out_shape=tuple(jax.ShapeDtypeStruct((len(g),) + g[0].shape, g[0].dtype) for g in groups),
        in_specs=whole(total) + anywhere(len(after)),
        out_specs=tuple(whole(len(groups))),
        compiler_params=params(2),
        cost_estimate=cost(0, 2 * 2 * sum(len(g) * math.prod(g[0].shape) for g in groups)),
        name="bundle",
    )(*[x for g in groups for x in g], *after)


def spread(values, v_ref, at):
    lane = lax.broadcasted_iota(jnp.int32, (values.shape[0], 128), 1) // 64
    for head in range(v_ref.shape[0]):
        pair = values[:, (head // 2) * 128 : (head // 2 + 1) * 128]
        v_ref[head, at, :] = jnp.where(lane == head % 2, pair, jnp.ones_like(pair))


def order_kernel(sources, ids_ref, order_ref, *refs):
    k_ref, v_ref, cache_ref = refs[-3:]
    for ref, (relative, numbers) in zip(refs, sources):
        rows = ref.shape[2] // 2
        for piece, number in enumerate(numbers):
            block = ids_ref[0] ^ number if relative else jnp.int32(number)
            for half in range(2):
                at = rows_at(order_ref[2 * block + half], rows)
                here = slice(half * rows, (half + 1) * rows)
                k_ref[at, :] = ref[piece, 0, here, :]
                spread(ref[piece, 1, here, :], v_ref, at)
    length = cache_ref.shape[1]
    at = rows_at(ids_ref[0], length)
    cache_ref[0] = k_ref[at, :]
    lane = lax.broadcasted_iota(jnp.int32, (length, 128), 1) // 64
    for pair in range(v_ref.shape[0] // 2):
        cache_ref[1, :, pair * 128 : (pair + 1) * 128] = jnp.where(
            lane == 0, v_ref[2 * pair, at, :], v_ref[2 * pair + 1, at, :]
        )


def order(ids, block_order, chunks, sources):
    rows, width = chunks[0].shape[2:]
    total = rows * sum(c.shape[0] for c in chunks)
    return pl.pallas_call(
        functools.partial(order_kernel, sources),
        out_shape=(
            jax.ShapeDtypeStruct((total, width), jnp.bfloat16),
            jax.ShapeDtypeStruct((width // 64, total, 128), jnp.bfloat16),
            jax.ShapeDtypeStruct((2, rows, width), jnp.bfloat16),
        ),
        in_specs=smem(2) + whole(len(chunks)),
        out_specs=tuple(whole(3)),
        compiler_params=params(4),
        cost_estimate=cost(0, 5 * 2 * total * width),
        name="order",
    )(ids, block_order, *chunks)


def prepare_kernel(sources, ids_ref, *refs):
    k_ref, v_ref, w_ref = refs[-3:]
    for ref, (relative, numbers) in zip(refs, sources):
        rows = ref.shape[2]
        for piece, number in enumerate(numbers):
            at = rows_at(ids_ref[0] ^ number if relative else jnp.int32(number), rows)
            k_ref[at, :] = ref[piece, 0]
            spread(ref[piece, 1], v_ref, at)
    parts = refs[len(sources) : -3]
    for i, part in enumerate(parts):
        for j in range(part.shape[0]):
            w_ref[ids_ref[1] ^ j, ids_ref[0] % 2 ^ i] = part[j]


def prepare(ids, chunks, sources, parts):
    rows, width = chunks[0].shape[2:]
    total = rows * sum(c.shape[0] for c in chunks)
    group, depth, model = parts[0].shape
    return pl.pallas_call(
        functools.partial(prepare_kernel, sources),
        out_shape=(
            jax.ShapeDtypeStruct((total, width), jnp.bfloat16),
            jax.ShapeDtypeStruct((width // 64, total, 128), jnp.bfloat16),
            jax.ShapeDtypeStruct((group, 2, depth, model), jnp.bfloat16),
        ),
        in_specs=smem(1) + whole(len(chunks) + len(parts)),
        out_specs=tuple(whole(3)),
        compiler_params=params(4),
        cost_estimate=cost(0, 5 * 2 * total * width),
        name="prepare",
    )(ids, *chunks, *parts)


def flash(queries, k_ref, v_ref, low, high, first, last):
    rows, width = queries.shape
    heads = width // 64
    lane = lax.broadcasted_iota(jnp.int32, (rows, 128), 1) // 64
    masked = []
    for head in range(heads):
        pair = queries[:, (head // 2) * 128 : (head // 2 + 1) * 128]
        pair = (pair.astype(jnp.float32) * SCALING).astype(jnp.bfloat16)
        masked.append(jnp.where(lane == head % 2, pair, jnp.zeros_like(pair)))

    def step(tile, carry):
        start = pl.multiple_of(tile * TILE, TILE)
        keys = start + lax.broadcasted_iota(jnp.int32, (rows, TILE), 1)
        seen = (keys >= low) & (keys < high)
        bias = jnp.where(seen, 0.0, NEGATIVE)
        after = []
        for head in range(heads):
            peak, total = carry[head]
            at = slice((head // 2) * 128, (head // 2 + 1) * 128)
            scores = lax.dot_general(
                masked[head],
                k_ref[pl.ds(start, TILE), at],
                (((1,), (1,)), ((), ())),
                preferred_element_type=jnp.float32,
            )
            scores = scores + bias
            top = jnp.maximum(peak, jnp.max(scores, axis=1, keepdims=True))
            weights = jnp.exp(scores - top)
            total = total * jnp.exp(peak - top) + jnp.dot(
                weights.astype(jnp.bfloat16),
                v_ref[head, pl.ds(start, TILE), :],
                preferred_element_type=jnp.float32,
            )
            after.append((top, total))
        return tuple(after)

    begin = tuple(
        (jnp.full((rows, 1), NEGATIVE, jnp.float32), jnp.zeros((rows, 128), jnp.float32))
        for _ in range(heads)
    )
    carry = lax.fori_loop(first, last + 1, step, begin)
    outs = []
    for pair in range(heads // 2):
        even, odd = carry[2 * pair][1], carry[2 * pair + 1][1]
        sums = pltpu.roll(jnp.where(lane == 0, odd, even), 64, 1)
        outs.append(jnp.where(lane == 0, even, odd) / sums)
    return jnp.concatenate(outs, axis=1)


def half_of(turn, ids_ref, order_ref):
    first = order_ref[2 * ids_ref[0]]
    second = order_ref[2 * ids_ref[0] + 1]
    return jnp.where(first < second, turn, 1 - turn)


def self_kernel(turn, ids_ref, order_ref, lengths_ref, q_ref, k_ref, v_ref, out_ref):
    rows = out_ref.shape[0]
    half = half_of(turn, ids_ref, order_ref)
    queries = q_ref[rows_at(half, rows), :]
    base = order_ref[2 * ids_ref[0] + half] * rows
    places = base + lax.broadcasted_iota(jnp.int32, (rows, 1), 0)
    low = jnp.zeros((rows, 1), jnp.int32)
    least = jnp.int32(0)
    for end in sums_of(lengths_ref):
        low = jnp.where(places >= end, end, low)
        least = jnp.where(base >= end, end, least)
    first, last = least // TILE, (base + rows - 1) // TILE
    result = flash(queries, k_ref, v_ref, low, places + 1, first, last)
    out_ref[...] = result.astype(jnp.bfloat16)


def self_attention(turn, ids, block_order, lengths, queries, keys, values):
    rows, width = queries.shape
    return pl.pallas_call(
        functools.partial(self_kernel, turn),
        out_shape=jax.ShapeDtypeStruct((rows // 2, width), jnp.bfloat16),
        in_specs=smem(3) + whole(3),
        out_specs=whole(1)[0],
        compiler_params=params(4),
        cost_estimate=cost(5e9, 0),
        name="self_attention",
    )(ids, block_order, lengths, queries, keys, values)


def cross_kernel(
    turn, ids_ref, order_ref, lengths_ref, encs_ref,
    a0, a1, a2, a3, x_ref, wo_ref, wq_ref, k_ref, v_ref, hidden_ref, out_ref,
):
    rows, width = a0.shape
    member = ids_ref[1]
    half = half_of(turn, ids_ref, order_ref)
    mixed = x_ref[rows_at(half, rows), :].astype(jnp.float32)
    for i, piece in enumerate((a0, a1, a2, a3)):
        mixed = mixed + jnp.dot(
            piece[...], wo_ref[member ^ i], preferred_element_type=jnp.float32
        )
    hidden = normalize(mixed)
    hidden_ref[...] = hidden
    queries = jnp.dot(
        hidden.astype(jnp.bfloat16), wq_ref[...], preferred_element_type=jnp.float32
    ).astype(jnp.bfloat16)
    base = order_ref[2 * ids_ref[0] + half] * rows
    places = base + lax.broadcasted_iota(jnp.int32, (rows, 1), 0)
    ends, encs = sums_of(lengths_ref), sums_of(encs_ref)
    low = jnp.zeros((rows, 1), jnp.int32)
    least = jnp.int32(0)
    for end, enc in zip(ends, encs):
        low = jnp.where(places >= end, enc, low)
        least = jnp.where(base >= end, enc, least)
    high = jnp.full((rows, 1), encs[-1], jnp.int32)
    most = encs[-1]
    for end, enc in zip(reversed(ends), reversed(encs)):
        high = jnp.where(places < end, enc, high)
        most = jnp.where(base + rows - 1 < end, enc, most)
    result = flash(queries, k_ref, v_ref, low, high, least // TILE, (most - 1) // TILE)
    out_ref[...] = result.astype(jnp.bfloat16)


def cross_attention(turn, ids, block_order, lengths, encs, pieces, x, w_out, w_cq, keys, values):
    rows, width = pieces[0].shape
    model = x.shape[1]
    return pl.pallas_call(
        functools.partial(cross_kernel, turn),
        out_shape=(
            jax.ShapeDtypeStruct((rows, model), jnp.float32),
            jax.ShapeDtypeStruct((rows, width), jnp.bfloat16),
        ),
        in_specs=smem(4) + whole(9),
        out_specs=tuple(whole(2)),
        compiler_params=params(5),
        cost_estimate=cost(5e9, 0),
        name="cross_attention",
    )(ids, block_order, lengths, encs, *pieces, x, w_out, w_cq, keys, values)


PART = 1024


def mlp_kernel(
    turn, ids_ref, order_ref, c0, c1, c2, c3, hidden_ref, wco_ref, up_ref, down_ref, wn_ref, *refs
):
    out_ref, next_ref, bf_ref, sum_ref, held_ref, sems = refs[-6:]
    member = ids_ref[1]
    half = half_of(turn, ids_ref, order_ref)
    rows, width = c0.shape
    mixed = hidden_ref[...]
    for i, piece in enumerate((c0, c1, c2, c3)):
        mixed = mixed + jnp.dot(
            piece[...], wco_ref[rows_at(member ^ i, width), :], preferred_element_type=jnp.float32
        )
    second = normalize(mixed)
    bf_ref[...] = second.astype(jnp.bfloat16)
    sum_ref[...] = second
    for i in range(up_ref.shape[1] // PART):
        at = slice(i * PART, (i + 1) * PART)
        raised = jnp.dot(bf_ref[...], up_ref[:, at], preferred_element_type=jnp.float32)
        inner = (raised * (1.0 + lax.erf(raised * (0.5**0.5))) * 0.5).astype(jnp.bfloat16)
        sum_ref[...] += jnp.dot(inner, down_ref[at, :], preferred_element_type=jnp.float32)
    output = normalize(sum_ref[...])
    sum_ref[...] = output
    own = pltpu.make_async_copy(
        sum_ref.at[rows_at(member % 2, rows // 2), :], out_ref, sems.at[3]
    )

    @pl.when(member // 2 == half)
    def _():
        own.start()

    bf_ref[...] = output.astype(jnp.bfloat16)
    copies = []
    for c in range(3):
        held_ref[c] = jnp.dot(bf_ref[...], wn_ref[c], preferred_element_type=jnp.float32)
        copy = pltpu.make_async_copy(
            held_ref.at[c], next_ref.at[c, rows_at(half, rows), :], sems.at[c]
        )
        copy.start()
        copies.append(copy)
    for copy in copies:
        copy.wait()

    @pl.when(member // 2 == half)
    def _():
        own.wait()


def mlp(turn, ids, block_order, pieces, hidden, w_co, weights, before):
    rows, width = pieces[0].shape
    model = w_co.shape[0]
    return pl.pallas_call(
        functools.partial(mlp_kernel, turn),
        out_shape=(
            jax.ShapeDtypeStruct((rows // 2, model), jnp.float32),
            jax.ShapeDtypeStruct((3, 2 * rows, width), jnp.float32),
        ),
        in_specs=smem(2) + whole(9) + anywhere(len(before)),
        out_specs=tuple(anywhere(2)),
        scratch_shapes=[
            pltpu.VMEM((rows, model), jnp.bfloat16),
            pltpu.VMEM((rows, model), jnp.float32),
            pltpu.VMEM((3, rows, width), jnp.float32),
            pltpu.SemaphoreType.DMA((4,)),
        ],
        input_output_aliases={11 + i: i for i in range(len(before))},
        compiler_params=params(8),
        cost_estimate=cost(6e9, 0),
        name="mlp",
    )(ids, block_order, *pieces, hidden, w_co, *weights, *before)


def over_head(x, size):
    return [x] + [lax.ppermute(x, "head", xor(size, j)) for j in range(1, size)]


def over_chips(x, size):
    return [x] + [lax.ppermute(x, "blk", xor(size, s)) for s in range(2, size, 2)]


def on_device(
    tokens, block_order, request_lengths, enc_lengths, w_qkv, w_out, enc_kv, w_cq, w_co, w_up,
    w_down, w_next,
):
    group = lax.axis_size("head")
    cycle = lax.axis_size("blk")
    width = w_qkv.shape[2]
    ids = jnp.stack([lax.axis_index("blk"), lax.axis_index("head")]).astype(jnp.int32)
    paired = cycle == 8

    rows = over_head(tokens, group)
    if paired:
        enc = over_chips(enc_kv, cycle)
    x, queries, kv, part = project(ids, rows, w_qkv, w_out)
    w_cq, w_co, w_up, w_down, w_next = fetch(
        ids, (w_cq, w_co, w_up, w_down, w_next), {0: width}, 34, (queries,)
    )
    if paired:
        kvs, parts = over_chips(kv, cycle), over_head(part, group)
        own = bundle([kvs, enc, parts], (w_up,))
        other = [lax.ppermute(y, "blk", xor(cycle, 1)) for y in own]
        kvs, enc, parts = zip(own, other)
        near = tuple(range(0, cycle, 2))
        sources = [(True, near), (True, tuple(s + 1 for s in near))]
    else:
        kvs, enc = [lax.all_gather(y, "blk", axis=0)[None] for y in (kv, enc_kv)]
        kvs, enc = list(kvs), list(enc)
        sources = [(False, tuple(range(cycle)))]
        halves = w_out.reshape(2, width // 2, -1)
        parts = [
            bundle([over_head(lax.dynamic_index_in_dim(halves, ids[0] % 2 ^ i, 0, False), group)], ())[0]
            for i in range(2)
        ]
    keys, values, cache = order(ids, block_order, kvs, sources)
    enc_keys, enc_values, w_out = prepare(ids, enc, sources, parts)
    w_out = w_out.reshape(group, width, -1)

    outs = ()
    for turn in range(2):
        attended = self_attention(turn, ids, block_order, request_lengths, queries, keys, values)
        hidden, crossed = cross_attention(
            turn, ids, block_order, request_lengths, enc_lengths, over_head(attended, group), x,
            w_out, w_cq, enc_keys, enc_values,
        )
        outs = mlp(
            turn, ids, block_order, over_head(crossed, group), hidden, w_co,
            (w_up, w_down, w_next), outs,
        )
    return (outs[0], cache, outs[1])


def solution(mesh):
    in_specs = (
        P(("blk", "head"), None),
        P(),
        P(),
        P(),
        P(None, None, "head"),
        P("head", None),
        P(None, "blk", "head"),
        P(),
        P(),
        P(),
        P(),
        P(None, None, "head"),
    )
    out_specs = (P(("blk", "head"), None), P(None, "blk", "head"), P(None, "blk", "head"))
    return jax.shard_map(
        on_device, mesh=mesh, in_specs=in_specs, out_specs=out_specs, check_vma=False
    )
```

time: 166 us -> 118 us (0.71)
  the two profiles are of different devices: /device:TPU:2 before, /device:TPU:0 now
where the time goes in v2:
time: 118 us
  starting transfers between devices  51.3 us (43%)
  Pallas kernels  45.9 us (39%)
  waiting for transfers between devices  13.5 us (11%)
  local copies, waits for them, and re-layouts  6.41 us (5%)
    ppermute x18, starting transfers between devices, over_head(): return [x] + [lax.ppermute(x, 'head', xor(size, j)) for j in range(1, size)]  40.9 us
    pallas_call x2, Pallas kernels, mlp(): pl.pallas_call(functools.partial(mlp_kernel, turn), out_shape=(jax.ShapeD...  12.9 us
    pallas_call x2, Pallas kernels, self_attention(): pl.pallas_call(functools.partial(self_kernel, turn), out_shape=jax.ShapeD...  12.5 us
    ppermute x18, waiting for transfers between devices, over_head(): return [x] + [lax.ppermute(x, 'head', xor(size, j)) for j in range(1, size)]  10.6 us
    pallas_call x1, Pallas kernels, fetch(): pl.pallas_call(skipping(functools.partial(fetch_kernel, count, columns),...  9.82 us
    ppermute x6, starting transfers between devices, over_chips(): lax.ppermute(x, 'blk', xor(size, s))  9.71 us
    unnamed x24, local copies, waits for them, and re-layouts  6.41 us
    pallas_call x2, Pallas kernels, cross_attention(): pl.pallas_call(functools.partial(cross_kernel, turn), out_shape=(jax.Shap...  5.92 us
  transfers between devices with their start and end apart: 27, of which 4 were waited for; matrix products, arithmetic and copies ran while one was open for 0% of the time, Pallas kernels for 33%

profile of v2, /device:TPU:0, one launch (start us, length us, event | category | flops | bytes accessed | tf_op | source)
XLA Modules:
  0.0 118.2 jit_solution(9126594678222177075)
XLA Ops:
  0.6 4.1 %collective-permute-start.1 = (bf16[96,1024]{1,0:T(8,128)(2,1)}, bf16[96,1024]{1,0:T(8,128)(2,1)S(1)}, u32[]{:S(2)}, u32[]{:S(2)}) collective-permute-start(bf16[96,1024]{1,0:T(8,128)(2,1)} %x0.1), channel_id=1, source_target_pairs={{0,2},{1,3},{2,0},{3,1},{4,6},{5,7},{6,4},{7,5},{8,10},{9,11},{10,... | collective-permute-start | bytes 589832 | tf_op jit(solution)/shard_map/ppermute | solution.py:437
  4.7 1.6 %collective-permute-start = (bf16[96,1024]{1,0:T(8,128)(2,1)}, bf16[96,1024]{1,0:T(8,128)(2,1)S(1)}, u32[]{:S(2)}, u32[]{:S(2)}) collective-permute-start(bf16[96,1024]{1,0:T(8,128)(2,1)} %x0.1), channel_id=1, source_target_pairs={{0,1},{1,0},{2,3},{3,2},{4,5},{5,4},{6,7},{7,6},{8,9},{9,8},{10,11... | collective-permute-start | bytes 589832 | tf_op jit(solution)/shard_map/ppermute | solution.py:437
  6.3 1.7 %collective-permute-start.7 = (bf16[2,256,256]{2,1,0:T(8,128)(2,1)}, bf16[2,256,256]{2,1,0:T(8,128)(2,1)S(1)}, u32[]{:S(2)}, u32[]{:S(2)}) collective-permute-start(bf16[2,256,256]{2,1,0:T(8,128)(2,1)} %refs_4_.3), channel_id=1, source_target_pairs={{0,16},{4,20},{8,24},{12,28},{16,0},{20,4},{24,8},{28,12},{1,17},{... | collective-permute-start | bytes 786440 | tf_op jit(solution)/shard_map/ppermute | solution.py:441
  8.1 1.5 %collective-permute-start.6 = (bf16[2,256,256]{2,1,0:T(8,128)(2,1)}, bf16[2,256,256]{2,1,0:T(8,128)(2,1)S(1)}, u32[]{:S(2)}, u32[]{:S(2)}) collective-permute-start(bf16[2,256,256]{2,1,0:T(8,128)(2,1)} %refs_4_.3), channel_id=1, source_target_pairs={{0,8},{4,12},{8,0},{12,4},{16,24},{20,28},{24,16},{28,20},{1,9},{5... | collective-permute-start | bytes 786440 | tf_op jit(solution)/shard_map/ppermute | solution.py:441
  9.6 0.1 pad_add_fusion.ids_ref.refs_0_
  9.6 6.2 %collective-permute-done.1.x2 = bf16[96,1024]{1,0:T(8,128)(2,1)S(1)} collective-permute-done((bf16[96,1024]{1,0:T(8,128)(2,1)}, bf16[96,1024]{1,0:T(8,128)(2,1)S(1)}, u32[]{:S(2)}, u32[]{:S(2)}) %collective-permute-start.1) | collective-permute-done | bytes 196640 | tf_op jit(solution)/shard_map/ppermute | solution.py:437
  15.8 3.0 %collective-permute-start.8 = (bf16[2,256,256]{2,1,0:T(8,128)(2,1)}, bf16[2,256,256]{2,1,0:T(8,128)(2,1)S(1)}, u32[]{:S(2)}, u32[]{:S(2)}) collective-permute-start(bf16[2,256,256]{2,1,0:T(8,128)(2,1)} %refs_4_.3), channel_id=1, source_target_pairs={{0,24},{4,28},{8,16},{12,20},{16,8},{20,12},{24,0},{28,4},{1,25},{... | collective-permute-start | bytes 786440 | tf_op jit(solution)/shard_map/ppermute | solution.py:441
  18.8 0.0 collective-permute-done.x1
  18.8 0.7 collective-permute-done.2.x3
  19.5 1.4 %copy-done.3 = bf16[3,1024,256]{2,1,0:T(8,128)(2,1)S(1)} copy-done((bf16[3,1024,256]{2,1,0:T(8,128)(2,1)S(1)}, bf16[3,1024,256]{2,1,0:T(8,128)(2,1)}, u32[]{:S(2)}) %copy-start.3) | copy-done | bytes 1572888
  20.9 1.0 copy-done.4
  22.0 0.9 copy-done.6
  22.9 1.4 %project.1 = (bf16[384,1024]{1,0:T(8,128)(2,1)S(1)}, bf16[384,256]{1,0:T(8,128)(2,1)S(1)}, bf16[2,384,256]{2,1,0:T(8,128)(2,1)S(1)}, bf16[128,1024]{1,0:T(8,128)(2,1)S(1)}) custom-call(s32[2]{0:T(128)S(1)} %pad_add_fusion.ids_ref.refs_0_, bf16[96,1024]{1,0:T(8,128)(2,1)S(1)} %copy-done.6, bf16[96,1024]{1,0:T(8,128)(2,1)S(1)} %collective-permute-done.x1, ...), custom_call_target="tpu_custom_call" | custom-call | flops 30198988 | bytes 78643 | tf_op jit(solution)/shard_map/project/pallas_call | solution.py:81
  24.3 2.5 %collective-permute-start.11 = (bf16[128,1024]{1,0:T(8,128)(2,1)S(1)}, bf16[128,1024]{1,0:T(8,128)(2,1)S(1)}, u32[]{:S(2)}, u32[]{:S(2)}) collective-permute-start(bf16[128,1024]{1,0:T(8,128)(2,1)S(1)} %get-tuple-element.31.refs_8_), channel_id=1, source_target_pairs={{0,3},{1,2},{2,1},{3,0},{4,7},{5,6},{6,5},{7,4},{8,11},{9,10},{10,... | collective-permute-start | bytes 786440 | tf_op jit(solution)/shard_map/ppermute | solution.py:437
  26.8 2.4 %collective-permute-start.5 = (bf16[2,384,256]{2,1,0:T(8,128)(2,1)S(1)}, bf16[2,384,256]{2,1,0:T(8,128)(2,1)S(1)}, u32[]{:S(2)}, u32[]{:S(2)}) collective-permute-start(bf16[2,384,256]{2,1,0:T(8,128)(2,1)S(1)} %get-tuple-element.30.refs_0_), channel_id=1, source_target_pairs={{0,24},{4,28},{8,16},{12,20},{16,8},{20,12},{24,0},{28,4},{1,25},{... | collective-permute-start | bytes 1179656 | tf_op jit(solution)/shard_map/ppermute | solution.py:441
  29.2 0.5 collective-permute-start.4
  29.7 0.5 collective-permute-start.3
  30.3 3.2 %collective-permute-start.10 = (bf16[128,1024]{1,0:T(8,128)(2,1)S(1)}, bf16[128,1024]{1,0:T(8,128)(2,1)S(1)}, u32[]{:S(2)}, u32[]{:S(2)}) collective-permute-start(bf16[128,1024]{1,0:T(8,128)(2,1)S(1)} %get-tuple-element.31.refs_8_), channel_id=1, source_target_pairs={{0,2},{1,3},{2,0},{3,1},{4,6},{5,7},{6,4},{7,5},{8,10},{9,11},{10,... | collective-permute-start | bytes 786440 | tf_op jit(solution)/shard_map/ppermute | solution.py:437
  33.5 11.6 %collective-permute-start.9 = (bf16[128,1024]{1,0:T(8,128)(2,1)S(1)}, bf16[128,1024]{1,0:T(8,128)(2,1)S(1)}, u32[]{:S(2)}, u32[]{:S(2)}) collective-permute-start(bf16[128,1024]{1,0:T(8,128)(2,1)S(1)} %get-tuple-element.31.refs_8_), channel_id=1, source_target_pairs={{0,1},{1,0},{2,3},{3,2},{4,5},{5,4},{6,7},{7,6},{8,9},{9,8},{10,11... | collective-permute-start | bytes 786440 | tf_op jit(solution)/shard_map/ppermute | solution.py:437
  45.1 1.6 %copy-done.1 = bf16[1024,1024]{1,0:T(8,128)(2,1)S(1)} copy-done((bf16[1024,1024]{1,0:T(8,128)(2,1)S(1)}, bf16[1024,1024]{1,0:T(8,128)(2,1)}, u32[]{:S(2)}) %copy-start.1) | copy-done | bytes 2097176
  46.7 1.4 %copy-done.2 = bf16[3,1024,256]{2,1,0:T(8,128)(2,1)S(1)} copy-done((bf16[3,1024,256]{2,1,0:T(8,128)(2,1)S(1)}, bf16[3,1024,256]{2,1,0:T(8,128)(2,1)}, u32[]{:S(2)}) %copy-start.2) | copy-done | bytes 1572888
  48.1 9.8 %fetch.1 = (bf16[1024,256]{1,0:T(8,128)(2,1)S(1)}, bf16[1024,1024]{1,0:T(8,128)(2,1)S(1)}, bf16[1024,4096]{1,0:T(8,128)(2,1)S(1)}, bf16[4096,1024]{1,0:T(8,128)(2,1)}, bf16[3,1024,256]{2,1,0:T(8,128)(2,1)S(1)}) custom-call(s32[2]{0:T(128)S(1)} %pad_add_fusion.ids_ref.refs_0_, bf16[1024,1024]{1,0:T(8,128)(2,1)S(1)} %copy-done, ...), custom_call_target="tpu_custom_call" | custom-call | bytes 1048576 | tf_op jit(solution)/shard_map/fetch/pallas_call | solution.py:115
  58.0 0.0 copy-start.7
  58.0 0.2 bundle.1
  58.3 0.0 copy-start.8
  58.3 0.1 collective-permute-start.12
  58.4 0.5 collective-permute-start.16
  58.9 0.1 collective-permute-start.17
  59.0 2.8 %collective-permute-done.12.refs_1_ = bf16[4,2,384,256]{3,2,1,0:T(8,128)(2,1)S(1)} collective-permute-done((bf16[4,2,384,256]{3,2,1,0:T(8,128)(2,1)S(1)}, bf16[4,2,384,256]{3,2,1,0:T(8,128)(2,1)S(1)}, u32[]{:S(2)}, u32[]{:S(2)}) %collective-permute-start.12) | collective-permute-done | bytes 1572896 | tf_op jit(solution)/shard_map/ppermute | solution.py:464
  61.8 2.0 %order.1 = (bf16[3072,256]{1,0:T(8,128)(2,1)S(1)}, bf16[4,3072,128]{2,1,0:T(8,128)(2,1)S(1)}, bf16[2,384,256]{2,1,0:T(8,128)(2,1)}) custom-call(s32[2]{0:T(128)S(1)} %pad_add_fusion.ids_ref.refs_0_, s32[16]{0:T(128)S(1)} %copy-done.7, bf16[4,2,384,256]{3,2,1,0:T(8,128)(2,1)S(1)} %get-tuple-element.33.refs_0_, ...), custom_call_target="tpu_custom_call" | custom-call | bytes 393216 | tf_op jit(solution)/shard_map/order/pallas_call | solution.py:179
  63.8 3.3 %self_attention.3.a0 = bf16[192,256]{1,0:T(8,128)(2,1)S(1)} custom-call(s32[2]{0:T(128)S(1)} %pad_add_fusion.ids_ref.refs_0_, s32[16]{0:T(128)S(1)} %copy-done.7, s32[9]{0:T(128)S(1)} %copy-done.8, bf16[384,256]{1,0:T(8,128)(2,1)S(1)} %get-tuple-element.29.refs_6_.q_ref, bf16[3072,256]{1,0:T(8,128)(2,1)S(1)} %get-tuple-element.34.k_ref, ...), custom_call_target="tpu_custom_call" | custom-call | flops 250000000 | tf_op jit(solution)/shard_map/self_attention/pallas_call | solution.py:300
  67.2 2.5 %collective-permute-start.23 = (bf16[192,256]{1,0:T(8,128)(2,1)S(1)}, bf16[192,256]{1,0:T(8,128)(2,1)S(1)}, u32[]{:S(2)}, u32[]{:S(2)}) collective-permute-start(bf16[192,256]{1,0:T(8,128)(2,1)S(1)} %self_attention.3.a0), channel_id=1, source_target_pairs={{0,3},{1,2},{2,1},{3,0},{4,7},{5,6},{6,5},{7,4},{8,11},{9,10},{10,... | collective-permute-start | bytes 294920 | tf_op jit(solution)/shard_map/ppermute | solution.py:437
  69.7 1.9 %collective-permute-start.21 = (bf16[192,256]{1,0:T(8,128)(2,1)S(1)}, bf16[192,256]{1,0:T(8,128)(2,1)S(1)}, u32[]{:S(2)}, u32[]{:S(2)}) collective-permute-start(bf16[192,256]{1,0:T(8,128)(2,1)S(1)} %self_attention.3.a0), channel_id=1, source_target_pairs={{0,1},{1,0},{2,3},{3,2},{4,5},{5,4},{6,7},{7,6},{8,9},{9,8},{10,11... | collective-permute-start | bytes 294920 | tf_op jit(solution)/shard_map/ppermute | solution.py:437
  71.6 9.2 %self_attention.2.a0 = bf16[192,256]{1,0:T(8,128)(2,1)S(1)} custom-call(s32[2]{0:T(128)S(1)} %pad_add_fusion.ids_ref.refs_0_, s32[16]{0:T(128)S(1)} %copy-done.7, s32[9]{0:T(128)S(1)} %copy-done.8, bf16[384,256]{1,0:T(8,128)(2,1)S(1)} %get-tuple-element.29.refs_6_.q_ref, bf16[3072,256]{1,0:T(8,128)(2,1)S(1)} %get-tuple-element.34.k_ref, ...), custom_call_target="tpu_custom_call" | custom-call | flops 250000000 | tf_op jit(solution)/shard_map/self_attention/pallas_call | solution.py:300
  80.8 0.0 copy-start.9
  80.8 2.5 %collective-permute-start.15 = (bf16[192,256]{1,0:T(8,128)(2,1)S(1)}, bf16[192,256]{1,0:T(8,128)(2,1)S(1)}, u32[]{:S(2)}, u32[]{:S(2)}) collective-permute-start(bf16[192,256]{1,0:T(8,128)(2,1)S(1)} %self_attention.2.a0), channel_id=1, source_target_pairs={{0,3},{1,2},{2,1},{3,0},{4,7},{5,6},{6,5},{7,4},{8,11},{9,10},{10,... | collective-permute-start | bytes 294920 | tf_op jit(solution)/shard_map/ppermute | solution.py:437
  83.3 1.1 prepare.1
  84.5 0.1 collective-permute-start.14
  84.6 1.9 %collective-permute-start.13 = (bf16[192,256]{1,0:T(8,128)(2,1)S(1)}, bf16[192,256]{1,0:T(8,128)(2,1)S(1)}, u32[]{:S(2)}, u32[]{:S(2)}) collective-permute-start(bf16[192,256]{1,0:T(8,128)(2,1)S(1)} %self_attention.2.a0), channel_id=1, source_target_pairs={{0,1},{1,0},{2,3},{3,2},{4,5},{5,4},{6,7},{7,6},{8,9},{9,8},{10,11... | collective-permute-start | bytes 294920 | tf_op jit(solution)/shard_map/ppermute | solution.py:437
  86.5 2.9 %cross_attention.3 = (f32[192,1024]{1,0:T(8,128)S(1)}, bf16[192,256]{1,0:T(8,128)(2,1)S(1)}) custom-call(s32[2]{0:T(128)S(1)} %pad_add_fusion.ids_ref.refs_0_, s32[16]{0:T(128)S(1)} %copy-done.7, s32[9]{0:T(128)S(1)} %copy-done.8, s32[9]{0:T(128)S(1)} %copy-done.9, bf16[192,256]{1,0:T(8,128)(2,1)S(1)} %self_attention.3.a0, ...), custom_call_target="tpu_custom_call" | custom-call | flops 250000000 | tf_op jit(solution)/shard_map/cross_attention/pallas_call | solution.py:348
  89.4 2.5 %collective-permute-start.26 = (bf16[192,256]{1,0:T(8,128)(2,1)S(1)}, bf16[192,256]{1,0:T(8,128)(2,1)S(1)}, u32[]{:S(2)}, u32[]{:S(2)}) collective-permute-start(bf16[192,256]{1,0:T(8,128)(2,1)S(1)} %get-tuple-element.48.c0), channel_id=1, source_target_pairs={{0,3},{1,2},{2,1},{3,0},{4,7},{5,6},{6,5},{7,4},{8,11},{9,10},{10,... | collective-permute-start | bytes 294920 | tf_op jit(solution)/shard_map/ppermute | solution.py:437
  91.9 1.9 %collective-permute-start.24 = (bf16[192,256]{1,0:T(8,128)(2,1)S(1)}, bf16[192,256]{1,0:T(8,128)(2,1)S(1)}, u32[]{:S(2)}, u32[]{:S(2)}) collective-permute-start(bf16[192,256]{1,0:T(8,128)(2,1)S(1)} %get-tuple-element.48.c0), channel_id=1, source_target_pairs={{0,1},{1,0},{2,3},{3,2},{4,5},{5,4},{6,7},{7,6},{8,9},{9,8},{10,11... | collective-permute-start | bytes 294920 | tf_op jit(solution)/shard_map/ppermute | solution.py:437
  93.9 3.0 %cross_attention.2 = (f32[192,1024]{1,0:T(8,128)S(1)}, bf16[192,256]{1,0:T(8,128)(2,1)S(1)}) custom-call(s32[2]{0:T(128)S(1)} %pad_add_fusion.ids_ref.refs_0_, s32[16]{0:T(128)S(1)} %copy-done.7, s32[9]{0:T(128)S(1)} %copy-done.8, s32[9]{0:T(128)S(1)} %copy-done.9, bf16[192,256]{1,0:T(8,128)(2,1)S(1)} %self_attention.2.a0, ...), custom_call_target="tpu_custom_call" | custom-call | flops 250000000 | tf_op jit(solution)/shard_map/cross_attention/pallas_call | solution.py:348
  96.9 2.5 %collective-permute-start.20 = (bf16[192,256]{1,0:T(8,128)(2,1)S(1)}, bf16[192,256]{1,0:T(8,128)(2,1)S(1)}, u32[]{:S(2)}, u32[]{:S(2)}) collective-permute-start(bf16[192,256]{1,0:T(8,128)(2,1)S(1)} %get-tuple-element.43.c0), channel_id=1, source_target_pairs={{0,3},{1,2},{2,1},{3,0},{4,7},{5,6},{6,5},{7,4},{8,11},{9,10},{10,... | collective-permute-start | bytes 294920 | tf_op jit(solution)/shard_map/ppermute | solution.py:437
  99.4 1.9 %collective-permute-start.18 = (bf16[192,256]{1,0:T(8,128)(2,1)S(1)}, bf16[192,256]{1,0:T(8,128)(2,1)S(1)}, u32[]{:S(2)}, u32[]{:S(2)}) collective-permute-start(bf16[192,256]{1,0:T(8,128)(2,1)S(1)} %get-tuple-element.43.c0), channel_id=1, source_target_pairs={{0,1},{1,0},{2,3},{3,2},{4,5},{5,4},{6,7},{7,6},{8,9},{9,8},{10,11... | collective-permute-start | bytes 294920 | tf_op jit(solution)/shard_map/ppermute | solution.py:437
  101.4 3.7 %collective-permute-done.25.c2 = bf16[192,256]{1,0:T(8,128)(2,1)S(1)} collective-permute-done((bf16[192,256]{1,0:T(8,128)(2,1)S(1)}, bf16[192,256]{1,0:T(8,128)(2,1)S(1)}, u32[]{:S(2)}, u32[]{:S(2)}) %collective-permute-start.25) | collective-permute-done | bytes 98336 | tf_op jit(solution)/shard_map/ppermute | solution.py:437
  105.1 6.5 %mlp.2 = (f32[96,1024]{1,0:T(8,128)}, f32[3,384,256]{2,1,0:T(8,128)}) custom-call(s32[2]{0:T(128)S(1)} %pad_add_fusion.ids_ref.refs_0_, s32[16]{0:T(128)S(1)} %copy-done.7, bf16[192,256]{1,0:T(8,128)(2,1)S(1)} %get-tuple-element.48.c0, bf16[192,256]{1,0:T(8,128)(2,1)S(1)} %collective-permute-done.24.c1, bf16[192,256]{1,0:T(8,128)(2,1)S(1)} %collective-permute-done.25.c2, ...), custom_call_target="tpu_custom_call" | custom-call | flops 300000000 | tf_op jit(solution)/shard_map/mlp/pallas_call | solution.py:415
  111.6 6.4 %mlp.3 = (f32[96,1024]{1,0:T(8,128)}, f32[3,384,256]{2,1,0:T(8,128)}) custom-call(s32[2]{0:T(128)S(1)} %pad_add_fusion.ids_ref.refs_0_, s32[16]{0:T(128)S(1)} %copy-done.7, bf16[192,256]{1,0:T(8,128)(2,1)S(1)} %get-tuple-element.43.c0, bf16[192,256]{1,0:T(8,128)(2,1)S(1)} %collective-permute-done.18.c1, ...), custom_call_target="tpu_custom_call", output_to_operand_aliasing={{0}: (11, {}), {1}: (12, {})} | custom-call | flops 300000000 | tf_op jit(solution)/shard_map/mlp/pallas_call | solution.py:415
  (43 shorter events, 0.1 us)
Async XLA Ops:
  0.6 44.5 %copy-start = (bf16[1024,1024]{1,0:T(8,128)(2,1)S(1)}, bf16[1024,1024]{1,0:T(8,128)(2,1)}, u32[]{:S(2)}) copy-start(bf16[1024,1024]{1,0:T(8,128)(2,1)} %refs_1_.1) | copy-start | bytes 6291460
  0.6 15.2 %collective-permute-start.1 = (bf16[96,1024]{1,0:T(8,128)(2,1)}, bf16[96,1024]{1,0:T(8,128)(2,1)S(1)}, u32[]{:S(2)}, u32[]{:S(2)}) collective-permute-start(bf16[96,1024]{1,0:T(8,128)(2,1)} %x0.1), channel_id=1, source_target_pairs={{0,2},{1,3},{2,0},{3,1},{4,6},{5,7},{6,4},{7,5},{8,10},{9,11},{10,... | collective-permute-start | bytes 589832 | tf_op jit(solution)/shard_map/ppermute | solution.py:437
  4.7 14.1 %collective-permute-start = (bf16[96,1024]{1,0:T(8,128)(2,1)}, bf16[96,1024]{1,0:T(8,128)(2,1)S(1)}, u32[]{:S(2)}, u32[]{:S(2)}) collective-permute-start(bf16[96,1024]{1,0:T(8,128)(2,1)} %x0.1), channel_id=1, source_target_pairs={{0,1},{1,0},{2,3},{3,2},{4,5},{5,4},{6,7},{7,6},{8,9},{9,8},{10,11... | collective-permute-start | bytes 589832 | tf_op jit(solution)/shard_map/ppermute | solution.py:437
  6.3 13.2 %collective-permute-start.2 = (bf16[96,1024]{1,0:T(8,128)(2,1)}, bf16[96,1024]{1,0:T(8,128)(2,1)S(1)}, u32[]{:S(2)}, u32[]{:S(2)}) collective-permute-start(bf16[96,1024]{1,0:T(8,128)(2,1)} %x0.1), channel_id=1, source_target_pairs={{0,3},{1,2},{2,1},{3,0},{4,7},{5,6},{6,5},{7,4},{8,11},{9,10},{10,... | collective-permute-start | bytes 589832 | tf_op jit(solution)/shard_map/ppermute | solution.py:437
  6.3 22.9 %collective-permute-start.7 = (bf16[2,256,256]{2,1,0:T(8,128)(2,1)}, bf16[2,256,256]{2,1,0:T(8,128)(2,1)S(1)}, u32[]{:S(2)}, u32[]{:S(2)}) collective-permute-start(bf16[2,256,256]{2,1,0:T(8,128)(2,1)} %refs_4_.3), channel_id=1, source_target_pairs={{0,16},{4,20},{8,24},{12,28},{16,0},{20,4},{24,8},{28,12},{1,17},{... | collective-permute-start | bytes 786440 | tf_op jit(solution)/shard_map/ppermute | solution.py:441
  8.1 21.7 %collective-permute-start.6 = (bf16[2,256,256]{2,1,0:T(8,128)(2,1)}, bf16[2,256,256]{2,1,0:T(8,128)(2,1)S(1)}, u32[]{:S(2)}, u32[]{:S(2)}) collective-permute-start(bf16[2,256,256]{2,1,0:T(8,128)(2,1)} %refs_4_.3), channel_id=1, source_target_pairs={{0,8},{4,12},{8,0},{12,4},{16,24},{20,28},{24,16},{28,20},{1,9},{5... | collective-permute-start | bytes 786440 | tf_op jit(solution)/shard_map/ppermute | solution.py:441
  15.8 14.5 %collective-permute-start.8 = (bf16[2,256,256]{2,1,0:T(8,128)(2,1)}, bf16[2,256,256]{2,1,0:T(8,128)(2,1)S(1)}, u32[]{:S(2)}, u32[]{:S(2)}) collective-permute-start(bf16[2,256,256]{2,1,0:T(8,128)(2,1)} %refs_4_.3), channel_id=1, source_target_pairs={{0,24},{4,28},{8,16},{12,20},{16,8},{20,12},{24,0},{28,4},{1,25},{... | collective-permute-start | bytes 786440 | tf_op jit(solution)/shard_map/ppermute | solution.py:441
  19.5 1.4 %copy-start.3 = (bf16[3,1024,256]{2,1,0:T(8,128)(2,1)S(1)}, bf16[3,1024,256]{2,1,0:T(8,128)(2,1)}, u32[]{:S(2)}) copy-start(bf16[3,1024,256]{2,1,0:T(8,128)(2,1)} %w_ref.1) | copy-start | bytes 4718596
  20.9 1.0 copy-start.4
  21.9 0.9 copy-start.6
  24.3 9.3 %collective-permute-start.11 = (bf16[128,1024]{1,0:T(8,128)(2,1)S(1)}, bf16[128,1024]{1,0:T(8,128)(2,1)S(1)}, u32[]{:S(2)}, u32[]{:S(2)}) collective-permute-start(bf16[128,1024]{1,0:T(8,128)(2,1)S(1)} %get-tuple-element.31.refs_8_), channel_id=1, source_target_pairs={{0,3},{1,2},{2,1},{3,0},{4,7},{5,6},{6,5},{7,4},{8,11},{9,10},{10,... | collective-permute-start | bytes 786440 | tf_op jit(solution)/shard_map/ppermute | solution.py:437
  26.8 31.2 %collective-permute-start.5 = (bf16[2,384,256]{2,1,0:T(8,128)(2,1)S(1)}, bf16[2,384,256]{2,1,0:T(8,128)(2,1)S(1)}, u32[]{:S(2)}, u32[]{:S(2)}) collective-permute-start(bf16[2,384,256]{2,1,0:T(8,128)(2,1)S(1)} %get-tuple-element.30.refs_0_), channel_id=1, source_target_pairs={{0,24},{4,28},{8,16},{12,20},{16,8},{20,12},{24,0},{28,4},{1,25},{... | collective-permute-start | bytes 1179656 | tf_op jit(solution)/shard_map/ppermute | solution.py:441
  29.2 28.8 %collective-permute-start.4 = (bf16[2,384,256]{2,1,0:T(8,128)(2,1)S(1)}, bf16[2,384,256]{2,1,0:T(8,128)(2,1)S(1)}, u32[]{:S(2)}, u32[]{:S(2)}) collective-permute-start(bf16[2,384,256]{2,1,0:T(8,128)(2,1)S(1)} %get-tuple-element.30.refs_0_), channel_id=1, source_target_pairs={{0,16},{4,20},{8,24},{12,28},{16,0},{20,4},{24,8},{28,12},{1,17},{... | collective-permute-start | bytes 1179656 | tf_op jit(solution)/shard_map/ppermute | solution.py:441
  29.7 28.3 %collective-permute-start.3 = (bf16[2,384,256]{2,1,0:T(8,128)(2,1)S(1)}, bf16[2,384,256]{2,1,0:T(8,128)(2,1)S(1)}, u32[]{:S(2)}, u32[]{:S(2)}) collective-permute-start(bf16[2,384,256]{2,1,0:T(8,128)(2,1)S(1)} %get-tuple-element.30.refs_0_), channel_id=1, source_target_pairs={{0,8},{4,12},{8,0},{12,4},{16,24},{20,28},{24,16},{28,20},{1,9},{5... | collective-permute-start | bytes 1179656 | tf_op jit(solution)/shard_map/ppermute | solution.py:441
  30.3 27.7 %collective-permute-start.10 = (bf16[128,1024]{1,0:T(8,128)(2,1)S(1)}, bf16[128,1024]{1,0:T(8,128)(2,1)S(1)}, u32[]{:S(2)}, u32[]{:S(2)}) collective-permute-start(bf16[128,1024]{1,0:T(8,128)(2,1)S(1)} %get-tuple-element.31.refs_8_), channel_id=1, source_target_pairs={{0,2},{1,3},{2,0},{3,1},{4,6},{5,7},{6,4},{7,5},{8,10},{9,11},{10,... | collective-permute-start | bytes 786440 | tf_op jit(solution)/shard_map/ppermute | solution.py:437
  33.5 24.4 %collective-permute-start.9 = (bf16[128,1024]{1,0:T(8,128)(2,1)S(1)}, bf16[128,1024]{1,0:T(8,128)(2,1)S(1)}, u32[]{:S(2)}, u32[]{:S(2)}) collective-permute-start(bf16[128,1024]{1,0:T(8,128)(2,1)S(1)} %get-tuple-element.31.refs_8_), channel_id=1, source_target_pairs={{0,1},{1,0},{2,3},{3,2},{4,5},{5,4},{6,7},{7,6},{8,9},{9,8},{10,11... | collective-permute-start | bytes 786440 | tf_op jit(solution)/shard_map/ppermute | solution.py:437
  45.1 1.6 %copy-start.1 = (bf16[1024,1024]{1,0:T(8,128)(2,1)S(1)}, bf16[1024,1024]{1,0:T(8,128)(2,1)}, u32[]{:S(2)}) copy-start(bf16[1024,1024]{1,0:T(8,128)(2,1)} %refs_2_.1) | copy-start | bytes 6291460
  46.7 1.4 %copy-start.2 = (bf16[3,1024,256]{2,1,0:T(8,128)(2,1)S(1)}, bf16[3,1024,256]{2,1,0:T(8,128)(2,1)}, u32[]{:S(2)}) copy-start(bf16[3,1024,256]{2,1,0:T(8,128)(2,1)} %refs_5_.1) | copy-start | bytes 4718596
  48.1 9.9 %copy-start.5 = (bf16[2,256,256]{2,1,0:T(8,128)(2,1)S(1)}, bf16[2,256,256]{2,1,0:T(8,128)(2,1)}, u32[]{:S(2)}) copy-start(bf16[2,256,256]{2,1,0:T(8,128)(2,1)} %refs_4_.3) | copy-start | bytes 786436
  58.0 3.8 %copy-start.7 = (s32[16]{0:T(128)S(1)}, s32[16]{0:T(128)}, u32[]{:S(2)}) copy-start(s32[16]{0:T(128)} %order_ref.13) | copy-start | bytes 196
  58.3 5.5 %copy-start.8 = (s32[9]{0:T(128)S(1)}, s32[9]{0:T(128)}, u32[]{:S(2)}) copy-start(s32[9]{0:T(128)} %lengths_ref.7) | copy-start | bytes 112
  58.3 3.5 %collective-permute-start.12 = (bf16[4,2,384,256]{3,2,1,0:T(8,128)(2,1)S(1)}, bf16[4,2,384,256]{3,2,1,0:T(8,128)(2,1)S(1)}, u32[]{:S(2)}, u32[]{:S(2)}) collective-permute-start(bf16[4,2,384,256]{3,2,1,0:T(8,128)(2,1)S(1)} %get-tuple-element.33.refs_0_), channel_id=1, source_target_pairs={{0,4},{4,0},{8,12},{12,8},{16,20},{20,16},{24,28},{28,24},{1,5},{5... | collective-permute-start | bytes 4718600 | tf_op jit(solution)/shard_map/ppermute | solution.py:464
  58.4 22.4 %collective-permute-start.16 = (bf16[4,2,256,256]{3,2,1,0:T(8,128)(2,1)S(1)}, bf16[4,2,256,256]{3,2,1,0:T(8,128)(2,1)S(1)}, u32[]{:S(2)}, u32[]{:S(2)}) collective-permute-start(bf16[4,2,256,256]{3,2,1,0:T(8,128)(2,1)S(1)} %get-tuple-element.37.refs_0_), channel_id=1, source_target_pairs={{0,4},{4,0},{8,12},{12,8},{16,20},{20,16},{24,28},{28,24},{1,5},{5... | collective-permute-start | bytes 3145736 | tf_op jit(solution)/shard_map/ppermute | solution.py:464
  58.9 24.5 %collective-permute-start.17 = (bf16[4,128,1024]{2,1,0:T(8,128)(2,1)S(1)}, bf16[4,128,1024]{2,1,0:T(8,128)(2,1)S(1)}, u32[]{:S(2)}, u32[]{:S(2)}) collective-permute-start(bf16[4,128,1024]{2,1,0:T(8,128)(2,1)S(1)} %get-tuple-element.38.refs_2_), channel_id=1, source_target_pairs={{0,4},{4,0},{8,12},{12,8},{16,20},{20,16},{24,28},{28,24},{1,5},{5... | collective-permute-start | bytes 3145736 | tf_op jit(solution)/shard_map/ppermute | solution.py:464
  67.2 17.4 %collective-permute-start.23 = (bf16[192,256]{1,0:T(8,128)(2,1)S(1)}, bf16[192,256]{1,0:T(8,128)(2,1)S(1)}, u32[]{:S(2)}, u32[]{:S(2)}) collective-permute-start(bf16[192,256]{1,0:T(8,128)(2,1)S(1)} %self_attention.3.a0), channel_id=1, source_target_pairs={{0,3},{1,2},{2,1},{3,0},{4,7},{5,6},{6,5},{7,4},{8,11},{9,10},{10,... | collective-permute-start | bytes 294920 | tf_op jit(solution)/shard_map/ppermute | solution.py:437
  69.7 16.8 %collective-permute-start.22 = (bf16[192,256]{1,0:T(8,128)(2,1)S(1)}, bf16[192,256]{1,0:T(8,128)(2,1)S(1)}, u32[]{:S(2)}, u32[]{:S(2)}) collective-permute-start(bf16[192,256]{1,0:T(8,128)(2,1)S(1)} %self_attention.3.a0), channel_id=1, source_target_pairs={{0,2},{1,3},{2,0},{3,1},{4,6},{5,7},{6,4},{7,5},{8,10},{9,11},{10,... | collective-permute-start | bytes 294920 | tf_op jit(solution)/shard_map/ppermute | solution.py:437
  69.7 16.8 %collective-permute-start.21 = (bf16[192,256]{1,0:T(8,128)(2,1)S(1)}, bf16[192,256]{1,0:T(8,128)(2,1)S(1)}, u32[]{:S(2)}, u32[]{:S(2)}) collective-permute-start(bf16[192,256]{1,0:T(8,128)(2,1)S(1)} %self_attention.3.a0), channel_id=1, source_target_pairs={{0,1},{1,0},{2,3},{3,2},{4,5},{5,4},{6,7},{7,6},{8,9},{9,8},{10,11... | collective-permute-start | bytes 294920 | tf_op jit(solution)/shard_map/ppermute | solution.py:437
  80.8 5.7 %copy-start.9 = (s32[9]{0:T(128)S(1)}, s32[9]{0:T(128)}, u32[]{:S(2)}) copy-start(s32[9]{0:T(128)} %encs_ref.3) | copy-start | bytes 112
  80.8 11.1 %collective-permute-start.15 = (bf16[192,256]{1,0:T(8,128)(2,1)S(1)}, bf16[192,256]{1,0:T(8,128)(2,1)S(1)}, u32[]{:S(2)}, u32[]{:S(2)}) collective-permute-start(bf16[192,256]{1,0:T(8,128)(2,1)S(1)} %self_attention.2.a0), channel_id=1, source_target_pairs={{0,3},{1,2},{2,1},{3,0},{4,7},{5,6},{6,5},{7,4},{8,11},{9,10},{10,... | collective-permute-start | bytes 294920 | tf_op jit(solution)/shard_map/ppermute | solution.py:437
  83.3 21.8 %slice-start = ((s8[8388608]{0:T(1024)(128)(4,1)}), s8[4194304]{0:T(1024)(128)(4,1)S(1)}, s32[]{:S(2)}) async-start(s8[8388608]{0:T(1024)(128)(4,1)} %bitcast.3), calls=%async_computation | async-start | bytes 8388608
  84.5 9.4 %collective-permute-start.14 = (bf16[192,256]{1,0:T(8,128)(2,1)S(1)}, bf16[192,256]{1,0:T(8,128)(2,1)S(1)}, u32[]{:S(2)}, u32[]{:S(2)}) collective-permute-start(bf16[192,256]{1,0:T(8,128)(2,1)S(1)} %self_attention.2.a0), channel_id=1, source_target_pairs={{0,2},{1,3},{2,0},{3,1},{4,6},{5,7},{6,4},{7,5},{8,10},{9,11},{10,... | collective-permute-start | bytes 294920 | tf_op jit(solution)/shard_map/ppermute | solution.py:437
  84.6 9.3 %collective-permute-start.13 = (bf16[192,256]{1,0:T(8,128)(2,1)S(1)}, bf16[192,256]{1,0:T(8,128)(2,1)S(1)}, u32[]{:S(2)}, u32[]{:S(2)}) collective-permute-start(bf16[192,256]{1,0:T(8,128)(2,1)S(1)} %self_attention.2.a0), channel_id=1, source_target_pairs={{0,1},{1,0},{2,3},{3,2},{4,5},{5,4},{6,7},{7,6},{8,9},{9,8},{10,11... | collective-permute-start | bytes 294920 | tf_op jit(solution)/shard_map/ppermute | solution.py:437
  86.5 18.6 %slice-start.1 = ((s8[8388608]{0:T(1024)(128)(4,1)}), s8[4194304]{0:T(1024)(128)(4,1)S(1)}, s32[]{:S(2)}) async-start(s8[8388608]{0:T(1024)(128)(4,1)} %bitcast.3), calls=%async_computation.1 | async-start | bytes 8388608
  89.4 10.0 %collective-permute-start.26 = (bf16[192,256]{1,0:T(8,128)(2,1)S(1)}, bf16[192,256]{1,0:T(8,128)(2,1)S(1)}, u32[]{:S(2)}, u32[]{:S(2)}) collective-permute-start(bf16[192,256]{1,0:T(8,128)(2,1)S(1)} %get-tuple-element.48.c0), channel_id=1, source_target_pairs={{0,3},{1,2},{2,1},{3,0},{4,7},{5,6},{6,5},{7,4},{8,11},{9,10},{10,... | collective-permute-start | bytes 294920 | tf_op jit(solution)/shard_map/ppermute | solution.py:437
  91.9 13.2 %collective-permute-start.25 = (bf16[192,256]{1,0:T(8,128)(2,1)S(1)}, bf16[192,256]{1,0:T(8,128)(2,1)S(1)}, u32[]{:S(2)}, u32[]{:S(2)}) collective-permute-start(bf16[192,256]{1,0:T(8,128)(2,1)S(1)} %get-tuple-element.48.c0), channel_id=1, source_target_pairs={{0,2},{1,3},{2,0},{3,1},{4,6},{5,7},{6,4},{7,5},{8,10},{9,11},{10,... | collective-permute-start | bytes 294920 | tf_op jit(solution)/shard_map/ppermute | solution.py:437
  91.9 13.2 %collective-permute-start.24 = (bf16[192,256]{1,0:T(8,128)(2,1)S(1)}, bf16[192,256]{1,0:T(8,128)(2,1)S(1)}, u32[]{:S(2)}, u32[]{:S(2)}) collective-permute-start(bf16[192,256]{1,0:T(8,128)(2,1)S(1)} %get-tuple-element.48.c0), channel_id=1, source_target_pairs={{0,1},{1,0},{2,3},{3,2},{4,5},{5,4},{6,7},{7,6},{8,9},{9,8},{10,11... | collective-permute-start | bytes 294920 | tf_op jit(solution)/shard_map/ppermute | solution.py:437
  96.9 14.7 %collective-permute-start.20 = (bf16[192,256]{1,0:T(8,128)(2,1)S(1)}, bf16[192,256]{1,0:T(8,128)(2,1)S(1)}, u32[]{:S(2)}, u32[]{:S(2)}) collective-permute-start(bf16[192,256]{1,0:T(8,128)(2,1)S(1)} %get-tuple-element.43.c0), channel_id=1, source_target_pairs={{0,3},{1,2},{2,1},{3,0},{4,7},{5,6},{6,5},{7,4},{8,11},{9,10},{10,... | collective-permute-start | bytes 294920 | tf_op jit(solution)/shard_map/ppermute | solution.py:437
  99.4 12.2 %collective-permute-start.19 = (bf16[192,256]{1,0:T(8,128)(2,1)S(1)}, bf16[192,256]{1,0:T(8,128)(2,1)S(1)}, u32[]{:S(2)}, u32[]{:S(2)}) collective-permute-start(bf16[192,256]{1,0:T(8,128)(2,1)S(1)} %get-tuple-element.43.c0), channel_id=1, source_target_pairs={{0,2},{1,3},{2,0},{3,1},{4,6},{5,7},{6,4},{7,5},{8,10},{9,11},{10,... | collective-permute-start | bytes 294920 | tf_op jit(solution)/shard_map/ppermute | solution.py:437
  99.4 12.2 %collective-permute-start.18 = (bf16[192,256]{1,0:T(8,128)(2,1)S(1)}, bf16[192,256]{1,0:T(8,128)(2,1)S(1)}, u32[]{:S(2)}, u32[]{:S(2)}) collective-permute-start(bf16[192,256]{1,0:T(8,128)(2,1)S(1)} %get-tuple-element.43.c0), channel_id=1, source_target_pairs={{0,1},{1,0},{2,3},{3,2},{4,5},{5,4},{6,7},{7,6},{8,9},{9,8},{10,11... | collective-permute-start | bytes 294920 | tf_op jit(solution)/shard_map/ppermute | solution.py:437

commit v3 on v2

v3 whole, which is shorter than its diff:
```python
import functools
import math

import jax
import jax.numpy as jnp
from jax import lax
from jax.experimental import pallas as pl
from jax.experimental.pallas import tpu as pltpu
from jax.sharding import PartitionSpec as P

HEADS = 16
NEGATIVE = -1e30
SCALING = 0.125
EPSILON = 1e-05
TILE = 512
ALIGN = 256
ONES = 16
MIB = 1024 * 1024


def whole(count):
    return [pl.BlockSpec(memory_space=pltpu.VMEM)] * count


def anywhere(count):
    return [pl.BlockSpec(memory_space=pl.ANY)] * count


def smem(count):
    return [pl.BlockSpec(memory_space=pltpu.SMEM)] * count


def params(mib):
    return pltpu.CompilerParams(vmem_limit_bytes=mib * MIB)


def xor(size, bits):
    return [(i, i ^ bits) for i in range(size)]


def normalize(matrix):
    center = matrix - jnp.mean(matrix, axis=-1, keepdims=True)
    return center * lax.rsqrt(jnp.mean(center * center, axis=-1, keepdims=True) + EPSILON)


def cost(flops, moved):
    return pl.CostEstimate(flops=int(flops) // 20, bytes_accessed=int(moved) // 20, transcendentals=0)


def skipping(kernel, at, count):
    def body(*refs):
        kernel(*refs[:at], *refs[at + count :])

    return body


def placed(kernel):
    def body(*refs):
        kernel((lax.axis_index("blk"), lax.axis_index("head")), *refs)

    return body


def rows_at(index, rows):
    return pl.ds(pl.multiple_of(index * rows, rows), rows)


def sums_of(lengths_ref):
    sums, total = [], jnp.int32(0)
    for j in range(lengths_ref.shape[0]):
        total = total + lengths_ref[j]
        sums.append(total)
    return sums


def project_kernel(ids, x0, x1, x2, x3, w_ref, part_in, x_ref, q_ref, kv_ref, part_ref):
    part_ref[...] = part_in[...]
    for i, piece in enumerate((x0, x1, x2, x3)):
        x_ref[rows_at(ids[1] ^ i, x0.shape[0]), :] = piece[...]
    x = x_ref[...]
    for c in range(2):
        kv_ref[c] = jnp.dot(x, w_ref[1 + c], preferred_element_type=jnp.float32).astype(
            jnp.bfloat16
        )
    q_ref[...] = jnp.dot(x, w_ref[0], preferred_element_type=jnp.float32).astype(jnp.bfloat16)


def project(pieces, w_qkv, part):
    rows, width, model = 4 * pieces[0].shape[0], w_qkv.shape[2], pieces[0].shape[1]
    return pl.pallas_call(
        placed(project_kernel),
        out_shape=(
            jax.ShapeDtypeStruct((rows, model), jnp.bfloat16),
            jax.ShapeDtypeStruct((rows, width), jnp.bfloat16),
            jax.ShapeDtypeStruct((2, rows, width), jnp.bfloat16),
            jax.ShapeDtypeStruct(part.shape, jnp.bfloat16),
        ),
        in_specs=whole(6),
        out_specs=tuple(whole(4)),
        compiler_params=params(4),
        cost_estimate=cost(2 * rows * model * 3 * width, 2 * 3 * model * width),
        name="project",
    )(*pieces, w_qkv, part)


def fetch_kernel(cuts, ids, *refs):
    count, sem = len(cuts), refs[-1]
    copies = []
    for i, cut in enumerate(cuts):
        source, target = refs[i], refs[count + i]
        if cut == "columns":
            width = target.shape[1]
            source = source.at[:, pl.ds(pl.multiple_of(ids[1] * width, width), width)]
        if cut == "rows":
            source = source.at[rows_at(ids[0] % 2, target.shape[0]), :]
        copy = pltpu.make_async_copy(source, target, sem)
        copy.start()
        copies.append(copy)
    for copy in copies:
        copy.wait()


def fetch(arrays, shapes, cuts, room, after=()):
    count = len(arrays)
    return pl.pallas_call(
        placed(skipping(functools.partial(fetch_kernel, cuts), 1 + count, len(after))),
        out_shape=tuple(jax.ShapeDtypeStruct(s, a.dtype) for s, a in zip(shapes, arrays)),
        in_specs=anywhere(count + len(after)),
        out_specs=tuple(whole(count)),
        scratch_shapes=[pltpu.SemaphoreType.DMA],
        compiler_params=params(room),
        cost_estimate=cost(0, 2 * sum(math.prod(s) for s in shapes)),
        name="fetch",
    )(*arrays, *after)


def bundle_kernel(groups, *refs):
    at = sum(groups)
    for i, count in enumerate(groups):
        for j in range(count):
            refs[at + i][j] = refs[sum(groups[:i]) + j][...]


def bundle(groups, after):
    counts = [len(g) for g in groups]
    total = sum(counts)
    return pl.pallas_call(
        skipping(functools.partial(bundle_kernel, counts), total, len(after)),
        out_shape=tuple(jax.ShapeDtypeStruct((len(g),) + g[0].shape, g[0].dtype) for g in groups),
        in_specs=whole(total) + anywhere(len(after)),
        out_specs=tuple(whole(len(groups))),
        compiler_params=params(2),
        cost_estimate=cost(0, 2 * 2 * sum(len(g) * math.prod(g[0].shape) for g in groups)),
        name="bundle",
    )(*[x for g in groups for x in g], *after)


def turned(v_ref, vt_ref):
    def step(tile, carry):
        at = rows_at(tile, ALIGN)
        for pair in range(vt_ref.shape[0]):
            vt_ref[pair, :128, at] = v_ref[at, pair * 128 : (pair + 1) * 128].T
            vt_ref[pair, 128:, at] = jnp.ones((ONES, ALIGN), jnp.bfloat16)
        return carry

    lax.fori_loop(0, v_ref.shape[0] // ALIGN, step, 0)


def order_kernel(sources, ids, order_ref, *refs):
    passed_in, k_ref, vt_ref, cache_ref, passed_ref, v_ref, sem = refs[-7:]
    passing = pltpu.make_async_copy(passed_in, passed_ref, sem)
    passing.start()
    for ref, (relative, numbers) in zip(refs, sources):
        rows = ref.shape[2] // 2
        for piece, number in enumerate(numbers):
            block = ids[0] ^ number if relative else jnp.int32(number)
            for half in range(2):
                at = rows_at(order_ref[2 * block + half], rows)
                here = slice(half * rows, (half + 1) * rows)
                k_ref[at, :] = ref[piece, 0, here, :]
                v_ref[at, :] = ref[piece, 1, here, :]
    turned(v_ref, vt_ref)
    at = rows_at(ids[0], cache_ref.shape[1])
    cache_ref[0] = k_ref[at, :]
    cache_ref[1] = v_ref[at, :]
    passing.wait()


def order(block_order, chunks, sources, passed):
    rows, width = chunks[0].shape[2:]
    total = rows * sum(c.shape[0] for c in chunks)
    return pl.pallas_call(
        placed(functools.partial(order_kernel, sources)),
        out_shape=(
            jax.ShapeDtypeStruct((total, width), jnp.bfloat16),
            jax.ShapeDtypeStruct((width // 128, 128 + ONES, total), jnp.bfloat16),
            jax.ShapeDtypeStruct((2, rows, width), jnp.bfloat16),
            jax.ShapeDtypeStruct(passed.shape, jnp.bfloat16),
        ),
        in_specs=smem(1) + whole(len(chunks)) + anywhere(1),
        out_specs=tuple(whole(4)),
        scratch_shapes=[pltpu.VMEM((total, width), jnp.bfloat16), pltpu.SemaphoreType.DMA],
        compiler_params=params(4 + total * width * 2 // MIB),
        cost_estimate=cost(0, 5 * 2 * total * width),
        name="order",
    )(block_order, *chunks, passed)


def prepare_kernel(sources, ids, *refs):
    k_ref, vt_ref, w_ref, v_ref = refs[-4:]
    for ref, (relative, numbers) in zip(refs, sources):
        rows = ref.shape[2]
        for piece, number in enumerate(numbers):
            at = rows_at(ids[0] ^ number if relative else jnp.int32(number), rows)
            k_ref[at, :] = ref[piece, 0]
            v_ref[at, :] = ref[piece, 1]
    turned(v_ref, vt_ref)
    parts = refs[len(sources) : -4]
    for i, part in enumerate(parts):
        for j in range(part.shape[0]):
            w_ref[ids[1] ^ j, ids[0] % 2 ^ i] = part[j]


def prepare(chunks, sources, parts):
    rows, width = chunks[0].shape[2:]
    total = rows * sum(c.shape[0] for c in chunks)
    group, depth, model = parts[0].shape
    return pl.pallas_call(
        placed(functools.partial(prepare_kernel, sources)),
        out_shape=(
            jax.ShapeDtypeStruct((total, width), jnp.bfloat16),
            jax.ShapeDtypeStruct((width // 128, 128 + ONES, total), jnp.bfloat16),
            jax.ShapeDtypeStruct((group, 2, depth, model), jnp.bfloat16),
        ),
        in_specs=whole(len(chunks) + len(parts)),
        out_specs=tuple(whole(3)),
        scratch_shapes=[pltpu.VMEM((total, width), jnp.bfloat16)],
        compiler_params=params(4),
        cost_estimate=cost(0, 5 * 2 * total * width),
        name="prepare",
    )(*chunks, *parts)


def flash(queries, k_ref, vt_ref, low, high, least, most):
    rows, width = queries.shape
    pairs = width // 128
    lane = lax.broadcasted_iota(jnp.int32, (rows, 128), 1) // 64
    masked = []
    for pair in range(pairs):
        part = queries[:, pair * 128 : (pair + 1) * 128]
        part = (part.astype(jnp.float32) * SCALING).astype(jnp.bfloat16)
        zero = jnp.zeros_like(part)
        masked.append(
            jnp.concatenate([jnp.where(lane == 0, part, zero), jnp.where(lane == 1, part, zero)], axis=0)
        )
    begin = least // ALIGN * ALIGN

    def step(tile, carry):
        due = begin + tile * TILE
        start = pl.multiple_of(jnp.minimum(due, k_ref.shape[0] - TILE), ALIGN)
        keys = start + lax.broadcasted_iota(jnp.int32, (TILE, 2 * rows), 0)
        bias = jnp.where((keys >= jnp.maximum(low, due)) & (keys < high), 0.0, NEGATIVE)
        after = []
        for pair in range(pairs):
            peak, total = carry[pair]
            scores = lax.dot_general(
                k_ref[pl.ds(start, TILE), pair * 128 : (pair + 1) * 128],
                masked[pair],
                (((1,), (1,)), ((), ())),
                preferred_element_type=jnp.float32,
            )
            scores = scores + bias
            top = jnp.maximum(peak, jnp.max(scores, axis=0, keepdims=True))
            weights = jnp.exp(scores - top).astype(jnp.bfloat16)
            total = total * jnp.exp(peak - top) + jnp.dot(
                vt_ref[pair, :, pl.ds(start, TILE)], weights, preferred_element_type=jnp.float32
            )
            after.append((top, total))
        return tuple(after)

    empty = (
        jnp.full((1, 2 * rows), NEGATIVE, jnp.float32),
        jnp.zeros((128 + ONES, 2 * rows), jnp.float32),
    )
    tiles = (most - begin + TILE - 1) // TILE
    carry = lax.fori_loop(0, tiles, step, (empty,) * pairs)
    outs = []
    for _, total in carry:
        result = total[:128] / total[128:129]
        outs += [result[:64, :rows], result[64:, rows:]]
    return jnp.concatenate(outs, axis=0).T


def twice(base, rows):
    lane = lax.broadcasted_iota(jnp.int32, (1, 2 * rows), 1)
    return base + jnp.where(lane >= rows, lane - rows, lane)


def half_of(turn, ids, order_ref):
    first = order_ref[2 * ids[0]]
    second = order_ref[2 * ids[0] + 1]
    return jnp.where(first < second, turn, 1 - turn)


def self_kernel(turn, ids, order_ref, lengths_ref, q_ref, k_ref, v_ref, out_ref):
    rows = out_ref.shape[0]
    half = half_of(turn, ids, order_ref)
    queries = q_ref[rows_at(half, rows), :]
    base = order_ref[2 * ids[0] + half] * rows
    places = twice(base, rows)
    low = jnp.zeros_like(places)
    least = jnp.int32(0)
    for end in sums_of(lengths_ref):
        low = jnp.where(places >= end, end, low)
        least = jnp.where(base >= end, end, least)
    result = flash(queries, k_ref, v_ref, low, places + 1, least, base + rows)
    out_ref[...] = result.astype(jnp.bfloat16)


def self_attention(turn, block_order, lengths, queries, keys, values, after=()):
    rows, width = queries.shape
    return pl.pallas_call(
        placed(skipping(functools.partial(self_kernel, turn), 6, len(after))),
        out_shape=jax.ShapeDtypeStruct((rows // 2, width), jnp.bfloat16),
        in_specs=smem(2) + whole(3) + anywhere(len(after)),
        out_specs=whole(1)[0],
        compiler_params=params(4),
        cost_estimate=cost(2e11, 0),
        name="self_attention",
    )(block_order, lengths, queries, keys, values, *after)


def cross_kernel(
    turn, ids, order_ref, lengths_ref, encs_ref,
    a0, a1, a2, a3, x_ref, wo_ref, wq_ref, k_ref, v_ref, hidden_ref, out_ref,
):
    rows, width = a0.shape
    member = ids[1]
    half = half_of(turn, ids, order_ref)
    mixed = x_ref[rows_at(half, rows), :].astype(jnp.float32)
    for i, piece in enumerate((a0, a1, a2, a3)):
        mixed = mixed + jnp.dot(
            piece[...], wo_ref[member ^ i], preferred_element_type=jnp.float32
        )
    hidden = normalize(mixed)
    hidden_ref[...] = hidden
    queries = jnp.dot(
        hidden.astype(jnp.bfloat16), wq_ref[...], preferred_element_type=jnp.float32
    ).astype(jnp.bfloat16)
    base = order_ref[2 * ids[0] + half] * rows
    places = twice(base, rows)
    ends, encs = sums_of(lengths_ref), sums_of(encs_ref)
    low = jnp.zeros_like(places)
    least = jnp.int32(0)
    for end, enc in zip(ends, encs):
        low = jnp.where(places >= end, enc, low)
        least = jnp.where(base >= end, enc, least)
    high = jnp.full_like(places, encs[-1])
    most = encs[-1]
    for end, enc in zip(reversed(ends), reversed(encs)):
        high = jnp.where(places < end, enc, high)
        most = jnp.where(base + rows - 1 < end, enc, most)
    result = flash(queries, k_ref, v_ref, low, high, least, most)
    out_ref[...] = result.astype(jnp.bfloat16)


def cross_attention(turn, block_order, lengths, encs, pieces, x, w_out, w_cq, keys, values):
    rows, width = pieces[0].shape
    model = x.shape[1]
    return pl.pallas_call(
        placed(functools.partial(cross_kernel, turn)),
        out_shape=(
            jax.ShapeDtypeStruct((rows, model), jnp.float32),
            jax.ShapeDtypeStruct((rows, width), jnp.bfloat16),
        ),
        in_specs=smem(3) + whole(9),
        out_specs=tuple(whole(2)),
        compiler_params=params(5),
        cost_estimate=cost(2e11, 0),
        name="cross_attention",
    )(block_order, lengths, encs, *pieces, x, w_out, w_cq, keys, values)


PART = 1024


def mlp_kernel(
    turn, ids, order_ref, c0, c1, c2, c3, hidden_ref, wco_ref, up_ref, down_ref, wn_ref, *refs
):
    out_ref, next_ref, bf_ref, sum_ref, held_ref, sems = refs[-6:]
    member = ids[1]
    half = half_of(turn, ids, order_ref)
    rows, width = c0.shape
    mixed = hidden_ref[...]
    for i, piece in enumerate((c0, c1, c2, c3)):
        mixed = mixed + jnp.dot(
            piece[...], wco_ref[rows_at(member ^ i, width), :], preferred_element_type=jnp.float32
        )
    second = normalize(mixed)
    bf_ref[...] = second.astype(jnp.bfloat16)
    sum_ref[...] = second
    for i in range(up_ref.shape[1] // PART):
        at = slice(i * PART, (i + 1) * PART)
        raised = jnp.dot(bf_ref[...], up_ref[:, at], preferred_element_type=jnp.float32)
        inner = (raised * (1.0 + lax.erf(raised * (0.5**0.5))) * 0.5).astype(jnp.bfloat16)
        sum_ref[...] += jnp.dot(inner, down_ref[at, :], preferred_element_type=jnp.float32)
    output = normalize(sum_ref[...])
    sum_ref[...] = output
    own = pltpu.make_async_copy(
        sum_ref.at[rows_at(member % 2, rows // 2), :], out_ref, sems.at[3]
    )

    @pl.when(member // 2 == half)
    def _():
        own.start()

    bf_ref[...] = output.astype(jnp.bfloat16)
    copies = []
    for c in range(3):
        held_ref[c] = jnp.dot(bf_ref[...], wn_ref[c], preferred_element_type=jnp.float32)
        copy = pltpu.make_async_copy(
            held_ref.at[c], next_ref.at[c, rows_at(half, rows), :], sems.at[c]
        )
        copy.start()
        copies.append(copy)
    for copy in copies:
        copy.wait()

    @pl.when(member // 2 == half)
    def _():
        own.wait()


def mlp(turn, block_order, pieces, hidden, w_co, weights, before):
    rows, width = pieces[0].shape
    model = w_co.shape[0]
    return pl.pallas_call(
        placed(functools.partial(mlp_kernel, turn)),
        out_shape=(
            jax.ShapeDtypeStruct((rows // 2, model), jnp.float32),
            jax.ShapeDtypeStruct((3, 2 * rows, width), jnp.float32),
        ),
        in_specs=smem(1) + whole(9) + anywhere(len(before)),
        out_specs=tuple(anywhere(2)),
        scratch_shapes=[
            pltpu.VMEM((rows, model), jnp.bfloat16),
            pltpu.VMEM((rows, model), jnp.float32),
            pltpu.VMEM((3, rows, width), jnp.float32),
            pltpu.SemaphoreType.DMA((4,)),
        ],
        input_output_aliases={10 + i: i for i in range(len(before))},
        compiler_params=params(8),
        cost_estimate=cost(6e9, 0),
        name="mlp",
    )(block_order, *pieces, hidden, w_co, *weights, *before)


def over_head(x, size):
    return [x] + [lax.ppermute(x, "head", xor(size, j)) for j in range(1, size)]


def over_chips(x, size):
    return [x] + [lax.ppermute(x, "blk", xor(size, s)) for s in range(2, size, 2)]


def on_device(
    tokens, block_order, request_lengths, enc_lengths, w_qkv, w_out, enc_kv, w_cq, w_co, w_up,
    w_down, w_next,
):
    group = lax.axis_size("head")
    cycle = lax.axis_size("blk")
    width = w_qkv.shape[2]
    paired = cycle == 8

    rows = over_head(tokens, group)
    tokens, w_qkv, part = fetch(
        (tokens, w_qkv, w_out),
        (tokens.shape, w_qkv.shape, (width // 2, w_out.shape[1])),
        ("", "", "rows"), 2,
    )
    x, queries, kv, part = project([tokens] + rows[1:], w_qkv, part)
    w_cq, w_co, w_up, w_down, w_next = fetch(
        (w_cq, w_co, w_up, w_down, w_next),
        ((w_cq.shape[0], width), w_co.shape, w_up.shape, w_down.shape, w_next.shape),
        ("columns", "", "", "", ""), 34, (queries,),
    )
    near = tuple(range(0, cycle, 2))
    if paired:
        kvs = over_chips(kv, cycle)
        parts = over_head(part, group)
        (kvs,) = bundle([kvs], [w_up] + parts[1:3])
        kvs = [kvs, lax.ppermute(kvs, "blk", xor(cycle, 1))]
        sources = [(True, near), (True, tuple(s + 1 for s in near))]
    else:
        kvs = [lax.all_gather(kv, "blk", axis=0)]
        sources = [(False, tuple(range(cycle)))]
    keys, values, cache, enc_kv = order(block_order, kvs, sources, enc_kv)
    attended = []
    for turn in range(2):
        mine = self_attention(
            turn, block_order, request_lengths, queries, keys, values, attended[0][:1] if turn else ()
        )
        attended.append(over_head(mine, group))
    if paired:
        own = bundle([parts, over_chips(enc_kv, cycle)], attended[1][:1] + attended[0][1:])
        parts, enc = zip(own, [lax.ppermute(y, "blk", xor(cycle, 1)) for y in own])
    else:
        enc = [lax.all_gather(enc_kv, "blk", axis=0)]
        halves = w_out.reshape(2, width // 2, -1)
        side = lax.axis_index("blk") % 2
        parts = [
            bundle([over_head(lax.dynamic_index_in_dim(halves, side ^ i, 0, False), group)], ())[0]
            for i in range(2)
        ]
    enc_keys, enc_values, w_out = prepare(enc, sources, parts)
    w_out = w_out.reshape(group, width, -1)

    outs = ()
    for turn in range(2):
        hidden, crossed = cross_attention(
            turn, block_order, request_lengths, enc_lengths, attended[turn], x, w_out,
            w_cq, enc_keys, enc_values,
        )
        outs = mlp(
            turn, block_order, over_head(crossed, group), hidden, w_co, (w_up, w_down, w_next),
            outs,
        )
    return (outs[0], cache, outs[1])


def solution(mesh):
    in_specs = (
        P(("blk", "head"), None),
        P(),
        P(),
        P(),
        P(None, None, "head"),
        P("head", None),
        P(None, "blk", "head"),
        P(),
        P(),
        P(),
        P(),
        P(None, None, "head"),
    )
    out_specs = (P(("blk", "head"), None), P(None, "blk", "head"), P(None, "blk", "head"))
    return jax.shard_map(
        on_device, mesh=mesh, in_specs=in_specs, out_specs=out_specs, check_vma=False
    )
```

time: 118 us -> 107 us (0.907)
  the two profiles are of different devices: /device:TPU:0 before, /device:TPU:8 now
where the time goes in v3:
time: 107 us; the launch traced here: 106 us
  Pallas kernels  41.7 us (39%)
  starting transfers between devices  30.9 us (29%)
  waiting for transfers between devices  27.7 us (26%)
  local copies, waits for them, and re-layouts  4.82 us (5%)
    ppermute x18, waiting for transfers between devices, over_head(): return [x] + [lax.ppermute(x, 'head', xor(size, j)) for j in range(1, size)]  23.4 us
    ppermute x18, starting transfers between devices, over_head(): return [x] + [lax.ppermute(x, 'head', xor(size, j)) for j in range(1, size)]  23.1 us
    pallas_call x2, Pallas kernels, mlp(): pl.pallas_call(placed(functools.partial(mlp_kernel, turn)), out_shape=(ja...  12.8 us
    pallas_call x2, Pallas kernels, fetch(): pl.pallas_call(placed(skipping(functools.partial(fetch_kernel, cuts), 1 +...  9.65 us
    pallas_call x2, Pallas kernels, self_attention(): pl.pallas_call(placed(skipping(functools.partial(self_kernel, turn), 6, l...  8.58 us
    ppermute x6, starting transfers between devices, over_chips(): lax.ppermute(x, 'blk', xor(size, s))  7.1 us
    pallas_call x2, Pallas kernels, cross_attention(): pl.pallas_call(placed(functools.partial(cross_kernel, turn)), out_shape=(...  6.03 us
    unnamed x24, local copies, waits for them, and re-layouts  4.82 us
  transfers between devices with their start and end apart: 27, of which 10 were waited for; matrix products, arithmetic and copies ran while one was open for 0% of the time, Pallas kernels for 32%

profile of v3, /device:TPU:8, one launch (start us, length us, event | category | flops | bytes accessed | tf_op | source)
XLA Modules:
  0.0 106.1 jit_solution(6904701945441418776)
XLA Ops:
  0.7 3.0 %collective-permute-start.1 = (bf16[96,1024]{1,0:T(8,128)(2,1)}, bf16[96,1024]{1,0:T(8,128)(2,1)S(1)}, u32[]{:S(2)}, u32[]{:S(2)}) collective-permute-start(bf16[96,1024]{1,0:T(8,128)(2,1)} %refs_0_.9), channel_id=1, source_target_pairs={{0,2},{1,3},{2,0},{3,1},{4,6},{5,7},{6,4},{7,5},{8,10},{9,11},{10,... | collective-permute-start | bytes 589832 | tf_op jit(solution)/shard_map/ppermute | solution.py:459
  3.7 0.5 collective-permute-start.2
  4.2 1.4 %copy-done.2 = bf16[3,1024,256]{2,1,0:T(8,128)(2,1)S(1)} copy-done((bf16[3,1024,256]{2,1,0:T(8,128)(2,1)S(1)}, bf16[3,1024,256]{2,1,0:T(8,128)(2,1)}, u32[]{:S(2)}) %copy-start.2) | copy-done | bytes 1572888
  5.6 1.0 copy-done.4
  6.6 0.9 copy-done.6
  7.6 0.4 fetch.2
  8.0 0.9 collective-permute-done.refs_1_
  8.8 9.0 %collective-permute-done.1.refs_2_ = bf16[96,1024]{1,0:T(8,128)(2,1)S(1)} collective-permute-done((bf16[96,1024]{1,0:T(8,128)(2,1)}, bf16[96,1024]{1,0:T(8,128)(2,1)S(1)}, u32[]{:S(2)}, u32[]{:S(2)}) %collective-permute-start.1) | collective-permute-done | bytes 196640 | tf_op jit(solution)/shard_map/ppermute | solution.py:459
  17.8 3.6 %collective-permute-done.2.refs_3_ = bf16[96,1024]{1,0:T(8,128)(2,1)S(1)} collective-permute-done((bf16[96,1024]{1,0:T(8,128)(2,1)}, bf16[96,1024]{1,0:T(8,128)(2,1)S(1)}, u32[]{:S(2)}, u32[]{:S(2)}) %collective-permute-start.2) | collective-permute-done | bytes 196640 | tf_op jit(solution)/shard_map/ppermute | solution.py:459
  21.4 0.8 project.1
  22.3 1.6 %collective-permute-start.3 = (bf16[2,384,256]{2,1,0:T(8,128)(2,1)S(1)}, bf16[2,384,256]{2,1,0:T(8,128)(2,1)S(1)}, u32[]{:S(2)}, u32[]{:S(2)}) collective-permute-start(bf16[2,384,256]{2,1,0:T(8,128)(2,1)S(1)} %get-tuple-element.36.refs_0_), channel_id=1, source_target_pairs={{0,8},{4,12},{8,0},{12,4},{16,24},{20,28},{24,16},{28,20},{1,9},{5... | collective-permute-start | bytes 1179656 | tf_op jit(solution)/shard_map/ppermute | solution.py:463
  23.8 1.5 %collective-permute-start.4 = (bf16[2,384,256]{2,1,0:T(8,128)(2,1)S(1)}, bf16[2,384,256]{2,1,0:T(8,128)(2,1)S(1)}, u32[]{:S(2)}, u32[]{:S(2)}) collective-permute-start(bf16[2,384,256]{2,1,0:T(8,128)(2,1)S(1)} %get-tuple-element.36.refs_0_), channel_id=1, source_target_pairs={{0,16},{4,20},{8,24},{12,28},{16,0},{20,4},{24,8},{28,12},{1,17},{... | collective-permute-start | bytes 1179656 | tf_op jit(solution)/shard_map/ppermute | solution.py:463
  25.3 0.5 collective-permute-start.5
  25.8 3.0 %collective-permute-start.7 = (bf16[128,1024]{1,0:T(8,128)(2,1)S(1)}, bf16[128,1024]{1,0:T(8,128)(2,1)S(1)}, u32[]{:S(2)}, u32[]{:S(2)}) collective-permute-start(bf16[128,1024]{1,0:T(8,128)(2,1)S(1)} %get-tuple-element.38.refs_0_), channel_id=1, source_target_pairs={{0,2},{1,3},{2,0},{3,1},{4,6},{5,7},{6,4},{7,5},{8,10},{9,11},{10,... | collective-permute-start | bytes 786440 | tf_op jit(solution)/shard_map/ppermute | solution.py:459
  28.8 1.4 %copy-done.3 = bf16[3,1024,256]{2,1,0:T(8,128)(2,1)S(1)} copy-done((bf16[3,1024,256]{2,1,0:T(8,128)(2,1)S(1)}, bf16[3,1024,256]{2,1,0:T(8,128)(2,1)}, u32[]{:S(2)}) %copy-start.3) | copy-done | bytes 1572888
  30.3 9.3 %fetch.3 = (bf16[1024,256]{1,0:T(8,128)(2,1)S(1)}, bf16[1024,1024]{1,0:T(8,128)(2,1)S(1)}, bf16[1024,4096]{1,0:T(8,128)(2,1)S(1)}, bf16[4096,1024]{1,0:T(8,128)(2,1)}, bf16[3,1024,256]{2,1,0:T(8,128)(2,1)S(1)}) custom-call(bf16[1024,1024]{1,0:T(8,128)(2,1)S(1)} %copy-done, bf16[1024,1024]{1,0:T(8,128)(2,1)S(1)} %copy-done.1, bf16[1024,4096]{1,0:T(8,128)(2,1)} %refs_2_.5, ...), custom_call_target="tpu_custom_call" | custom-call | bytes 1048576 | tf_op jit(solution)/shard_map/fetch/pallas_call | solution.py:125
  39.6 2.1 %collective-permute-done.4.refs_2_ = bf16[2,384,256]{2,1,0:T(8,128)(2,1)S(1)} collective-permute-done((bf16[2,384,256]{2,1,0:T(8,128)(2,1)S(1)}, bf16[2,384,256]{2,1,0:T(8,128)(2,1)S(1)}, u32[]{:S(2)}, u32[]{:S(2)}) %collective-permute-start.4) | collective-permute-done | bytes 393248 | tf_op jit(solution)/shard_map/ppermute | solution.py:463
  41.9 1.6 %collective-permute-start.12 = (bf16[128,1024]{1,0:T(8,128)(2,1)S(1)}, bf16[128,1024]{1,0:T(8,128)(2,1)S(1)}, u32[]{:S(2)}, u32[]{:S(2)}) collective-permute-start(bf16[128,1024]{1,0:T(8,128)(2,1)S(1)} %get-tuple-element.38.refs_0_), channel_id=1, source_target_pairs={{0,3},{1,2},{2,1},{3,0},{4,7},{5,6},{6,5},{7,4},{8,11},{9,10},{10,... | collective-permute-start | bytes 786440 | tf_op jit(solution)/shard_map/ppermute | solution.py:459
  43.5 1.8 %collective-permute-done.8.refs_2_ = bf16[4,2,384,256]{3,2,1,0:T(8,128)(2,1)S(1)} collective-permute-done((bf16[4,2,384,256]{3,2,1,0:T(8,128)(2,1)S(1)}, bf16[4,2,384,256]{3,2,1,0:T(8,128)(2,1)S(1)}, u32[]{:S(2)}, u32[]{:S(2)}) %collective-permute-start.8) | collective-permute-done | bytes 1572896 | tf_op jit(solution)/shard_map/ppermute | solution.py:492
  45.3 2.6 %order.1 = (bf16[3072,256]{1,0:T(8,128)(2,1)S(1)}, bf16[2,144,3072]{2,1,0:T(8,128)(2,1)S(1)}, bf16[2,384,256]{2,1,0:T(8,128)(2,1)}, bf16[2,256,256]{2,1,0:T(8,128)(2,1)S(1)}) custom-call(s32[16]{0:T(128)S(1)} %copy-done.7, bf16[4,2,384,256]{3,2,1,0:T(8,128)(2,1)S(1)} %bundle.2.refs_1_, bf16[4,2,384,256]{3,2,1,0:T(8,128)(2,1)S(1)} %collective-permute-done.8.refs_2_, ...), custom_call_target="tpu_custom_call" | custom-call | bytes 393216 | tf_op jit(solution)/shard_map/order/pallas_call | solution.py:192
  47.9 3.8 %self_attention.2.refs_5_.refs_3_ = bf16[192,256]{1,0:T(8,128)(2,1)S(1)} custom-call(s32[16]{0:T(128)S(1)} %copy-done.7, s32[9]{0:T(128)S(1)} %copy-done.8, bf16[384,256]{1,0:T(8,128)(2,1)S(1)} %get-tuple-element.35.refs_5_.refs_2_, bf16[3072,256]{1,0:T(8,128)(2,1)S(1)} %get-tuple-element.39.refs_3_, bf16[2,144,3072]{2,1,0:T(8,128)(2,1)S(1)} %get-tuple-element.40.refs_4_), custom_call_target="tpu_custom_call" | custom-call | flops 10000000000 | tf_op jit(solution)/shard_map/self_attention/pallas_call | solution.py:322
  51.9 1.6 %collective-permute-start.14 = (bf16[2,256,256]{2,1,0:T(8,128)(2,1)S(1)}, bf16[2,256,256]{2,1,0:T(8,128)(2,1)S(1)}, u32[]{:S(2)}, u32[]{:S(2)}) collective-permute-start(bf16[2,256,256]{2,1,0:T(8,128)(2,1)S(1)} %get-tuple-element.42.refs_4_), channel_id=1, source_target_pairs={{0,16},{4,20},{8,24},{12,28},{16,0},{20,4},{24,8},{28,12},{1,17},{... | collective-permute-start | bytes 786440 | tf_op jit(solution)/shard_map/ppermute | solution.py:463
  53.5 1.9 %collective-permute-start.15 = (bf16[2,256,256]{2,1,0:T(8,128)(2,1)S(1)}, bf16[2,256,256]{2,1,0:T(8,128)(2,1)S(1)}, u32[]{:S(2)}, u32[]{:S(2)}) collective-permute-start(bf16[2,256,256]{2,1,0:T(8,128)(2,1)S(1)} %get-tuple-element.42.refs_4_), channel_id=1, source_target_pairs={{0,24},{4,28},{8,16},{12,20},{16,8},{20,12},{24,0},{28,4},{1,25},{... | collective-permute-start | bytes 786440 | tf_op jit(solution)/shard_map/ppermute | solution.py:463
  55.4 2.9 %collective-permute-start.17 = (bf16[192,256]{1,0:T(8,128)(2,1)S(1)}, bf16[192,256]{1,0:T(8,128)(2,1)S(1)}, u32[]{:S(2)}, u32[]{:S(2)}) collective-permute-start(bf16[192,256]{1,0:T(8,128)(2,1)S(1)} %self_attention.2.refs_5_.refs_3_), channel_id=1, source_target_pairs={{0,2},{1,3},{2,0},{3,1},{4,6},{5,7},{6,4},{7,5},{8,10},{9,11},{10,... | collective-permute-start | bytes 294920 | tf_op jit(solution)/shard_map/ppermute | solution.py:459
  58.3 0.5 collective-permute-start.18
  58.8 4.8 %self_attention.3.refs_8_.refs_3_ = bf16[192,256]{1,0:T(8,128)(2,1)S(1)} custom-call(s32[16]{0:T(128)S(1)} %copy-done.7, s32[9]{0:T(128)S(1)} %copy-done.8, bf16[384,256]{1,0:T(8,128)(2,1)S(1)} %get-tuple-element.35.refs_5_.refs_2_, bf16[3072,256]{1,0:T(8,128)(2,1)S(1)} %get-tuple-element.39.refs_3_, bf16[2,144,3072]{2,1,0:T(8,128)(2,1)S(1)} %get-tuple-element.40.refs_4_, ...), custom_call_target="tpu_custom_call" | custom-call | flops 10000000000 | tf_op jit(solution)/shard_map/self_attention/pallas_call | solution.py:322
  63.6 0.6 collective-permute-done.17.refs_10_.refs_5_
  64.2 2.1 %collective-permute-done.18.refs_11_.refs_6_ = bf16[192,256]{1,0:T(8,128)(2,1)S(1)} collective-permute-done((bf16[192,256]{1,0:T(8,128)(2,1)S(1)}, bf16[192,256]{1,0:T(8,128)(2,1)S(1)}, u32[]{:S(2)}, u32[]{:S(2)}) %collective-permute-start.18) | collective-permute-done | bytes 98336 | tf_op jit(solution)/shard_map/ppermute | solution.py:459
  66.3 0.4 collective-permute-done.14.refs_6_
  66.7 0.1 bundle.3
  66.8 0.2 collective-permute-start.19
  67.0 0.4 collective-permute-start.20
  67.4 2.7 %collective-permute-start.10 = (bf16[192,256]{1,0:T(8,128)(2,1)S(1)}, bf16[192,256]{1,0:T(8,128)(2,1)S(1)}, u32[]{:S(2)}, u32[]{:S(2)}) collective-permute-start(bf16[192,256]{1,0:T(8,128)(2,1)S(1)} %self_attention.3.refs_8_.refs_3_), channel_id=1, source_target_pairs={{0,2},{1,3},{2,0},{3,1},{4,6},{5,7},{6,4},{7,5},{8,10},{9,11},{10,... | collective-permute-start | bytes 294920 | tf_op jit(solution)/shard_map/ppermute | solution.py:459
  70.2 0.5 collective-permute-start.11
  70.7 1.1 %collective-permute-start.9 = (bf16[192,256]{1,0:T(8,128)(2,1)S(1)}, bf16[192,256]{1,0:T(8,128)(2,1)S(1)}, u32[]{:S(2)}, u32[]{:S(2)}) collective-permute-start(bf16[192,256]{1,0:T(8,128)(2,1)S(1)} %self_attention.3.refs_8_.refs_3_), channel_id=1, source_target_pairs={{0,1},{1,0},{2,3},{3,2},{4,5},{5,4},{6,7},{7,6},{8,9},{9,8},{10,11... | collective-permute-start | bytes 294920 | tf_op jit(solution)/shard_map/ppermute | solution.py:459
  71.8 1.0 prepare.1
  72.8 2.9 %cross_attention.3 = (f32[192,1024]{1,0:T(8,128)S(1)}, bf16[192,256]{1,0:T(8,128)(2,1)S(1)}) custom-call(s32[16]{0:T(128)S(1)} %copy-done.7, s32[9]{0:T(128)S(1)} %copy-done.8, s32[9]{0:T(128)S(1)} %copy-done.9, bf16[192,256]{1,0:T(8,128)(2,1)S(1)} %self_attention.2.refs_5_.refs_3_, bf16[192,256]{1,0:T(8,128)(2,1)S(1)} %collective-permute-done.16.refs_9_.refs_4_, ...), custom_call_target="tpu_custom_call" | custom-call | flops 10000000000 | tf_op jit(solution)/shard_map/cross_attention/pallas_call | solution.py:370
  75.8 1.1 %collective-permute-start.24 = (bf16[192,256]{1,0:T(8,128)(2,1)S(1)}, bf16[192,256]{1,0:T(8,128)(2,1)S(1)}, u32[]{:S(2)}, u32[]{:S(2)}) collective-permute-start(bf16[192,256]{1,0:T(8,128)(2,1)S(1)} %get-tuple-element.54.refs_1_), channel_id=1, source_target_pairs={{0,1},{1,0},{2,3},{3,2},{4,5},{5,4},{6,7},{7,6},{8,9},{9,8},{10,11... | collective-permute-start | bytes 294920 | tf_op jit(solution)/shard_map/ppermute | solution.py:459
  76.9 2.0 %collective-permute-start.25 = (bf16[192,256]{1,0:T(8,128)(2,1)S(1)}, bf16[192,256]{1,0:T(8,128)(2,1)S(1)}, u32[]{:S(2)}, u32[]{:S(2)}) collective-permute-start(bf16[192,256]{1,0:T(8,128)(2,1)S(1)} %get-tuple-element.54.refs_1_), channel_id=1, source_target_pairs={{0,2},{1,3},{2,0},{3,1},{4,6},{5,7},{6,4},{7,5},{8,10},{9,11},{10,... | collective-permute-start | bytes 294920 | tf_op jit(solution)/shard_map/ppermute | solution.py:459
  78.9 0.4 collective-permute-start.26
  79.3 0.3 collective-permute-done.11.refs_6_
  79.7 3.1 %cross_attention.2 = (f32[192,1024]{1,0:T(8,128)S(1)}, bf16[192,256]{1,0:T(8,128)(2,1)S(1)}) custom-call(s32[16]{0:T(128)S(1)} %copy-done.7, s32[9]{0:T(128)S(1)} %copy-done.8, s32[9]{0:T(128)S(1)} %copy-done.9, bf16[192,256]{1,0:T(8,128)(2,1)S(1)} %self_attention.3.refs_8_.refs_3_, bf16[192,256]{1,0:T(8,128)(2,1)S(1)} %collective-permute-done.9.refs_4_, ...), custom_call_target="tpu_custom_call" | custom-call | flops 10000000000 | tf_op jit(solution)/shard_map/cross_attention/pallas_call | solution.py:370
  82.8 1.8 %collective-permute-start.21 = (bf16[192,256]{1,0:T(8,128)(2,1)S(1)}, bf16[192,256]{1,0:T(8,128)(2,1)S(1)}, u32[]{:S(2)}, u32[]{:S(2)}) collective-permute-start(bf16[192,256]{1,0:T(8,128)(2,1)S(1)} %get-tuple-element.49.refs_1_), channel_id=1, source_target_pairs={{0,1},{1,0},{2,3},{3,2},{4,5},{5,4},{6,7},{7,6},{8,9},{9,8},{10,11... | collective-permute-start | bytes 294920 | tf_op jit(solution)/shard_map/ppermute | solution.py:459
  84.6 1.2 %collective-permute-start.22 = (bf16[192,256]{1,0:T(8,128)(2,1)S(1)}, bf16[192,256]{1,0:T(8,128)(2,1)S(1)}, u32[]{:S(2)}, u32[]{:S(2)}) collective-permute-start(bf16[192,256]{1,0:T(8,128)(2,1)S(1)} %get-tuple-element.49.refs_1_), channel_id=1, source_target_pairs={{0,2},{1,3},{2,0},{3,1},{4,6},{5,7},{6,4},{7,5},{8,10},{9,11},{10,... | collective-permute-start | bytes 294920 | tf_op jit(solution)/shard_map/ppermute | solution.py:459
  85.8 0.5 collective-permute-start.23
  86.3 6.8 %collective-permute-done.26.refs_4_ = bf16[192,256]{1,0:T(8,128)(2,1)S(1)} collective-permute-done((bf16[192,256]{1,0:T(8,128)(2,1)S(1)}, bf16[192,256]{1,0:T(8,128)(2,1)S(1)}, u32[]{:S(2)}, u32[]{:S(2)}) %collective-permute-start.26) | collective-permute-done | bytes 98336 | tf_op jit(solution)/shard_map/ppermute | solution.py:459
  93.2 6.4 %mlp.2 = (f32[96,1024]{1,0:T(8,128)}, f32[3,384,256]{2,1,0:T(8,128)}) custom-call(s32[16]{0:T(128)S(1)} %copy-done.7, bf16[192,256]{1,0:T(8,128)(2,1)S(1)} %get-tuple-element.54.refs_1_, bf16[192,256]{1,0:T(8,128)(2,1)S(1)} %collective-permute-done.24.refs_2_, bf16[192,256]{1,0:T(8,128)(2,1)S(1)} %collective-permute-done.25.refs_3_, ...), custom_call_target="tpu_custom_call" | custom-call | flops 300000000 | tf_op jit(solution)/shard_map/mlp/pallas_call | solution.py:437
  99.6 6.4 %mlp.3 = (f32[96,1024]{1,0:T(8,128)}, f32[3,384,256]{2,1,0:T(8,128)}) custom-call(s32[16]{0:T(128)S(1)} %copy-done.7, bf16[192,256]{1,0:T(8,128)(2,1)S(1)} %get-tuple-element.49.refs_1_, bf16[192,256]{1,0:T(8,128)(2,1)S(1)} %collective-permute-done.21.refs_2_, ...), custom_call_target="tpu_custom_call", output_to_operand_aliasing={{0}: (10, {}), {1}: (11, {})} | custom-call | flops 300000000 | tf_op jit(solution)/shard_map/mlp/pallas_call | solution.py:437
  (44 shorter events, 0.5 us)
Async XLA Ops:
  0.6 8.2 %collective-permute-start = (bf16[96,1024]{1,0:T(8,128)(2,1)}, bf16[96,1024]{1,0:T(8,128)(2,1)S(1)}, u32[]{:S(2)}, u32[]{:S(2)}) collective-permute-start(bf16[96,1024]{1,0:T(8,128)(2,1)} %refs_0_.9), channel_id=1, source_target_pairs={{0,1},{1,0},{2,3},{3,2},{4,5},{5,4},{6,7},{7,6},{8,9},{9,8},{10,11... | collective-permute-start | bytes 589832 | tf_op jit(solution)/shard_map/ppermute | solution.py:459
  0.7 17.1 %collective-permute-start.1 = (bf16[96,1024]{1,0:T(8,128)(2,1)}, bf16[96,1024]{1,0:T(8,128)(2,1)S(1)}, u32[]{:S(2)}, u32[]{:S(2)}) collective-permute-start(bf16[96,1024]{1,0:T(8,128)(2,1)} %refs_0_.9), channel_id=1, source_target_pairs={{0,2},{1,3},{2,0},{3,1},{4,6},{5,7},{6,4},{7,5},{8,10},{9,11},{10,... | collective-permute-start | bytes 589832 | tf_op jit(solution)/shard_map/ppermute | solution.py:459
  3.7 17.7 %collective-permute-start.2 = (bf16[96,1024]{1,0:T(8,128)(2,1)}, bf16[96,1024]{1,0:T(8,128)(2,1)S(1)}, u32[]{:S(2)}, u32[]{:S(2)}) collective-permute-start(bf16[96,1024]{1,0:T(8,128)(2,1)} %refs_0_.9), channel_id=1, source_target_pairs={{0,3},{1,2},{2,1},{3,0},{4,7},{5,6},{6,5},{7,4},{8,11},{9,10},{10,... | collective-permute-start | bytes 589832 | tf_op jit(solution)/shard_map/ppermute | solution.py:459
  4.2 1.4 %copy-start.2 = (bf16[3,1024,256]{2,1,0:T(8,128)(2,1)S(1)}, bf16[3,1024,256]{2,1,0:T(8,128)(2,1)}, u32[]{:S(2)}) copy-start(bf16[3,1024,256]{2,1,0:T(8,128)(2,1)} %refs_1_.6) | copy-start | bytes 4718596
  5.6 1.0 copy-start.4
  6.6 0.9 copy-start.6
  7.6 21.3 %copy-start.1 = (bf16[1024,1024]{1,0:T(8,128)(2,1)S(1)}, bf16[1024,1024]{1,0:T(8,128)(2,1)}, u32[]{:S(2)}) copy-start(bf16[1024,1024]{1,0:T(8,128)(2,1)} %refs_1_.7) | copy-start | bytes 6291460
  7.9 20.9 %copy-start = (bf16[1024,1024]{1,0:T(8,128)(2,1)S(1)}, bf16[1024,1024]{1,0:T(8,128)(2,1)}, u32[]{:S(2)}) copy-start(bf16[1024,1024]{1,0:T(8,128)(2,1)} %refs_0_.10) | copy-start | bytes 6291460
  22.3 17.3 %collective-permute-start.3 = (bf16[2,384,256]{2,1,0:T(8,128)(2,1)S(1)}, bf16[2,384,256]{2,1,0:T(8,128)(2,1)S(1)}, u32[]{:S(2)}, u32[]{:S(2)}) collective-permute-start(bf16[2,384,256]{2,1,0:T(8,128)(2,1)S(1)} %get-tuple-element.36.refs_0_), channel_id=1, source_target_pairs={{0,8},{4,12},{8,0},{12,4},{16,24},{20,28},{24,16},{28,20},{1,9},{5... | collective-permute-start | bytes 1179656 | tf_op jit(solution)/shard_map/ppermute | solution.py:463
  23.8 17.9 %collective-permute-start.4 = (bf16[2,384,256]{2,1,0:T(8,128)(2,1)S(1)}, bf16[2,384,256]{2,1,0:T(8,128)(2,1)S(1)}, u32[]{:S(2)}, u32[]{:S(2)}) collective-permute-start(bf16[2,384,256]{2,1,0:T(8,128)(2,1)S(1)} %get-tuple-element.36.refs_0_), channel_id=1, source_target_pairs={{0,16},{4,20},{8,24},{12,28},{16,0},{20,4},{24,8},{28,12},{1,17},{... | collective-permute-start | bytes 1179656 | tf_op jit(solution)/shard_map/ppermute | solution.py:463
  25.3 16.4 %collective-permute-start.5 = (bf16[2,384,256]{2,1,0:T(8,128)(2,1)S(1)}, bf16[2,384,256]{2,1,0:T(8,128)(2,1)S(1)}, u32[]{:S(2)}, u32[]{:S(2)}) collective-permute-start(bf16[2,384,256]{2,1,0:T(8,128)(2,1)S(1)} %get-tuple-element.36.refs_0_), channel_id=1, source_target_pairs={{0,24},{4,28},{8,16},{12,20},{16,8},{20,12},{24,0},{28,4},{1,25},{... | collective-permute-start | bytes 1179656 | tf_op jit(solution)/shard_map/ppermute | solution.py:463
  25.8 13.7 %collective-permute-start.6 = (bf16[128,1024]{1,0:T(8,128)(2,1)S(1)}, bf16[128,1024]{1,0:T(8,128)(2,1)S(1)}, u32[]{:S(2)}, u32[]{:S(2)}) collective-permute-start(bf16[128,1024]{1,0:T(8,128)(2,1)S(1)} %get-tuple-element.38.refs_0_), channel_id=1, source_target_pairs={{0,1},{1,0},{2,3},{3,2},{4,5},{5,4},{6,7},{7,6},{8,9},{9,8},{10,11... | collective-permute-start | bytes 786440 | tf_op jit(solution)/shard_map/ppermute | solution.py:459
  25.8 13.7 %collective-permute-start.7 = (bf16[128,1024]{1,0:T(8,128)(2,1)S(1)}, bf16[128,1024]{1,0:T(8,128)(2,1)S(1)}, u32[]{:S(2)}, u32[]{:S(2)}) collective-permute-start(bf16[128,1024]{1,0:T(8,128)(2,1)S(1)} %get-tuple-element.38.refs_0_), channel_id=1, source_target_pairs={{0,2},{1,3},{2,0},{3,1},{4,6},{5,7},{6,4},{7,5},{8,10},{9,11},{10,... | collective-permute-start | bytes 786440 | tf_op jit(solution)/shard_map/ppermute | solution.py:459
  28.8 1.4 %copy-start.3 = (bf16[3,1024,256]{2,1,0:T(8,128)(2,1)S(1)}, bf16[3,1024,256]{2,1,0:T(8,128)(2,1)}, u32[]{:S(2)}) copy-start(bf16[3,1024,256]{2,1,0:T(8,128)(2,1)} %refs_4_.1) | copy-start | bytes 4718596
  41.7 3.6 %copy-start.5 = (bf16[2,256,256]{2,1,0:T(8,128)(2,1)S(1)}, bf16[2,256,256]{2,1,0:T(8,128)(2,1)}, u32[]{:S(2)}) copy-start(bf16[2,256,256]{2,1,0:T(8,128)(2,1)} %refs_3_.3) | copy-start | bytes 786436
  41.7 3.6 %copy-start.7 = (s32[16]{0:T(128)S(1)}, s32[16]{0:T(128)}, u32[]{:S(2)}) copy-start(s32[16]{0:T(128)} %refs_0_.17) | copy-start | bytes 196
  41.8 6.1 %copy-start.8 = (s32[9]{0:T(128)S(1)}, s32[9]{0:T(128)}, u32[]{:S(2)}) copy-start(s32[9]{0:T(128)} %refs_1_.11) | copy-start | bytes 112
  41.8 3.5 %collective-permute-start.8 = (bf16[4,2,384,256]{3,2,1,0:T(8,128)(2,1)S(1)}, bf16[4,2,384,256]{3,2,1,0:T(8,128)(2,1)S(1)}, u32[]{:S(2)}, u32[]{:S(2)}) collective-permute-start(bf16[4,2,384,256]{3,2,1,0:T(8,128)(2,1)S(1)} %bundle.2.refs_1_), channel_id=1, source_target_pairs={{0,4},{4,0},{8,12},{12,8},{16,20},{20,16},{24,28},{28,24},{1,5},{5... | collective-permute-start | bytes 4718600 | tf_op jit(solution)/shard_map/ppermute | solution.py:492
  41.9 13.5 %collective-permute-start.12 = (bf16[128,1024]{1,0:T(8,128)(2,1)S(1)}, bf16[128,1024]{1,0:T(8,128)(2,1)S(1)}, u32[]{:S(2)}, u32[]{:S(2)}) collective-permute-start(bf16[128,1024]{1,0:T(8,128)(2,1)S(1)} %get-tuple-element.38.refs_0_), channel_id=1, source_target_pairs={{0,3},{1,2},{2,1},{3,0},{4,7},{5,6},{6,5},{7,4},{8,11},{9,10},{10,... | collective-permute-start | bytes 786440 | tf_op jit(solution)/shard_map/ppermute | solution.py:459
  51.7 6.6 %collective-permute-start.16 = (bf16[192,256]{1,0:T(8,128)(2,1)S(1)}, bf16[192,256]{1,0:T(8,128)(2,1)S(1)}, u32[]{:S(2)}, u32[]{:S(2)}) collective-permute-start(bf16[192,256]{1,0:T(8,128)(2,1)S(1)} %self_attention.2.refs_5_.refs_3_), channel_id=1, source_target_pairs={{0,1},{1,0},{2,3},{3,2},{4,5},{5,4},{6,7},{7,6},{8,9},{9,8},{10,11... | collective-permute-start | bytes 294920 | tf_op jit(solution)/shard_map/ppermute | solution.py:459
  51.8 14.5 %collective-permute-start.13 = (bf16[2,256,256]{2,1,0:T(8,128)(2,1)S(1)}, bf16[2,256,256]{2,1,0:T(8,128)(2,1)S(1)}, u32[]{:S(2)}, u32[]{:S(2)}) collective-permute-start(bf16[2,256,256]{2,1,0:T(8,128)(2,1)S(1)} %get-tuple-element.42.refs_4_), channel_id=1, source_target_pairs={{0,8},{4,12},{8,0},{12,4},{16,24},{20,28},{24,16},{28,20},{1,9},{5... | collective-permute-start | bytes 786440 | tf_op jit(solution)/shard_map/ppermute | solution.py:463
  51.9 14.8 %collective-permute-start.14 = (bf16[2,256,256]{2,1,0:T(8,128)(2,1)S(1)}, bf16[2,256,256]{2,1,0:T(8,128)(2,1)S(1)}, u32[]{:S(2)}, u32[]{:S(2)}) collective-permute-start(bf16[2,256,256]{2,1,0:T(8,128)(2,1)S(1)} %get-tuple-element.42.refs_4_), channel_id=1, source_target_pairs={{0,16},{4,20},{8,24},{12,28},{16,0},{20,4},{24,8},{28,12},{1,17},{... | collective-permute-start | bytes 786440 | tf_op jit(solution)/shard_map/ppermute | solution.py:463
  53.5 13.2 %collective-permute-start.15 = (bf16[2,256,256]{2,1,0:T(8,128)(2,1)S(1)}, bf16[2,256,256]{2,1,0:T(8,128)(2,1)S(1)}, u32[]{:S(2)}, u32[]{:S(2)}) collective-permute-start(bf16[2,256,256]{2,1,0:T(8,128)(2,1)S(1)} %get-tuple-element.42.refs_4_), channel_id=1, source_target_pairs={{0,24},{4,28},{8,16},{12,20},{16,8},{20,12},{24,0},{28,4},{1,25},{... | collective-permute-start | bytes 786440 | tf_op jit(solution)/shard_map/ppermute | solution.py:463
  55.4 8.9 %collective-permute-start.17 = (bf16[192,256]{1,0:T(8,128)(2,1)S(1)}, bf16[192,256]{1,0:T(8,128)(2,1)S(1)}, u32[]{:S(2)}, u32[]{:S(2)}) collective-permute-start(bf16[192,256]{1,0:T(8,128)(2,1)S(1)} %self_attention.2.refs_5_.refs_3_), channel_id=1, source_target_pairs={{0,2},{1,3},{2,0},{3,1},{4,6},{5,7},{6,4},{7,5},{8,10},{9,11},{10,... | collective-permute-start | bytes 294920 | tf_op jit(solution)/shard_map/ppermute | solution.py:459
  58.3 8.0 %collective-permute-start.18 = (bf16[192,256]{1,0:T(8,128)(2,1)S(1)}, bf16[192,256]{1,0:T(8,128)(2,1)S(1)}, u32[]{:S(2)}, u32[]{:S(2)}) collective-permute-start(bf16[192,256]{1,0:T(8,128)(2,1)S(1)} %self_attention.2.refs_5_.refs_3_), channel_id=1, source_target_pairs={{0,3},{1,2},{2,1},{3,0},{4,7},{5,6},{6,5},{7,4},{8,11},{9,10},{10,... | collective-permute-start | bytes 294920 | tf_op jit(solution)/shard_map/ppermute | solution.py:459
  66.8 5.0 %collective-permute-start.19 = (bf16[4,2,256,256]{3,2,1,0:T(8,128)(2,1)S(1)}, bf16[4,2,256,256]{3,2,1,0:T(8,128)(2,1)S(1)}, u32[]{:S(2)}, u32[]{:S(2)}) collective-permute-start(bf16[4,2,256,256]{3,2,1,0:T(8,128)(2,1)S(1)} %get-tuple-element.43.refs_0_), channel_id=1, source_target_pairs={{0,4},{4,0},{8,12},{12,8},{16,20},{20,16},{24,28},{28,24},{1,5},{5... | collective-permute-start | bytes 3145736 | tf_op jit(solution)/shard_map/ppermute | solution.py:506
  67.0 5.8 %copy-start.9 = (s32[9]{0:T(128)S(1)}, s32[9]{0:T(128)}, u32[]{:S(2)}) copy-start(s32[9]{0:T(128)} %refs_2_.7) | copy-start | bytes 112
  67.0 4.8 %collective-permute-start.20 = (bf16[4,128,1024]{2,1,0:T(8,128)(2,1)S(1)}, bf16[4,128,1024]{2,1,0:T(8,128)(2,1)S(1)}, u32[]{:S(2)}, u32[]{:S(2)}) collective-permute-start(bf16[4,128,1024]{2,1,0:T(8,128)(2,1)S(1)} %get-tuple-element.44.refs_2_), channel_id=1, source_target_pairs={{0,4},{4,0},{8,12},{12,8},{16,20},{20,16},{24,28},{28,24},{1,5},{5... | collective-permute-start | bytes 3145736 | tf_op jit(solution)/shard_map/ppermute | solution.py:506
  67.4 11.5 %collective-permute-start.10 = (bf16[192,256]{1,0:T(8,128)(2,1)S(1)}, bf16[192,256]{1,0:T(8,128)(2,1)S(1)}, u32[]{:S(2)}, u32[]{:S(2)}) collective-permute-start(bf16[192,256]{1,0:T(8,128)(2,1)S(1)} %self_attention.3.refs_8_.refs_3_), channel_id=1, source_target_pairs={{0,2},{1,3},{2,0},{3,1},{4,6},{5,7},{6,4},{7,5},{8,10},{9,11},{10,... | collective-permute-start | bytes 294920 | tf_op jit(solution)/shard_map/ppermute | solution.py:459
  70.2 9.5 %collective-permute-start.11 = (bf16[192,256]{1,0:T(8,128)(2,1)S(1)}, bf16[192,256]{1,0:T(8,128)(2,1)S(1)}, u32[]{:S(2)}, u32[]{:S(2)}) collective-permute-start(bf16[192,256]{1,0:T(8,128)(2,1)S(1)} %self_attention.3.refs_8_.refs_3_), channel_id=1, source_target_pairs={{0,3},{1,2},{2,1},{3,0},{4,7},{5,6},{6,5},{7,4},{8,11},{9,10},{10,... | collective-permute-start | bytes 294920 | tf_op jit(solution)/shard_map/ppermute | solution.py:459
  70.7 9.0 %collective-permute-start.9 = (bf16[192,256]{1,0:T(8,128)(2,1)S(1)}, bf16[192,256]{1,0:T(8,128)(2,1)S(1)}, u32[]{:S(2)}, u32[]{:S(2)}) collective-permute-start(bf16[192,256]{1,0:T(8,128)(2,1)S(1)} %self_attention.3.refs_8_.refs_3_), channel_id=1, source_target_pairs={{0,1},{1,0},{2,3},{3,2},{4,5},{5,4},{6,7},{7,6},{8,9},{9,8},{10,11... | collective-permute-start | bytes 294920 | tf_op jit(solution)/shard_map/ppermute | solution.py:459
  75.8 17.4 %slice-start = ((s8[8388608]{0:T(1024)(128)(4,1)}), s8[4194304]{0:T(1024)(128)(4,1)S(1)}, s32[]{:S(2)}) async-start(s8[8388608]{0:T(1024)(128)(4,1)} %bitcast.1), calls=%async_computation | async-start | bytes 8388608
  75.8 17.4 %slice-start.1 = ((s8[8388608]{0:T(1024)(128)(4,1)}), s8[4194304]{0:T(1024)(128)(4,1)S(1)}, s32[]{:S(2)}) async-start(s8[8388608]{0:T(1024)(128)(4,1)} %bitcast.1), calls=%async_computation.1 | async-start | bytes 8388608
  75.8 10.0 %collective-permute-start.24 = (bf16[192,256]{1,0:T(8,128)(2,1)S(1)}, bf16[192,256]{1,0:T(8,128)(2,1)S(1)}, u32[]{:S(2)}, u32[]{:S(2)}) collective-permute-start(bf16[192,256]{1,0:T(8,128)(2,1)S(1)} %get-tuple-element.54.refs_1_), channel_id=1, source_target_pairs={{0,1},{1,0},{2,3},{3,2},{4,5},{5,4},{6,7},{7,6},{8,9},{9,8},{10,11... | collective-permute-start | bytes 294920 | tf_op jit(solution)/shard_map/ppermute | solution.py:459
  76.9 9.4 %collective-permute-start.25 = (bf16[192,256]{1,0:T(8,128)(2,1)S(1)}, bf16[192,256]{1,0:T(8,128)(2,1)S(1)}, u32[]{:S(2)}, u32[]{:S(2)}) collective-permute-start(bf16[192,256]{1,0:T(8,128)(2,1)S(1)} %get-tuple-element.54.refs_1_), channel_id=1, source_target_pairs={{0,2},{1,3},{2,0},{3,1},{4,6},{5,7},{6,4},{7,5},{8,10},{9,11},{10,... | collective-permute-start | bytes 294920 | tf_op jit(solution)/shard_map/ppermute | solution.py:459
  78.9 14.2 %collective-permute-start.26 = (bf16[192,256]{1,0:T(8,128)(2,1)S(1)}, bf16[192,256]{1,0:T(8,128)(2,1)S(1)}, u32[]{:S(2)}, u32[]{:S(2)}) collective-permute-start(bf16[192,256]{1,0:T(8,128)(2,1)S(1)} %get-tuple-element.54.refs_1_), channel_id=1, source_target_pairs={{0,3},{1,2},{2,1},{3,0},{4,7},{5,6},{6,5},{7,4},{8,11},{9,10},{10,... | collective-permute-start | bytes 294920 | tf_op jit(solution)/shard_map/ppermute | solution.py:459
  82.8 16.8 %collective-permute-start.21 = (bf16[192,256]{1,0:T(8,128)(2,1)S(1)}, bf16[192,256]{1,0:T(8,128)(2,1)S(1)}, u32[]{:S(2)}, u32[]{:S(2)}) collective-permute-start(bf16[192,256]{1,0:T(8,128)(2,1)S(1)} %get-tuple-element.49.refs_1_), channel_id=1, source_target_pairs={{0,1},{1,0},{2,3},{3,2},{4,5},{5,4},{6,7},{7,6},{8,9},{9,8},{10,11... | collective-permute-start | bytes 294920 | tf_op jit(solution)/shard_map/ppermute | solution.py:459
  84.6 15.0 %collective-permute-start.22 = (bf16[192,256]{1,0:T(8,128)(2,1)S(1)}, bf16[192,256]{1,0:T(8,128)(2,1)S(1)}, u32[]{:S(2)}, u32[]{:S(2)}) collective-permute-start(bf16[192,256]{1,0:T(8,128)(2,1)S(1)} %get-tuple-element.49.refs_1_), channel_id=1, source_target_pairs={{0,2},{1,3},{2,0},{3,1},{4,6},{5,7},{6,4},{7,5},{8,10},{9,11},{10,... | collective-permute-start | bytes 294920 | tf_op jit(solution)/shard_map/ppermute | solution.py:459
  85.8 13.8 %collective-permute-start.23 = (bf16[192,256]{1,0:T(8,128)(2,1)S(1)}, bf16[192,256]{1,0:T(8,128)(2,1)S(1)}, u32[]{:S(2)}, u32[]{:S(2)}) collective-permute-start(bf16[192,256]{1,0:T(8,128)(2,1)S(1)} %get-tuple-element.49.refs_1_), channel_id=1, source_target_pairs={{0,3},{1,2},{2,1},{3,0},{4,7},{5,6},{6,5},{7,4},{8,11},{9,10},{10,... | collective-permute-start | bytes 294920 | tf_op jit(solution)/shard_map/ppermute | solution.py:459

commit v4 on v3

--- a/solution.py
+++ b/solution.py
@@ -98,7 +98,7 @@
         in_specs=whole(6),
         out_specs=tuple(whole(4)),
         compiler_params=params(4),
-        cost_estimate=cost(2 * rows * model * 3 * width, 2 * 3 * model * width),
+        cost_estimate=cost(8e10, 0),
         name="project",
     )(*pieces, w_qkv, part)
 
@@ -167,9 +167,7 @@
 
 
 def order_kernel(sources, ids, order_ref, *refs):
-    passed_in, k_ref, vt_ref, cache_ref, passed_ref, v_ref, sem = refs[-7:]
-    passing = pltpu.make_async_copy(passed_in, passed_ref, sem)
-    passing.start()
+    k_ref, vt_ref, cache_ref, v_ref = refs[-4:]
     for ref, (relative, numbers) in zip(refs, sources):
         rows = ref.shape[2] // 2
         for piece, number in enumerate(numbers):
@@ -183,10 +181,9 @@
     at = rows_at(ids[0], cache_ref.shape[1])
     cache_ref[0] = k_ref[at, :]
     cache_ref[1] = v_ref[at, :]
-    passing.wait()
-
-
-def order(block_order, chunks, sources, passed):
+
+
+def order(block_order, chunks, sources):
     rows, width = chunks[0].shape[2:]
     total = rows * sum(c.shape[0] for c in chunks)
     return pl.pallas_call(
@@ -195,15 +192,14 @@
             jax.ShapeDtypeStruct((total, width), jnp.bfloat16),
             jax.ShapeDtypeStruct((width // 128, 128 + ONES, total), jnp.bfloat16),
             jax.ShapeDtypeStruct((2, rows, width), jnp.bfloat16),
-            jax.ShapeDtypeStruct(passed.shape, jnp.bfloat16),
         ),
-        in_specs=smem(1) + whole(len(chunks)) + anywhere(1),
-        out_specs=tuple(whole(4)),
-        scratch_shapes=[pltpu.VMEM((total, width), jnp.bfloat16), pltpu.SemaphoreType.DMA],
+        in_specs=smem(1) + whole(len(chunks)),
+        out_specs=tuple(whole(3)),
+        scratch_shapes=[pltpu.VMEM((total, width), jnp.bfloat16)],
         compiler_params=params(4 + total * width * 2 // MIB),
         cost_estimate=cost(0, 5 * 2 * total * width),
         name="order",
-    )(block_order, *chunks, passed)
+    )(block_order, *chunks)
 
 
 def prepare_kernel(sources, ids, *refs):
@@ -479,10 +475,11 @@
         ("", "", "rows"), 2,
     )
     x, queries, kv, part = project([tokens] + rows[1:], w_qkv, part)
+    enc = bundle([over_chips(enc_kv, cycle)], (queries,)) if paired else [queries]
     w_cq, w_co, w_up, w_down, w_next = fetch(
         (w_cq, w_co, w_up, w_down, w_next),
         ((w_cq.shape[0], width), w_co.shape, w_up.shape, w_down.shape, w_next.shape),
-        ("columns", "", "", "", ""), 34, (queries,),
+        ("columns", "", "", "", ""), 34, enc,
     )
     near = tuple(range(0, cycle, 2))
     if paired:
@@ -494,7 +491,7 @@
     else:
         kvs = [lax.all_gather(kv, "blk", axis=0)]
         sources = [(False, tuple(range(cycle)))]
-    keys, values, cache, enc_kv = order(block_order, kvs, sources, enc_kv)
+    keys, values, cache = order(block_order, kvs, sources)
     attended = []
     for turn in range(2):
         mine = self_attention(
@@ -502,7 +499,7 @@
         )
         attended.append(over_head(mine, group))
     if paired:
-        own = bundle([parts, over_chips(enc_kv, cycle)], attended[1][:1] + attended[0][1:])
+        own = bundle([parts], attended[1][:1] + attended[0][1:]) + enc
         parts, enc = zip(own, [lax.ppermute(y, "blk", xor(cycle, 1)) for y in own])
     else:
         enc = [lax.all_gather(enc_kv, "blk", axis=0)]

time: 107 us -> 104 us (0.972)
  the two profiles are of different devices: /device:TPU:8 before, /device:TPU:0 now
where the time goes in v4:
time: 104 us; the launch traced here: 105 us
  starting transfers between devices  46.1 us (44%)
  Pallas kernels  38.7 us (37%)
  waiting for transfers between devices  14.8 us (14%)
  local copies, waits for them, and re-layouts  3.98 us (4%)
  between operations  1.06 us (1%)
    ppermute x18, starting transfers between devices, over_head(): return [x] + [lax.ppermute(x, 'head', xor(size, j)) for j in range(1, size)]  38 us
    ppermute x18, waiting for transfers between devices, over_head(): return [x] + [lax.ppermute(x, 'head', xor(size, j)) for j in range(1, size)]  13.6 us
    pallas_call x2, Pallas kernels, mlp(): pl.pallas_call(placed(functools.partial(mlp_kernel, turn)), out_shape=(ja...  12.8 us
    pallas_call x2, Pallas kernels, fetch(): pl.pallas_call(placed(skipping(functools.partial(fetch_kernel, cuts), 1 +...  9.65 us
    ppermute x6, starting transfers between devices, over_chips(): lax.ppermute(x, 'blk', xor(size, s))  7.8 us
    pallas_call x2, Pallas kernels, cross_attention(): pl.pallas_call(placed(functools.partial(cross_kernel, turn)), out_shape=(...  7.01 us
    pallas_call x2, Pallas kernels, self_attention(): pl.pallas_call(placed(skipping(functools.partial(self_kernel, turn), 6, l...  4.59 us
    unnamed x24, local copies, waits for them, and re-layouts  3.98 us
  transfers between devices with their start and end apart: 27, of which 5 were waited for; matrix products, arithmetic and copies ran while one was open for 0% of the time, Pallas kernels for 31%

profile of v4, /device:TPU:0, one launch (start us, length us, event | category | flops | bytes accessed | tf_op | source)
XLA Modules:
  0.0 104.6 jit_solution(6245400488163253186)
XLA Ops:
  0.6 3.1 %collective-permute-start = (bf16[96,1024]{1,0:T(8,128)(2,1)}, bf16[96,1024]{1,0:T(8,128)(2,1)S(1)}, u32[]{:S(2)}, u32[]{:S(2)}) collective-permute-start(bf16[96,1024]{1,0:T(8,128)(2,1)} %refs_0_.10), channel_id=1, source_target_pairs={{0,1},{1,0},{2,3},{3,2},{4,5},{5,4},{6,7},{7,6},{8,9},{9,8},{10,11... | collective-permute-start | bytes 589832 | tf_op jit(solution)/shard_map/ppermute | solution.py:455
  3.7 2.6 %collective-permute-start.1 = (bf16[96,1024]{1,0:T(8,128)(2,1)}, bf16[96,1024]{1,0:T(8,128)(2,1)S(1)}, u32[]{:S(2)}, u32[]{:S(2)}) collective-permute-start(bf16[96,1024]{1,0:T(8,128)(2,1)} %refs_0_.10), channel_id=1, source_target_pairs={{0,2},{1,3},{2,0},{3,1},{4,6},{5,7},{6,4},{7,5},{8,10},{9,11},{10,... | collective-permute-start | bytes 589832 | tf_op jit(solution)/shard_map/ppermute | solution.py:455
  6.3 1.7 %collective-permute-start.6 = (bf16[2,256,256]{2,1,0:T(8,128)(2,1)}, bf16[2,256,256]{2,1,0:T(8,128)(2,1)S(1)}, u32[]{:S(2)}, u32[]{:S(2)}) collective-permute-start(bf16[2,256,256]{2,1,0:T(8,128)(2,1)} %refs_0_.11), channel_id=1, source_target_pairs={{0,8},{4,12},{8,0},{12,4},{16,24},{20,28},{24,16},{28,20},{1,9},{5... | collective-permute-start | bytes 786440 | tf_op jit(solution)/shard_map/ppermute | solution.py:459
  8.0 1.5 %collective-permute-start.7 = (bf16[2,256,256]{2,1,0:T(8,128)(2,1)}, bf16[2,256,256]{2,1,0:T(8,128)(2,1)S(1)}, u32[]{:S(2)}, u32[]{:S(2)}) collective-permute-start(bf16[2,256,256]{2,1,0:T(8,128)(2,1)} %refs_0_.11), channel_id=1, source_target_pairs={{0,16},{4,20},{8,24},{12,28},{16,0},{20,4},{24,8},{28,12},{1,17},{... | collective-permute-start | bytes 786440 | tf_op jit(solution)/shard_map/ppermute | solution.py:459
  9.5 1.4 %copy-done.3 = bf16[3,1024,256]{2,1,0:T(8,128)(2,1)S(1)} copy-done((bf16[3,1024,256]{2,1,0:T(8,128)(2,1)S(1)}, bf16[3,1024,256]{2,1,0:T(8,128)(2,1)}, u32[]{:S(2)}) %copy-start.3) | copy-done | bytes 1572888
  11.0 1.0 copy-done.4
  12.0 0.9 copy-done.6
  12.9 0.4 fetch.2
  13.3 0.6 copy-done.5
  13.9 1.0 collective-permute-start.8
  14.9 6.2 %collective-permute-done.1.refs_2_ = bf16[96,1024]{1,0:T(8,128)(2,1)S(1)} collective-permute-done((bf16[96,1024]{1,0:T(8,128)(2,1)}, bf16[96,1024]{1,0:T(8,128)(2,1)S(1)}, u32[]{:S(2)}, u32[]{:S(2)}) %collective-permute-start.1) | collective-permute-done | bytes 196640 | tf_op jit(solution)/shard_map/ppermute | solution.py:455
  21.1 0.8 project.1
  21.9 1.6 %collective-permute-start.3 = (bf16[2,384,256]{2,1,0:T(8,128)(2,1)S(1)}, bf16[2,384,256]{2,1,0:T(8,128)(2,1)S(1)}, u32[]{:S(2)}, u32[]{:S(2)}) collective-permute-start(bf16[2,384,256]{2,1,0:T(8,128)(2,1)S(1)} %get-tuple-element.33.refs_0_), channel_id=1, source_target_pairs={{0,8},{4,12},{8,0},{12,4},{16,24},{20,28},{24,16},{28,20},{1,9},{5... | collective-permute-start | bytes 1179656 | tf_op jit(solution)/shard_map/ppermute | solution.py:459
  23.5 1.5 %collective-permute-start.4 = (bf16[2,384,256]{2,1,0:T(8,128)(2,1)S(1)}, bf16[2,384,256]{2,1,0:T(8,128)(2,1)S(1)}, u32[]{:S(2)}, u32[]{:S(2)}) collective-permute-start(bf16[2,384,256]{2,1,0:T(8,128)(2,1)S(1)} %get-tuple-element.33.refs_0_), channel_id=1, source_target_pairs={{0,16},{4,20},{8,24},{12,28},{16,0},{20,4},{24,8},{28,12},{1,17},{... | collective-permute-start | bytes 1179656 | tf_op jit(solution)/shard_map/ppermute | solution.py:459
  25.0 0.5 collective-permute-start.5
  25.5 4.4 %collective-permute-start.10 = (bf16[128,1024]{1,0:T(8,128)(2,1)S(1)}, bf16[128,1024]{1,0:T(8,128)(2,1)S(1)}, u32[]{:S(2)}, u32[]{:S(2)}) collective-permute-start(bf16[128,1024]{1,0:T(8,128)(2,1)S(1)} %get-tuple-element.35.refs_0_), channel_id=1, source_target_pairs={{0,2},{1,3},{2,0},{3,1},{4,6},{5,7},{6,4},{7,5},{8,10},{9,11},{10,... | collective-permute-start | bytes 786440 | tf_op jit(solution)/shard_map/ppermute | solution.py:455
  29.9 0.1 bundle.3.refs_5_.refs_0_
  30.0 9.3 %fetch.3 = (bf16[1024,256]{1,0:T(8,128)(2,1)S(1)}, bf16[1024,1024]{1,0:T(8,128)(2,1)S(1)}, bf16[1024,4096]{1,0:T(8,128)(2,1)S(1)}, bf16[4096,1024]{1,0:T(8,128)(2,1)}, bf16[3,1024,256]{2,1,0:T(8,128)(2,1)S(1)}) custom-call(bf16[1024,1024]{1,0:T(8,128)(2,1)S(1)} %copy-done, bf16[1024,1024]{1,0:T(8,128)(2,1)S(1)} %copy-done.1, bf16[1024,4096]{1,0:T(8,128)(2,1)} %refs_2_.5, ...), custom_call_target="tpu_custom_call" | custom-call | bytes 1048576 | tf_op jit(solution)/shard_map/fetch/pallas_call | solution.py:125
  39.3 0.6 collective-permute-done.10.refs_6_.refs_2_
  39.9 0.2 collective-permute-done.9.refs_5_.refs_1_
  40.1 0.1 bundle.4.refs_1_
  40.2 0.1 collective-permute-start.11
  40.3 2.1 %collective-permute-start.16 = (bf16[128,1024]{1,0:T(8,128)(2,1)S(1)}, bf16[128,1024]{1,0:T(8,128)(2,1)S(1)}, u32[]{:S(2)}, u32[]{:S(2)}) collective-permute-start(bf16[128,1024]{1,0:T(8,128)(2,1)S(1)} %get-tuple-element.35.refs_0_), channel_id=1, source_target_pairs={{0,3},{1,2},{2,1},{3,0},{4,7},{5,6},{6,5},{7,4},{8,11},{9,10},{10,... | collective-permute-start | bytes 786440 | tf_op jit(solution)/shard_map/ppermute | solution.py:455
  42.4 0.2 collective-permute-start.15
  42.5 1.2 %collective-permute-done.11.refs_2_ = bf16[4,2,384,256]{3,2,1,0:T(8,128)(2,1)S(1)} collective-permute-done((bf16[4,2,384,256]{3,2,1,0:T(8,128)(2,1)S(1)}, bf16[4,2,384,256]{3,2,1,0:T(8,128)(2,1)S(1)}, u32[]{:S(2)}, u32[]{:S(2)}) %collective-permute-start.11) | collective-permute-done | bytes 1572896 | tf_op jit(solution)/shard_map/ppermute | solution.py:489
  43.7 2.6 %order.1 = (bf16[3072,256]{1,0:T(8,128)(2,1)S(1)}, bf16[2,144,3072]{2,1,0:T(8,128)(2,1)S(1)}, bf16[2,384,256]{2,1,0:T(8,128)(2,1)}) custom-call(s32[16]{0:T(128)S(1)} %copy-done.7, bf16[4,2,384,256]{3,2,1,0:T(8,128)(2,1)S(1)} %bundle.4.refs_1_, bf16[4,2,384,256]{3,2,1,0:T(8,128)(2,1)S(1)} %collective-permute-done.11.refs_2_), custom_call_target="tpu_custom_call" | custom-call | bytes 393216 | tf_op jit(solution)/shard_map/order/pallas_call | solution.py:189
  46.3 2.8 %self_attention.2.refs_5_.refs_3_ = bf16[192,256]{1,0:T(8,128)(2,1)S(1)} custom-call(s32[16]{0:T(128)S(1)} %copy-done.7, s32[9]{0:T(128)S(1)} %copy-done.8, bf16[384,256]{1,0:T(8,128)(2,1)S(1)} %get-tuple-element.32.refs_4_.refs_2_, bf16[3072,256]{1,0:T(8,128)(2,1)S(1)} %get-tuple-element.36.refs_3_, bf16[2,144,3072]{2,1,0:T(8,128)(2,1)S(1)} %get-tuple-element.37.refs_4_), custom_call_target="tpu_custom_call" | custom-call | flops 10000000000 | tf_op jit(solution)/shard_map/self_attention/pallas_call | solution.py:318
  49.1 4.7 %collective-permute-start.17 = (bf16[192,256]{1,0:T(8,128)(2,1)S(1)}, bf16[192,256]{1,0:T(8,128)(2,1)S(1)}, u32[]{:S(2)}, u32[]{:S(2)}) collective-permute-start(bf16[192,256]{1,0:T(8,128)(2,1)S(1)} %self_attention.2.refs_5_.refs_3_), channel_id=1, source_target_pairs={{0,1},{1,0},{2,3},{3,2},{4,5},{5,4},{6,7},{7,6},{8,9},{9,8},{10,11... | collective-permute-start | bytes 294920 | tf_op jit(solution)/shard_map/ppermute | solution.py:455
  53.8 1.1 %collective-permute-start.18 = (bf16[192,256]{1,0:T(8,128)(2,1)S(1)}, bf16[192,256]{1,0:T(8,128)(2,1)S(1)}, u32[]{:S(2)}, u32[]{:S(2)}) collective-permute-start(bf16[192,256]{1,0:T(8,128)(2,1)S(1)} %self_attention.2.refs_5_.refs_3_), channel_id=1, source_target_pairs={{0,2},{1,3},{2,0},{3,1},{4,6},{5,7},{6,4},{7,5},{8,10},{9,11},{10,... | collective-permute-start | bytes 294920 | tf_op jit(solution)/shard_map/ppermute | solution.py:455
  54.9 1.4 %collective-permute-start.19 = (bf16[192,256]{1,0:T(8,128)(2,1)S(1)}, bf16[192,256]{1,0:T(8,128)(2,1)S(1)}, u32[]{:S(2)}, u32[]{:S(2)}) collective-permute-start(bf16[192,256]{1,0:T(8,128)(2,1)S(1)} %self_attention.2.refs_5_.refs_3_), channel_id=1, source_target_pairs={{0,3},{1,2},{2,1},{3,0},{4,7},{5,6},{6,5},{7,4},{8,11},{9,10},{10,... | collective-permute-start | bytes 294920 | tf_op jit(solution)/shard_map/ppermute | solution.py:455
  56.3 1.8 %self_attention.3.refs_4_.refs_3_ = bf16[192,256]{1,0:T(8,128)(2,1)S(1)} custom-call(s32[16]{0:T(128)S(1)} %copy-done.7, s32[9]{0:T(128)S(1)} %copy-done.8, bf16[384,256]{1,0:T(8,128)(2,1)S(1)} %get-tuple-element.32.refs_4_.refs_2_, bf16[3072,256]{1,0:T(8,128)(2,1)S(1)} %get-tuple-element.36.refs_3_, bf16[2,144,3072]{2,1,0:T(8,128)(2,1)S(1)} %get-tuple-element.37.refs_4_, ...), custom_call_target="tpu_custom_call" | custom-call | flops 10000000000 | tf_op jit(solution)/shard_map/self_attention/pallas_call | solution.py:318
  58.1 6.5 %collective-permute-done.18.refs_6_.refs_5_ = bf16[192,256]{1,0:T(8,128)(2,1)S(1)} collective-permute-done((bf16[192,256]{1,0:T(8,128)(2,1)S(1)}, bf16[192,256]{1,0:T(8,128)(2,1)S(1)}, u32[]{:S(2)}, u32[]{:S(2)}) %collective-permute-start.18) | collective-permute-done | bytes 98336 | tf_op jit(solution)/shard_map/ppermute | solution.py:455
  64.6 0.1 bundle.5.refs_2_
  64.7 0.1 collective-permute-start.20
  64.7 2.6 %collective-permute-start.12 = (bf16[192,256]{1,0:T(8,128)(2,1)S(1)}, bf16[192,256]{1,0:T(8,128)(2,1)S(1)}, u32[]{:S(2)}, u32[]{:S(2)}) collective-permute-start(bf16[192,256]{1,0:T(8,128)(2,1)S(1)} %self_attention.3.refs_4_.refs_3_), channel_id=1, source_target_pairs={{0,1},{1,0},{2,3},{3,2},{4,5},{5,4},{6,7},{7,6},{8,9},{9,8},{10,11... | collective-permute-start | bytes 294920 | tf_op jit(solution)/shard_map/ppermute | solution.py:455
  67.4 1.0 %collective-permute-start.13 = (bf16[192,256]{1,0:T(8,128)(2,1)S(1)}, bf16[192,256]{1,0:T(8,128)(2,1)S(1)}, u32[]{:S(2)}, u32[]{:S(2)}) collective-permute-start(bf16[192,256]{1,0:T(8,128)(2,1)S(1)} %self_attention.3.refs_4_.refs_3_), channel_id=1, source_target_pairs={{0,2},{1,3},{2,0},{3,1},{4,6},{5,7},{6,4},{7,5},{8,10},{9,11},{10,... | collective-permute-start | bytes 294920 | tf_op jit(solution)/shard_map/ppermute | solution.py:455
  68.4 1.4 %collective-permute-start.14 = (bf16[192,256]{1,0:T(8,128)(2,1)S(1)}, bf16[192,256]{1,0:T(8,128)(2,1)S(1)}, u32[]{:S(2)}, u32[]{:S(2)}) collective-permute-start(bf16[192,256]{1,0:T(8,128)(2,1)S(1)} %self_attention.3.refs_4_.refs_3_), channel_id=1, source_target_pairs={{0,3},{1,2},{2,1},{3,0},{4,7},{5,6},{6,5},{7,4},{8,11},{9,10},{10,... | collective-permute-start | bytes 294920 | tf_op jit(solution)/shard_map/ppermute | solution.py:455
  69.8 1.0 prepare.1
  70.8 2.9 %cross_attention.3 = (f32[192,1024]{1,0:T(8,128)S(1)}, bf16[192,256]{1,0:T(8,128)(2,1)S(1)}) custom-call(s32[16]{0:T(128)S(1)} %copy-done.7, s32[9]{0:T(128)S(1)} %copy-done.8, s32[9]{0:T(128)S(1)} %copy-done.9, bf16[192,256]{1,0:T(8,128)(2,1)S(1)} %self_attention.2.refs_5_.refs_3_, bf16[192,256]{1,0:T(8,128)(2,1)S(1)} %collective-permute-done.17.refs_5_.refs_4_, ...), custom_call_target="tpu_custom_call" | custom-call | flops 10000000000 | tf_op jit(solution)/shard_map/cross_attention/pallas_call | solution.py:366
  73.8 1.1 %collective-permute-start.24 = (bf16[192,256]{1,0:T(8,128)(2,1)S(1)}, bf16[192,256]{1,0:T(8,128)(2,1)S(1)}, u32[]{:S(2)}, u32[]{:S(2)}) collective-permute-start(bf16[192,256]{1,0:T(8,128)(2,1)S(1)} %get-tuple-element.48.refs_1_), channel_id=1, source_target_pairs={{0,1},{1,0},{2,3},{3,2},{4,5},{5,4},{6,7},{7,6},{8,9},{9,8},{10,11... | collective-permute-start | bytes 294920 | tf_op jit(solution)/shard_map/ppermute | solution.py:455
  74.9 1.9 %collective-permute-start.25 = (bf16[192,256]{1,0:T(8,128)(2,1)S(1)}, bf16[192,256]{1,0:T(8,128)(2,1)S(1)}, u32[]{:S(2)}, u32[]{:S(2)}) collective-permute-start(bf16[192,256]{1,0:T(8,128)(2,1)S(1)} %get-tuple-element.48.refs_1_), channel_id=1, source_target_pairs={{0,2},{1,3},{2,0},{3,1},{4,6},{5,7},{6,4},{7,5},{8,10},{9,11},{10,... | collective-permute-start | bytes 294920 | tf_op jit(solution)/shard_map/ppermute | solution.py:455
  76.9 1.4 %collective-permute-start.26 = (bf16[192,256]{1,0:T(8,128)(2,1)S(1)}, bf16[192,256]{1,0:T(8,128)(2,1)S(1)}, u32[]{:S(2)}, u32[]{:S(2)}) collective-permute-start(bf16[192,256]{1,0:T(8,128)(2,1)S(1)} %get-tuple-element.48.refs_1_), channel_id=1, source_target_pairs={{0,3},{1,2},{2,1},{3,0},{4,7},{5,6},{6,5},{7,4},{8,11},{9,10},{10,... | collective-permute-start | bytes 294920 | tf_op jit(solution)/shard_map/ppermute | solution.py:455
  78.2 4.1 %cross_attention.2 = (f32[192,1024]{1,0:T(8,128)S(1)}, bf16[192,256]{1,0:T(8,128)(2,1)S(1)}) custom-call(s32[16]{0:T(128)S(1)} %copy-done.7, s32[9]{0:T(128)S(1)} %copy-done.8, s32[9]{0:T(128)S(1)} %copy-done.9, bf16[192,256]{1,0:T(8,128)(2,1)S(1)} %self_attention.3.refs_4_.refs_3_, bf16[192,256]{1,0:T(8,128)(2,1)S(1)} %collective-permute-done.12.refs_4_, ...), custom_call_target="tpu_custom_call" | custom-call | flops 10000000000 | tf_op jit(solution)/shard_map/cross_attention/pallas_call | solution.py:366
  82.3 6.8 %collective-permute-start.21 = (bf16[192,256]{1,0:T(8,128)(2,1)S(1)}, bf16[192,256]{1,0:T(8,128)(2,1)S(1)}, u32[]{:S(2)}, u32[]{:S(2)}) collective-permute-start(bf16[192,256]{1,0:T(8,128)(2,1)S(1)} %get-tuple-element.43.refs_1_), channel_id=1, source_target_pairs={{0,1},{1,0},{2,3},{3,2},{4,5},{5,4},{6,7},{7,6},{8,9},{9,8},{10,11... | collective-permute-start | bytes 294920 | tf_op jit(solution)/shard_map/ppermute | solution.py:455
  89.2 0.8 collective-permute-start.22
  90.0 1.6 %collective-permute-start.23 = (bf16[192,256]{1,0:T(8,128)(2,1)S(1)}, bf16[192,256]{1,0:T(8,128)(2,1)S(1)}, u32[]{:S(2)}, u32[]{:S(2)}) collective-permute-start(bf16[192,256]{1,0:T(8,128)(2,1)S(1)} %get-tuple-element.43.refs_1_), channel_id=1, source_target_pairs={{0,3},{1,2},{2,1},{3,0},{4,7},{5,6},{6,5},{7,4},{8,11},{9,10},{10,... | collective-permute-start | bytes 294920 | tf_op jit(solution)/shard_map/ppermute | solution.py:455
  91.7 6.4 %mlp.2 = (f32[96,1024]{1,0:T(8,128)}, f32[3,384,256]{2,1,0:T(8,128)}) custom-call(s32[16]{0:T(128)S(1)} %copy-done.7, bf16[192,256]{1,0:T(8,128)(2,1)S(1)} %get-tuple-element.48.refs_1_, bf16[192,256]{1,0:T(8,128)(2,1)S(1)} %collective-permute-done.24.refs_2_, bf16[192,256]{1,0:T(8,128)(2,1)S(1)} %collective-permute-done.25.refs_3_, ...), custom_call_target="tpu_custom_call" | custom-call | flops 300000000 | tf_op jit(solution)/shard_map/mlp/pallas_call | solution.py:433
  98.1 6.4 %mlp.3 = (f32[96,1024]{1,0:T(8,128)}, f32[3,384,256]{2,1,0:T(8,128)}) custom-call(s32[16]{0:T(128)S(1)} %copy-done.7, bf16[192,256]{1,0:T(8,128)(2,1)S(1)} %get-tuple-element.43.refs_1_, bf16[192,256]{1,0:T(8,128)(2,1)S(1)} %collective-permute-done.21.refs_2_, ...), custom_call_target="tpu_custom_call", output_to_operand_aliasing={{0}: (10, {}), {1}: (11, {})} | custom-call | flops 300000000 | tf_op jit(solution)/shard_map/mlp/pallas_call | solution.py:433
  (45 shorter events, 0.1 us)
Async XLA Ops:
  0.6 12.7 %collective-permute-start = (bf16[96,1024]{1,0:T(8,128)(2,1)}, bf16[96,1024]{1,0:T(8,128)(2,1)S(1)}, u32[]{:S(2)}, u32[]{:S(2)}) collective-permute-start(bf16[96,1024]{1,0:T(8,128)(2,1)} %refs_0_.10), channel_id=1, source_target_pairs={{0,1},{1,0},{2,3},{3,2},{4,5},{5,4},{6,7},{7,6},{8,9},{9,8},{10,11... | collective-permute-start | bytes 589832 | tf_op jit(solution)/shard_map/ppermute | solution.py:455
  3.7 17.4 %collective-permute-start.1 = (bf16[96,1024]{1,0:T(8,128)(2,1)}, bf16[96,1024]{1,0:T(8,128)(2,1)S(1)}, u32[]{:S(2)}, u32[]{:S(2)}) collective-permute-start(bf16[96,1024]{1,0:T(8,128)(2,1)} %refs_0_.10), channel_id=1, source_target_pairs={{0,2},{1,3},{2,0},{3,1},{4,6},{5,7},{6,4},{7,5},{8,10},{9,11},{10,... | collective-permute-start | bytes 589832 | tf_op jit(solution)/shard_map/ppermute | solution.py:455
  6.3 14.8 %collective-permute-start.2 = (bf16[96,1024]{1,0:T(8,128)(2,1)}, bf16[96,1024]{1,0:T(8,128)(2,1)S(1)}, u32[]{:S(2)}, u32[]{:S(2)}) collective-permute-start(bf16[96,1024]{1,0:T(8,128)(2,1)} %refs_0_.10), channel_id=1, source_target_pairs={{0,3},{1,2},{2,1},{3,0},{4,7},{5,6},{6,5},{7,4},{8,11},{9,10},{10,... | collective-permute-start | bytes 589832 | tf_op jit(solution)/shard_map/ppermute | solution.py:455
  6.3 18.7 %collective-permute-start.6 = (bf16[2,256,256]{2,1,0:T(8,128)(2,1)}, bf16[2,256,256]{2,1,0:T(8,128)(2,1)S(1)}, u32[]{:S(2)}, u32[]{:S(2)}) collective-permute-start(bf16[2,256,256]{2,1,0:T(8,128)(2,1)} %refs_0_.11), channel_id=1, source_target_pairs={{0,8},{4,12},{8,0},{12,4},{16,24},{20,28},{24,16},{28,20},{1,9},{5... | collective-permute-start | bytes 786440 | tf_op jit(solution)/shard_map/ppermute | solution.py:459
  8.0 17.5 %collective-permute-start.7 = (bf16[2,256,256]{2,1,0:T(8,128)(2,1)}, bf16[2,256,256]{2,1,0:T(8,128)(2,1)S(1)}, u32[]{:S(2)}, u32[]{:S(2)}) collective-permute-start(bf16[2,256,256]{2,1,0:T(8,128)(2,1)} %refs_0_.11), channel_id=1, source_target_pairs={{0,16},{4,20},{8,24},{12,28},{16,0},{20,4},{24,8},{28,12},{1,17},{... | collective-permute-start | bytes 786440 | tf_op jit(solution)/shard_map/ppermute | solution.py:459
  9.5 1.4 %copy-start.3 = (bf16[3,1024,256]{2,1,0:T(8,128)(2,1)S(1)}, bf16[3,1024,256]{2,1,0:T(8,128)(2,1)}, u32[]{:S(2)}) copy-start(bf16[3,1024,256]{2,1,0:T(8,128)(2,1)} %refs_1_.6) | copy-start | bytes 4718596
  11.0 1.0 copy-start.4
  12.0 0.9 copy-start.6
  12.9 0.9 copy-start.5
  13.9 16.0 %collective-permute-start.8 = (bf16[2,256,256]{2,1,0:T(8,128)(2,1)S(1)}, bf16[2,256,256]{2,1,0:T(8,128)(2,1)S(1)}, u32[]{:S(2)}, u32[]{:S(2)}) collective-permute-start(bf16[2,256,256]{2,1,0:T(8,128)(2,1)S(1)} %copy-done.5), channel_id=1, source_target_pairs={{0,24},{4,28},{8,16},{12,20},{16,8},{20,12},{24,0},{28,4},{1,25},{... | collective-permute-start | bytes 786440 | tf_op jit(solution)/shard_map/ppermute | solution.py:459
  21.1 8.9 %copy-start.1 = (bf16[1024,1024]{1,0:T(8,128)(2,1)S(1)}, bf16[1024,1024]{1,0:T(8,128)(2,1)}, u32[]{:S(2)}) copy-start(bf16[1024,1024]{1,0:T(8,128)(2,1)} %refs_1_.7) | copy-start | bytes 6291460
  21.1 8.9 %copy-start.2 = (bf16[3,1024,256]{2,1,0:T(8,128)(2,1)S(1)}, bf16[3,1024,256]{2,1,0:T(8,128)(2,1)}, u32[]{:S(2)}) copy-start(bf16[3,1024,256]{2,1,0:T(8,128)(2,1)} %refs_4_.1) | copy-start | bytes 4718596
  21.9 8.0 %copy-start = (bf16[1024,1024]{1,0:T(8,128)(2,1)S(1)}, bf16[1024,1024]{1,0:T(8,128)(2,1)}, u32[]{:S(2)}) copy-start(bf16[1024,1024]{1,0:T(8,128)(2,1)} %refs_0_.12) | copy-start | bytes 6291460
  21.9 18.2 %collective-permute-start.3 = (bf16[2,384,256]{2,1,0:T(8,128)(2,1)S(1)}, bf16[2,384,256]{2,1,0:T(8,128)(2,1)S(1)}, u32[]{:S(2)}, u32[]{:S(2)}) collective-permute-start(bf16[2,384,256]{2,1,0:T(8,128)(2,1)S(1)} %get-tuple-element.33.refs_0_), channel_id=1, source_target_pairs={{0,8},{4,12},{8,0},{12,4},{16,24},{20,28},{24,16},{28,20},{1,9},{5... | collective-permute-start | bytes 1179656 | tf_op jit(solution)/shard_map/ppermute | solution.py:459
  23.5 16.6 %collective-permute-start.4 = (bf16[2,384,256]{2,1,0:T(8,128)(2,1)S(1)}, bf16[2,384,256]{2,1,0:T(8,128)(2,1)S(1)}, u32[]{:S(2)}, u32[]{:S(2)}) collective-permute-start(bf16[2,384,256]{2,1,0:T(8,128)(2,1)S(1)} %get-tuple-element.33.refs_0_), channel_id=1, source_target_pairs={{0,16},{4,20},{8,24},{12,28},{16,0},{20,4},{24,8},{28,12},{1,17},{... | collective-permute-start | bytes 1179656 | tf_op jit(solution)/shard_map/ppermute | solution.py:459
  25.0 15.1 %collective-permute-start.5 = (bf16[2,384,256]{2,1,0:T(8,128)(2,1)S(1)}, bf16[2,384,256]{2,1,0:T(8,128)(2,1)S(1)}, u32[]{:S(2)}, u32[]{:S(2)}) collective-permute-start(bf16[2,384,256]{2,1,0:T(8,128)(2,1)S(1)} %get-tuple-element.33.refs_0_), channel_id=1, source_target_pairs={{0,24},{4,28},{8,16},{12,20},{16,8},{20,12},{24,0},{28,4},{1,25},{... | collective-permute-start | bytes 1179656 | tf_op jit(solution)/shard_map/ppermute | solution.py:459
  25.5 14.4 %collective-permute-start.10 = (bf16[128,1024]{1,0:T(8,128)(2,1)S(1)}, bf16[128,1024]{1,0:T(8,128)(2,1)S(1)}, u32[]{:S(2)}, u32[]{:S(2)}) collective-permute-start(bf16[128,1024]{1,0:T(8,128)(2,1)S(1)} %get-tuple-element.35.refs_0_), channel_id=1, source_target_pairs={{0,2},{1,3},{2,0},{3,1},{4,6},{5,7},{6,4},{7,5},{8,10},{9,11},{10,... | collective-permute-start | bytes 786440 | tf_op jit(solution)/shard_map/ppermute | solution.py:455
  29.9 10.2 %collective-permute-start.9 = (bf16[128,1024]{1,0:T(8,128)(2,1)S(1)}, bf16[128,1024]{1,0:T(8,128)(2,1)S(1)}, u32[]{:S(2)}, u32[]{:S(2)}) collective-permute-start(bf16[128,1024]{1,0:T(8,128)(2,1)S(1)} %get-tuple-element.35.refs_0_), channel_id=1, source_target_pairs={{0,1},{1,0},{2,3},{3,2},{4,5},{5,4},{6,7},{7,6},{8,9},{9,8},{10,11... | collective-permute-start | bytes 786440 | tf_op jit(solution)/shard_map/ppermute | solution.py:455
  40.1 3.6 %copy-start.7 = (s32[16]{0:T(128)S(1)}, s32[16]{0:T(128)}, u32[]{:S(2)}) copy-start(s32[16]{0:T(128)} %refs_0_.19) | copy-start | bytes 196
  40.2 6.1 %copy-start.8 = (s32[9]{0:T(128)S(1)}, s32[9]{0:T(128)}, u32[]{:S(2)}) copy-start(s32[9]{0:T(128)} %refs_1_.11) | copy-start | bytes 112
  40.2 3.5 %collective-permute-start.11 = (bf16[4,2,384,256]{3,2,1,0:T(8,128)(2,1)S(1)}, bf16[4,2,384,256]{3,2,1,0:T(8,128)(2,1)S(1)}, u32[]{:S(2)}, u32[]{:S(2)}) collective-permute-start(bf16[4,2,384,256]{3,2,1,0:T(8,128)(2,1)S(1)} %bundle.4.refs_1_), channel_id=1, source_target_pairs={{0,4},{4,0},{8,12},{12,8},{16,20},{20,16},{24,28},{28,24},{1,5},{5... | collective-permute-start | bytes 4718600 | tf_op jit(solution)/shard_map/ppermute | solution.py:489
  40.3 17.7 %collective-permute-start.16 = (bf16[128,1024]{1,0:T(8,128)(2,1)S(1)}, bf16[128,1024]{1,0:T(8,128)(2,1)S(1)}, u32[]{:S(2)}, u32[]{:S(2)}) collective-permute-start(bf16[128,1024]{1,0:T(8,128)(2,1)S(1)} %get-tuple-element.35.refs_0_), channel_id=1, source_target_pairs={{0,3},{1,2},{2,1},{3,0},{4,7},{5,6},{6,5},{7,4},{8,11},{9,10},{10,... | collective-permute-start | bytes 786440 | tf_op jit(solution)/shard_map/ppermute | solution.py:455
  42.4 27.4 %collective-permute-start.15 = (bf16[4,2,256,256]{3,2,1,0:T(8,128)(2,1)S(1)}, bf16[4,2,256,256]{3,2,1,0:T(8,128)(2,1)S(1)}, u32[]{:S(2)}, u32[]{:S(2)}) collective-permute-start(bf16[4,2,256,256]{3,2,1,0:T(8,128)(2,1)S(1)} %bundle.3.refs_5_.refs_0_), channel_id=1, source_target_pairs={{0,4},{4,0},{8,12},{12,8},{16,20},{20,16},{24,28},{28,24},{1,5},{5... | collective-permute-start | bytes 3145736 | tf_op jit(solution)/shard_map/ppermute | solution.py:503
  49.1 8.9 %collective-permute-start.17 = (bf16[192,256]{1,0:T(8,128)(2,1)S(1)}, bf16[192,256]{1,0:T(8,128)(2,1)S(1)}, u32[]{:S(2)}, u32[]{:S(2)}) collective-permute-start(bf16[192,256]{1,0:T(8,128)(2,1)S(1)} %self_attention.2.refs_5_.refs_3_), channel_id=1, source_target_pairs={{0,1},{1,0},{2,3},{3,2},{4,5},{5,4},{6,7},{7,6},{8,9},{9,8},{10,11... | collective-permute-start | bytes 294920 | tf_op jit(solution)/shard_map/ppermute | solution.py:455
  53.8 10.8 %collective-permute-start.18 = (bf16[192,256]{1,0:T(8,128)(2,1)S(1)}, bf16[192,256]{1,0:T(8,128)(2,1)S(1)}, u32[]{:S(2)}, u32[]{:S(2)}) collective-permute-start(bf16[192,256]{1,0:T(8,128)(2,1)S(1)} %self_attention.2.refs_5_.refs_3_), channel_id=1, source_target_pairs={{0,2},{1,3},{2,0},{3,1},{4,6},{5,7},{6,4},{7,5},{8,10},{9,11},{10,... | collective-permute-start | bytes 294920 | tf_op jit(solution)/shard_map/ppermute | solution.py:455
  54.9 9.7 %collective-permute-start.19 = (bf16[192,256]{1,0:T(8,128)(2,1)S(1)}, bf16[192,256]{1,0:T(8,128)(2,1)S(1)}, u32[]{:S(2)}, u32[]{:S(2)}) collective-permute-start(bf16[192,256]{1,0:T(8,128)(2,1)S(1)} %self_attention.2.refs_5_.refs_3_), channel_id=1, source_target_pairs={{0,3},{1,2},{2,1},{3,0},{4,7},{5,6},{6,5},{7,4},{8,11},{9,10},{10,... | collective-permute-start | bytes 294920 | tf_op jit(solution)/shard_map/ppermute | solution.py:455
  64.7 6.2 %copy-start.9 = (s32[9]{0:T(128)S(1)}, s32[9]{0:T(128)}, u32[]{:S(2)}) copy-start(s32[9]{0:T(128)} %refs_2_.7) | copy-start | bytes 112
  64.7 5.2 %collective-permute-start.20 = (bf16[4,128,1024]{2,1,0:T(8,128)(2,1)S(1)}, bf16[4,128,1024]{2,1,0:T(8,128)(2,1)S(1)}, u32[]{:S(2)}, u32[]{:S(2)}) collective-permute-start(bf16[4,128,1024]{2,1,0:T(8,128)(2,1)S(1)} %bundle.5.refs_2_), channel_id=1, source_target_pairs={{0,4},{4,0},{8,12},{12,8},{16,20},{20,16},{24,28},{28,24},{1,5},{5... | collective-permute-start | bytes 3145736 | tf_op jit(solution)/shard_map/ppermute | solution.py:503
  64.7 12.1 %collective-permute-start.12 = (bf16[192,256]{1,0:T(8,128)(2,1)S(1)}, bf16[192,256]{1,0:T(8,128)(2,1)S(1)}, u32[]{:S(2)}, u32[]{:S(2)}) collective-permute-start(bf16[192,256]{1,0:T(8,128)(2,1)S(1)} %self_attention.3.refs_4_.refs_3_), channel_id=1, source_target_pairs={{0,1},{1,0},{2,3},{3,2},{4,5},{5,4},{6,7},{7,6},{8,9},{9,8},{10,11... | collective-permute-start | bytes 294920 | tf_op jit(solution)/shard_map/ppermute | solution.py:455
  67.4 10.9 %collective-permute-start.13 = (bf16[192,256]{1,0:T(8,128)(2,1)S(1)}, bf16[192,256]{1,0:T(8,128)(2,1)S(1)}, u32[]{:S(2)}, u32[]{:S(2)}) collective-permute-start(bf16[192,256]{1,0:T(8,128)(2,1)S(1)} %self_attention.3.refs_4_.refs_3_), channel_id=1, source_target_pairs={{0,2},{1,3},{2,0},{3,1},{4,6},{5,7},{6,4},{7,5},{8,10},{9,11},{10,... | collective-permute-start | bytes 294920 | tf_op jit(solution)/shard_map/ppermute | solution.py:455
  68.4 9.8 %collective-permute-start.14 = (bf16[192,256]{1,0:T(8,128)(2,1)S(1)}, bf16[192,256]{1,0:T(8,128)(2,1)S(1)}, u32[]{:S(2)}, u32[]{:S(2)}) collective-permute-start(bf16[192,256]{1,0:T(8,128)(2,1)S(1)} %self_attention.3.refs_4_.refs_3_), channel_id=1, source_target_pairs={{0,3},{1,2},{2,1},{3,0},{4,7},{5,6},{6,5},{7,4},{8,11},{9,10},{10,... | collective-permute-start | bytes 294920 | tf_op jit(solution)/shard_map/ppermute | solution.py:455
  73.8 17.9 %slice-start = ((s8[8388608]{0:T(1024)(128)(4,1)}), s8[4194304]{0:T(1024)(128)(4,1)S(1)}, s32[]{:S(2)}) async-start(s8[8388608]{0:T(1024)(128)(4,1)} %bitcast.1), calls=%async_computation | async-start | bytes 8388608
  73.8 17.9 %slice-start.1 = ((s8[8388608]{0:T(1024)(128)(4,1)}), s8[4194304]{0:T(1024)(128)(4,1)S(1)}, s32[]{:S(2)}) async-start(s8[8388608]{0:T(1024)(128)(4,1)} %bitcast.1), calls=%async_computation.1 | async-start | bytes 8388608
  73.8 16.2 %collective-permute-start.24 = (bf16[192,256]{1,0:T(8,128)(2,1)S(1)}, bf16[192,256]{1,0:T(8,128)(2,1)S(1)}, u32[]{:S(2)}, u32[]{:S(2)}) collective-permute-start(bf16[192,256]{1,0:T(8,128)(2,1)S(1)} %get-tuple-element.48.refs_1_), channel_id=1, source_target_pairs={{0,1},{1,0},{2,3},{3,2},{4,5},{5,4},{6,7},{7,6},{8,9},{9,8},{10,11... | collective-permute-start | bytes 294920 | tf_op jit(solution)/shard_map/ppermute | solution.py:455
  74.9 16.7 %collective-permute-start.25 = (bf16[192,256]{1,0:T(8,128)(2,1)S(1)}, bf16[192,256]{1,0:T(8,128)(2,1)S(1)}, u32[]{:S(2)}, u32[]{:S(2)}) collective-permute-start(bf16[192,256]{1,0:T(8,128)(2,1)S(1)} %get-tuple-element.48.refs_1_), channel_id=1, source_target_pairs={{0,2},{1,3},{2,0},{3,1},{4,6},{5,7},{6,4},{7,5},{8,10},{9,11},{10,... | collective-permute-start | bytes 294920 | tf_op jit(solution)/shard_map/ppermute | solution.py:455
  76.9 14.8 %collective-permute-start.26 = (bf16[192,256]{1,0:T(8,128)(2,1)S(1)}, bf16[192,256]{1,0:T(8,128)(2,1)S(1)}, u32[]{:S(2)}, u32[]{:S(2)}) collective-permute-start(bf16[192,256]{1,0:T(8,128)(2,1)S(1)} %get-tuple-element.48.refs_1_), channel_id=1, source_target_pairs={{0,3},{1,2},{2,1},{3,0},{4,7},{5,6},{6,5},{7,4},{8,11},{9,10},{10,... | collective-permute-start | bytes 294920 | tf_op jit(solution)/shard_map/ppermute | solution.py:455
  82.3 15.7 %collective-permute-start.21 = (bf16[192,256]{1,0:T(8,128)(2,1)S(1)}, bf16[192,256]{1,0:T(8,128)(2,1)S(1)}, u32[]{:S(2)}, u32[]{:S(2)}) collective-permute-start(bf16[192,256]{1,0:T(8,128)(2,1)S(1)} %get-tuple-element.43.refs_1_), channel_id=1, source_target_pairs={{0,1},{1,0},{2,3},{3,2},{4,5},{5,4},{6,7},{7,6},{8,9},{9,8},{10,11... | collective-permute-start | bytes 294920 | tf_op jit(solution)/shard_map/ppermute | solution.py:455
  89.2 8.9 %collective-permute-start.22 = (bf16[192,256]{1,0:T(8,128)(2,1)S(1)}, bf16[192,256]{1,0:T(8,128)(2,1)S(1)}, u32[]{:S(2)}, u32[]{:S(2)}) collective-permute-start(bf16[192,256]{1,0:T(8,128)(2,1)S(1)} %get-tuple-element.43.refs_1_), channel_id=1, source_target_pairs={{0,2},{1,3},{2,0},{3,1},{4,6},{5,7},{6,4},{7,5},{8,10},{9,11},{10,... | collective-permute-start | bytes 294920 | tf_op jit(solution)/shard_map/ppermute | solution.py:455
  90.0 8.0 %collective-permute-start.23 = (bf16[192,256]{1,0:T(8,128)(2,1)S(1)}, bf16[192,256]{1,0:T(8,128)(2,1)S(1)}, u32[]{:S(2)}, u32[]{:S(2)}) collective-permute-start(bf16[192,256]{1,0:T(8,128)(2,1)S(1)} %get-tuple-element.43.refs_1_), channel_id=1, source_target_pairs={{0,3},{1,2},{2,1},{3,0},{4,7},{5,6},{6,5},{7,4},{8,11},{9,10},{10,... | collective-permute-start | bytes 294920 | tf_op jit(solution)/shard_map/ppermute | solution.py:455

commit v5 on v4

--- a/solution.py
+++ b/solution.py
@@ -217,24 +217,28 @@
             w_ref[ids[1] ^ j, ids[0] % 2 ^ i] = part[j]
 
 
-def prepare(chunks, sources, parts):
+def prepare(chunks, sources, parts, after=()):
     rows, width = chunks[0].shape[2:]
     total = rows * sum(c.shape[0] for c in chunks)
     group, depth, model = parts[0].shape
     return pl.pallas_call(
-        placed(functools.partial(prepare_kernel, sources)),
+        placed(
+            skipping(
+                functools.partial(prepare_kernel, sources), 1 + len(chunks) + len(parts), len(after)
+            )
+        ),
         out_shape=(
             jax.ShapeDtypeStruct((total, width), jnp.bfloat16),
             jax.ShapeDtypeStruct((width // 128, 128 + ONES, total), jnp.bfloat16),
             jax.ShapeDtypeStruct((group, 2, depth, model), jnp.bfloat16),
         ),
-        in_specs=whole(len(chunks) + len(parts)),
+        in_specs=whole(len(chunks) + len(parts)) + anywhere(len(after)),
         out_specs=tuple(whole(3)),
         scratch_shapes=[pltpu.VMEM((total, width), jnp.bfloat16)],
         compiler_params=params(4),
         cost_estimate=cost(0, 5 * 2 * total * width),
         name="prepare",
-    )(*chunks, *parts)
+    )(*chunks, *parts, *after)
 
 
 def flash(queries, k_ref, vt_ref, low, high, least, most):
@@ -499,7 +503,7 @@
         )
         attended.append(over_head(mine, group))
     if paired:
-        own = bundle([parts], attended[1][:1] + attended[0][1:]) + enc
+        own = bundle([parts], attended[0][:1]) + enc
         parts, enc = zip(own, [lax.ppermute(y, "blk", xor(cycle, 1)) for y in own])
     else:
         enc = [lax.all_gather(enc_kv, "blk", axis=0)]
@@ -509,7 +513,9 @@
             bundle([over_head(lax.dynamic_index_in_dim(halves, side ^ i, 0, False), group)], ())[0]
             for i in range(2)
         ]
-    enc_keys, enc_values, w_out = prepare(enc, sources, parts)
+    enc_keys, enc_values, w_out = prepare(
+        enc, sources, parts, attended[1][:1] + attended[0][1:]
+    )
     w_out = w_out.reshape(group, width, -1)
 
     outs = ()

time: 104 us -> 103 us (level)
  waiting for transfers between devices: 14.8 us -> 10.1 us
  Pallas kernels: 38.7 us -> 42.7 us
    ppermute x18, waiting for transfers between devices: 13.6 us -> 8.89 us  [over_head(): return [x] + [lax.ppermute(x, 'head', xor(size, j)) for j in range(1, size)]]
    pallas_call x2, Pallas kernels: 4.59 us -> 8.62 us  [self_attention(): pl.pallas_call(placed(skipping(functools.partial(self_kernel, turn), 6, l...]
  transfers between devices with their start and end apart: 27 -> 27, of which waited for: 5 -> 5; matrix products, arithmetic and copies ran while one was open for 0% -> 0% of each run, Pallas kernels for 31% -> 35%
where the time goes in v5:
time: 103 us
  starting transfers between devices  45.6 us (44%)
  Pallas kernels  42.7 us (41%)
  waiting for transfers between devices  10.1 us (10%)
  local copies, waits for them, and re-layouts  3.98 us (4%)
  between operations  1.05 us (1%)
    ppermute x18, starting transfers between devices, over_head(): return [x] + [lax.ppermute(x, 'head', xor(size, j)) for j in range(1, size)]  37.4 us
    pallas_call x2, Pallas kernels, mlp(): pl.pallas_call(placed(functools.partial(mlp_kernel, turn)), out_shape=(ja...  12.8 us
    pallas_call x2, Pallas kernels, fetch(): pl.pallas_call(placed(skipping(functools.partial(fetch_kernel, cuts), 1 +...  9.65 us
    ppermute x18, waiting for transfers between devices, over_head(): return [x] + [lax.ppermute(x, 'head', xor(size, j)) for j in range(1, size)]  8.89 us
    pallas_call x2, Pallas kernels, self_attention(): pl.pallas_call(placed(skipping(functools.partial(self_kernel, turn), 6, l...  8.62 us
    ppermute x6, starting transfers between devices, over_chips(): lax.ppermute(x, 'blk', xor(size, s))  7.8 us
    pallas_call x2, Pallas kernels, cross_attention(): pl.pallas_call(placed(functools.partial(cross_kernel, turn)), out_shape=(...  7.03 us
    unnamed x24, local copies, waits for them, and re-layouts  3.98 us
  transfers between devices with their start and end apart: 27, of which 5 were waited for; matrix products, arithmetic and copies ran while one was open for 0% of the time, Pallas kernels for 35%

profile of v5, /device:TPU:0, one launch (start us, length us, event | category | flops | bytes accessed | tf_op | source)
XLA Modules:
  0.0 103.4 jit_solution(13272669220467057274)
XLA Ops:
  0.6 3.1 %collective-permute-start = (bf16[96,1024]{1,0:T(8,128)(2,1)}, bf16[96,1024]{1,0:T(8,128)(2,1)S(1)}, u32[]{:S(2)}, u32[]{:S(2)}) collective-permute-start(bf16[96,1024]{1,0:T(8,128)(2,1)} %refs_0_.10), channel_id=1, source_target_pairs={{0,1},{1,0},{2,3},{3,2},{4,5},{5,4},{6,7},{7,6},{8,9},{9,8},{10,11... | collective-permute-start | bytes 589832 | tf_op jit(solution)/shard_map/ppermute | solution.py:459
  3.7 2.6 %collective-permute-start.1 = (bf16[96,1024]{1,0:T(8,128)(2,1)}, bf16[96,1024]{1,0:T(8,128)(2,1)S(1)}, u32[]{:S(2)}, u32[]{:S(2)}) collective-permute-start(bf16[96,1024]{1,0:T(8,128)(2,1)} %refs_0_.10), channel_id=1, source_target_pairs={{0,2},{1,3},{2,0},{3,1},{4,6},{5,7},{6,4},{7,5},{8,10},{9,11},{10,... | collective-permute-start | bytes 589832 | tf_op jit(solution)/shard_map/ppermute | solution.py:459
  6.3 1.7 %collective-permute-start.6 = (bf16[2,256,256]{2,1,0:T(8,128)(2,1)}, bf16[2,256,256]{2,1,0:T(8,128)(2,1)S(1)}, u32[]{:S(2)}, u32[]{:S(2)}) collective-permute-start(bf16[2,256,256]{2,1,0:T(8,128)(2,1)} %refs_0_.11), channel_id=1, source_target_pairs={{0,8},{4,12},{8,0},{12,4},{16,24},{20,28},{24,16},{28,20},{1,9},{5... | collective-permute-start | bytes 786440 | tf_op jit(solution)/shard_map/ppermute | solution.py:463
  8.0 1.5 %collective-permute-start.7 = (bf16[2,256,256]{2,1,0:T(8,128)(2,1)}, bf16[2,256,256]{2,1,0:T(8,128)(2,1)S(1)}, u32[]{:S(2)}, u32[]{:S(2)}) collective-permute-start(bf16[2,256,256]{2,1,0:T(8,128)(2,1)} %refs_0_.11), channel_id=1, source_target_pairs={{0,16},{4,20},{8,24},{12,28},{16,0},{20,4},{24,8},{28,12},{1,17},{... | collective-permute-start | bytes 786440 | tf_op jit(solution)/shard_map/ppermute | solution.py:463
  9.5 1.4 %copy-done.3 = bf16[3,1024,256]{2,1,0:T(8,128)(2,1)S(1)} copy-done((bf16[3,1024,256]{2,1,0:T(8,128)(2,1)S(1)}, bf16[3,1024,256]{2,1,0:T(8,128)(2,1)}, u32[]{:S(2)}) %copy-start.3) | copy-done | bytes 1572888
  11.0 1.0 %copy-done.4 = bf16[256,1024]{1,0:T(8,128)(2,1)S(1)} copy-done((bf16[256,1024]{1,0:T(8,128)(2,1)S(1)}, bf16[256,1024]{1,0:T(8,128)(2,1)}, u32[]{:S(2)}) %copy-start.4) | copy-done | bytes 524312
  12.0 0.9 copy-done.6
  12.9 0.4 fetch.2
  13.3 0.6 copy-done.5
  13.9 1.0 collective-permute-start.8
  14.9 6.2 %collective-permute-done.1.refs_2_ = bf16[96,1024]{1,0:T(8,128)(2,1)S(1)} collective-permute-done((bf16[96,1024]{1,0:T(8,128)(2,1)}, bf16[96,1024]{1,0:T(8,128)(2,1)S(1)}, u32[]{:S(2)}, u32[]{:S(2)}) %collective-permute-start.1) | collective-permute-done | bytes 196640 | tf_op jit(solution)/shard_map/ppermute | solution.py:459
  21.1 0.8 project.1
  21.9 1.6 %collective-permute-start.3 = (bf16[2,384,256]{2,1,0:T(8,128)(2,1)S(1)}, bf16[2,384,256]{2,1,0:T(8,128)(2,1)S(1)}, u32[]{:S(2)}, u32[]{:S(2)}) collective-permute-start(bf16[2,384,256]{2,1,0:T(8,128)(2,1)S(1)} %get-tuple-element.33.refs_0_), channel_id=1, source_target_pairs={{0,8},{4,12},{8,0},{12,4},{16,24},{20,28},{24,16},{28,20},{1,9},{5... | collective-permute-start | bytes 1179656 | tf_op jit(solution)/shard_map/ppermute | solution.py:463
  23.5 1.5 %collective-permute-start.4 = (bf16[2,384,256]{2,1,0:T(8,128)(2,1)S(1)}, bf16[2,384,256]{2,1,0:T(8,128)(2,1)S(1)}, u32[]{:S(2)}, u32[]{:S(2)}) collective-permute-start(bf16[2,384,256]{2,1,0:T(8,128)(2,1)S(1)} %get-tuple-element.33.refs_0_), channel_id=1, source_target_pairs={{0,16},{4,20},{8,24},{12,28},{16,0},{20,4},{24,8},{28,12},{1,17},{... | collective-permute-start | bytes 1179656 | tf_op jit(solution)/shard_map/ppermute | solution.py:463
  25.0 0.5 collective-permute-start.5
  25.5 4.4 %collective-permute-start.10 = (bf16[128,1024]{1,0:T(8,128)(2,1)S(1)}, bf16[128,1024]{1,0:T(8,128)(2,1)S(1)}, u32[]{:S(2)}, u32[]{:S(2)}) collective-permute-start(bf16[128,1024]{1,0:T(8,128)(2,1)S(1)} %get-tuple-element.35.refs_0_), channel_id=1, source_target_pairs={{0,2},{1,3},{2,0},{3,1},{4,6},{5,7},{6,4},{7,5},{8,10},{9,11},{10,... | collective-permute-start | bytes 786440 | tf_op jit(solution)/shard_map/ppermute | solution.py:459
  29.9 0.1 bundle.3.refs_5_.refs_0_
  30.0 9.3 %fetch.3 = (bf16[1024,256]{1,0:T(8,128)(2,1)S(1)}, bf16[1024,1024]{1,0:T(8,128)(2,1)S(1)}, bf16[1024,4096]{1,0:T(8,128)(2,1)S(1)}, bf16[4096,1024]{1,0:T(8,128)(2,1)}, bf16[3,1024,256]{2,1,0:T(8,128)(2,1)S(1)}) custom-call(bf16[1024,1024]{1,0:T(8,128)(2,1)S(1)} %copy-done, bf16[1024,1024]{1,0:T(8,128)(2,1)S(1)} %copy-done.1, bf16[1024,4096]{1,0:T(8,128)(2,1)} %refs_2_.5, ...), custom_call_target="tpu_custom_call" | custom-call | bytes 1048576 | tf_op jit(solution)/shard_map/fetch/pallas_call | solution.py:125
  39.3 0.6 collective-permute-done.10.refs_6_.refs_2_
  39.9 0.2 collective-permute-done.9.refs_5_.refs_1_
  40.1 0.1 bundle.4.refs_1_
  40.2 0.1 collective-permute-start.11
  40.3 2.1 %collective-permute-start.16 = (bf16[128,1024]{1,0:T(8,128)(2,1)S(1)}, bf16[128,1024]{1,0:T(8,128)(2,1)S(1)}, u32[]{:S(2)}, u32[]{:S(2)}) collective-permute-start(bf16[128,1024]{1,0:T(8,128)(2,1)S(1)} %get-tuple-element.35.refs_0_), channel_id=1, source_target_pairs={{0,3},{1,2},{2,1},{3,0},{4,7},{5,6},{6,5},{7,4},{8,11},{9,10},{10,... | collective-permute-start | bytes 786440 | tf_op jit(solution)/shard_map/ppermute | solution.py:459
  42.4 0.2 collective-permute-start.15
  42.5 1.2 %collective-permute-done.11.refs_2_ = bf16[4,2,384,256]{3,2,1,0:T(8,128)(2,1)S(1)} collective-permute-done((bf16[4,2,384,256]{3,2,1,0:T(8,128)(2,1)S(1)}, bf16[4,2,384,256]{3,2,1,0:T(8,128)(2,1)S(1)}, u32[]{:S(2)}, u32[]{:S(2)}) %collective-permute-start.11) | collective-permute-done | bytes 1572896 | tf_op jit(solution)/shard_map/ppermute | solution.py:493
  43.7 2.6 %order.1 = (bf16[3072,256]{1,0:T(8,128)(2,1)S(1)}, bf16[2,144,3072]{2,1,0:T(8,128)(2,1)S(1)}, bf16[2,384,256]{2,1,0:T(8,128)(2,1)}) custom-call(s32[16]{0:T(128)S(1)} %copy-done.7, bf16[4,2,384,256]{3,2,1,0:T(8,128)(2,1)S(1)} %bundle.4.refs_1_, bf16[4,2,384,256]{3,2,1,0:T(8,128)(2,1)S(1)} %collective-permute-done.11.refs_2_), custom_call_target="tpu_custom_call" | custom-call | bytes 393216 | tf_op jit(solution)/shard_map/order/pallas_call | solution.py:189
  46.3 2.8 %self_attention.2.refs_5_.refs_4_.refs_3_ = bf16[192,256]{1,0:T(8,128)(2,1)S(1)} custom-call(s32[16]{0:T(128)S(1)} %copy-done.7, s32[9]{0:T(128)S(1)} %copy-done.8, bf16[384,256]{1,0:T(8,128)(2,1)S(1)} %get-tuple-element.32.refs_4_.refs_2_, bf16[3072,256]{1,0:T(8,128)(2,1)S(1)} %get-tuple-element.36.refs_3_, bf16[2,144,3072]{2,1,0:T(8,128)(2,1)S(1)} %get-tuple-element.37.refs_4_), custom_call_target="tpu_custom_call" | custom-call | flops 10000000000 | tf_op jit(solution)/shard_map/self_attention/pallas_call | solution.py:322
  49.1 1.8 %collective-permute-done.16.refs_3_ = bf16[128,1024]{1,0:T(8,128)(2,1)S(1)} collective-permute-done((bf16[128,1024]{1,0:T(8,128)(2,1)S(1)}, bf16[128,1024]{1,0:T(8,128)(2,1)S(1)}, u32[]{:S(2)}, u32[]{:S(2)}) %collective-permute-start.16) | collective-permute-done | bytes 262176 | tf_op jit(solution)/shard_map/ppermute | solution.py:459
  50.9 0.1 bundle.5.refs_2_
  51.0 0.1 collective-permute-start.17
  51.1 6.1 %collective-permute-start.18 = (bf16[192,256]{1,0:T(8,128)(2,1)S(1)}, bf16[192,256]{1,0:T(8,128)(2,1)S(1)}, u32[]{:S(2)}, u32[]{:S(2)}) collective-permute-start(bf16[192,256]{1,0:T(8,128)(2,1)S(1)} %self_attention.2.refs_5_.refs_4_.refs_3_), channel_id=1, source_target_pairs={{0,1},{1,0},{2,3},{3,2},{4,5},{5,4},{6,7},{7,6},{8,9},{9,8},{10,11... | collective-permute-start | bytes 294920 | tf_op jit(solution)/shard_map/ppermute | solution.py:459
  57.2 0.6 collective-permute-start.19
  57.8 1.8 %collective-permute-start.20 = (bf16[192,256]{1,0:T(8,128)(2,1)S(1)}, bf16[192,256]{1,0:T(8,128)(2,1)S(1)}, u32[]{:S(2)}, u32[]{:S(2)}) collective-permute-start(bf16[192,256]{1,0:T(8,128)(2,1)S(1)} %self_attention.2.refs_5_.refs_4_.refs_3_), channel_id=1, source_target_pairs={{0,3},{1,2},{2,1},{3,0},{4,7},{5,6},{6,5},{7,4},{8,11},{9,10},{10,... | collective-permute-start | bytes 294920 | tf_op jit(solution)/shard_map/ppermute | solution.py:459
  59.7 5.8 %self_attention.3.refs_4_.refs_3_ = bf16[192,256]{1,0:T(8,128)(2,1)S(1)} custom-call(s32[16]{0:T(128)S(1)} %copy-done.7, s32[9]{0:T(128)S(1)} %copy-done.8, bf16[384,256]{1,0:T(8,128)(2,1)S(1)} %get-tuple-element.32.refs_4_.refs_2_, bf16[3072,256]{1,0:T(8,128)(2,1)S(1)} %get-tuple-element.36.refs_3_, bf16[2,144,3072]{2,1,0:T(8,128)(2,1)S(1)} %get-tuple-element.37.refs_4_, ...), custom_call_target="tpu_custom_call" | custom-call | flops 10000000000 | tf_op jit(solution)/shard_map/self_attention/pallas_call | solution.py:322
  65.5 1.1 %collective-permute-start.12 = (bf16[192,256]{1,0:T(8,128)(2,1)S(1)}, bf16[192,256]{1,0:T(8,128)(2,1)S(1)}, u32[]{:S(2)}, u32[]{:S(2)}) collective-permute-start(bf16[192,256]{1,0:T(8,128)(2,1)S(1)} %self_attention.3.refs_4_.refs_3_), channel_id=1, source_target_pairs={{0,1},{1,0},{2,3},{3,2},{4,5},{5,4},{6,7},{7,6},{8,9},{9,8},{10,11... | collective-permute-start | bytes 294920 | tf_op jit(solution)/shard_map/ppermute | solution.py:459
  66.6 1.5 %collective-permute-start.13 = (bf16[192,256]{1,0:T(8,128)(2,1)S(1)}, bf16[192,256]{1,0:T(8,128)(2,1)S(1)}, u32[]{:S(2)}, u32[]{:S(2)}) collective-permute-start(bf16[192,256]{1,0:T(8,128)(2,1)S(1)} %self_attention.3.refs_4_.refs_3_), channel_id=1, source_target_pairs={{0,2},{1,3},{2,0},{3,1},{4,6},{5,7},{6,4},{7,5},{8,10},{9,11},{10,... | collective-permute-start | bytes 294920 | tf_op jit(solution)/shard_map/ppermute | solution.py:459
  68.2 1.8 %collective-permute-start.14 = (bf16[192,256]{1,0:T(8,128)(2,1)S(1)}, bf16[192,256]{1,0:T(8,128)(2,1)S(1)}, u32[]{:S(2)}, u32[]{:S(2)}) collective-permute-start(bf16[192,256]{1,0:T(8,128)(2,1)S(1)} %self_attention.3.refs_4_.refs_3_), channel_id=1, source_target_pairs={{0,3},{1,2},{2,1},{3,0},{4,7},{5,6},{6,5},{7,4},{8,11},{9,10},{10,... | collective-permute-start | bytes 294920 | tf_op jit(solution)/shard_map/ppermute | solution.py:459
  70.0 1.0 prepare.1
  71.0 2.9 %cross_attention.3 = (f32[192,1024]{1,0:T(8,128)S(1)}, bf16[192,256]{1,0:T(8,128)(2,1)S(1)}) custom-call(s32[16]{0:T(128)S(1)} %copy-done.7, s32[9]{0:T(128)S(1)} %copy-done.8, s32[9]{0:T(128)S(1)} %copy-done.9, bf16[192,256]{1,0:T(8,128)(2,1)S(1)} %self_attention.2.refs_5_.refs_4_.refs_3_, bf16[192,256]{1,0:T(8,128)(2,1)S(1)} %collective-permute-done.18.refs_5_.refs_4_, ...), custom_call_target="tpu_custom_call" | custom-call | flops 10000000000 | tf_op jit(solution)/shard_map/cross_attention/pallas_call | solution.py:370
  74.0 0.2 collective-permute-start.24
  74.2 2.4 %collective-permute-start.25 = (bf16[192,256]{1,0:T(8,128)(2,1)S(1)}, bf16[192,256]{1,0:T(8,128)(2,1)S(1)}, u32[]{:S(2)}, u32[]{:S(2)}) collective-permute-start(bf16[192,256]{1,0:T(8,128)(2,1)S(1)} %get-tuple-element.48.refs_1_), channel_id=1, source_target_pairs={{0,2},{1,3},{2,0},{3,1},{4,6},{5,7},{6,4},{7,5},{8,10},{9,11},{10,... | collective-permute-start | bytes 294920 | tf_op jit(solution)/shard_map/ppermute | solution.py:459
  76.6 1.8 %collective-permute-start.26 = (bf16[192,256]{1,0:T(8,128)(2,1)S(1)}, bf16[192,256]{1,0:T(8,128)(2,1)S(1)}, u32[]{:S(2)}, u32[]{:S(2)}) collective-permute-start(bf16[192,256]{1,0:T(8,128)(2,1)S(1)} %get-tuple-element.48.refs_1_), channel_id=1, source_target_pairs={{0,3},{1,2},{2,1},{3,0},{4,7},{5,6},{6,5},{7,4},{8,11},{9,10},{10,... | collective-permute-start | bytes 294920 | tf_op jit(solution)/shard_map/ppermute | solution.py:459
  78.4 4.1 %cross_attention.2 = (f32[192,1024]{1,0:T(8,128)S(1)}, bf16[192,256]{1,0:T(8,128)(2,1)S(1)}) custom-call(s32[16]{0:T(128)S(1)} %copy-done.7, s32[9]{0:T(128)S(1)} %copy-done.8, s32[9]{0:T(128)S(1)} %copy-done.9, bf16[192,256]{1,0:T(8,128)(2,1)S(1)} %self_attention.3.refs_4_.refs_3_, bf16[192,256]{1,0:T(8,128)(2,1)S(1)} %collective-permute-done.12.refs_4_, ...), custom_call_target="tpu_custom_call" | custom-call | flops 10000000000 | tf_op jit(solution)/shard_map/cross_attention/pallas_call | solution.py:370
  82.5 5.4 %collective-permute-start.21 = (bf16[192,256]{1,0:T(8,128)(2,1)S(1)}, bf16[192,256]{1,0:T(8,128)(2,1)S(1)}, u32[]{:S(2)}, u32[]{:S(2)}) collective-permute-start(bf16[192,256]{1,0:T(8,128)(2,1)S(1)} %get-tuple-element.43.refs_1_), channel_id=1, source_target_pairs={{0,1},{1,0},{2,3},{3,2},{4,5},{5,4},{6,7},{7,6},{8,9},{9,8},{10,11... | collective-permute-start | bytes 294920 | tf_op jit(solution)/shard_map/ppermute | solution.py:459
  88.0 0.7 collective-permute-start.22
  88.6 1.8 %collective-permute-start.23 = (bf16[192,256]{1,0:T(8,128)(2,1)S(1)}, bf16[192,256]{1,0:T(8,128)(2,1)S(1)}, u32[]{:S(2)}, u32[]{:S(2)}) collective-permute-start(bf16[192,256]{1,0:T(8,128)(2,1)S(1)} %get-tuple-element.43.refs_1_), channel_id=1, source_target_pairs={{0,3},{1,2},{2,1},{3,0},{4,7},{5,6},{6,5},{7,4},{8,11},{9,10},{10,... | collective-permute-start | bytes 294920 | tf_op jit(solution)/shard_map/ppermute | solution.py:459
  90.4 6.4 %mlp.2 = (f32[96,1024]{1,0:T(8,128)}, f32[3,384,256]{2,1,0:T(8,128)}) custom-call(s32[16]{0:T(128)S(1)} %copy-done.7, bf16[192,256]{1,0:T(8,128)(2,1)S(1)} %get-tuple-element.48.refs_1_, bf16[192,256]{1,0:T(8,128)(2,1)S(1)} %collective-permute-done.24.refs_2_, bf16[192,256]{1,0:T(8,128)(2,1)S(1)} %collective-permute-done.25.refs_3_, ...), custom_call_target="tpu_custom_call" | custom-call | flops 300000000 | tf_op jit(solution)/shard_map/mlp/pallas_call | solution.py:437
  96.9 6.4 %mlp.3 = (f32[96,1024]{1,0:T(8,128)}, f32[3,384,256]{2,1,0:T(8,128)}) custom-call(s32[16]{0:T(128)S(1)} %copy-done.7, bf16[192,256]{1,0:T(8,128)(2,1)S(1)} %get-tuple-element.43.refs_1_, bf16[192,256]{1,0:T(8,128)(2,1)S(1)} %collective-permute-done.21.refs_2_, ...), custom_call_target="tpu_custom_call", output_to_operand_aliasing={{0}: (10, {}), {1}: (11, {})} | custom-call | flops 300000000 | tf_op jit(solution)/shard_map/mlp/pallas_call | solution.py:437
  (45 shorter events, 0.1 us)
Async XLA Ops:
  0.6 12.7 %collective-permute-start = (bf16[96,1024]{1,0:T(8,128)(2,1)}, bf16[96,1024]{1,0:T(8,128)(2,1)S(1)}, u32[]{:S(2)}, u32[]{:S(2)}) collective-permute-start(bf16[96,1024]{1,0:T(8,128)(2,1)} %refs_0_.10), channel_id=1, source_target_pairs={{0,1},{1,0},{2,3},{3,2},{4,5},{5,4},{6,7},{7,6},{8,9},{9,8},{10,11... | collective-permute-start | bytes 589832 | tf_op jit(solution)/shard_map/ppermute | solution.py:459
  3.7 17.4 %collective-permute-start.1 = (bf16[96,1024]{1,0:T(8,128)(2,1)}, bf16[96,1024]{1,0:T(8,128)(2,1)S(1)}, u32[]{:S(2)}, u32[]{:S(2)}) collective-permute-start(bf16[96,1024]{1,0:T(8,128)(2,1)} %refs_0_.10), channel_id=1, source_target_pairs={{0,2},{1,3},{2,0},{3,1},{4,6},{5,7},{6,4},{7,5},{8,10},{9,11},{10,... | collective-permute-start | bytes 589832 | tf_op jit(solution)/shard_map/ppermute | solution.py:459
  6.3 14.8 %collective-permute-start.2 = (bf16[96,1024]{1,0:T(8,128)(2,1)}, bf16[96,1024]{1,0:T(8,128)(2,1)S(1)}, u32[]{:S(2)}, u32[]{:S(2)}) collective-permute-start(bf16[96,1024]{1,0:T(8,128)(2,1)} %refs_0_.10), channel_id=1, source_target_pairs={{0,3},{1,2},{2,1},{3,0},{4,7},{5,6},{6,5},{7,4},{8,11},{9,10},{10,... | collective-permute-start | bytes 589832 | tf_op jit(solution)/shard_map/ppermute | solution.py:459
  6.3 18.7 %collective-permute-start.6 = (bf16[2,256,256]{2,1,0:T(8,128)(2,1)}, bf16[2,256,256]{2,1,0:T(8,128)(2,1)S(1)}, u32[]{:S(2)}, u32[]{:S(2)}) collective-permute-start(bf16[2,256,256]{2,1,0:T(8,128)(2,1)} %refs_0_.11), channel_id=1, source_target_pairs={{0,8},{4,12},{8,0},{12,4},{16,24},{20,28},{24,16},{28,20},{1,9},{5... | collective-permute-start | bytes 786440 | tf_op jit(solution)/shard_map/ppermute | solution.py:463
  8.0 17.5 %collective-permute-start.7 = (bf16[2,256,256]{2,1,0:T(8,128)(2,1)}, bf16[2,256,256]{2,1,0:T(8,128)(2,1)S(1)}, u32[]{:S(2)}, u32[]{:S(2)}) collective-permute-start(bf16[2,256,256]{2,1,0:T(8,128)(2,1)} %refs_0_.11), channel_id=1, source_target_pairs={{0,16},{4,20},{8,24},{12,28},{16,0},{20,4},{24,8},{28,12},{1,17},{... | collective-permute-start | bytes 786440 | tf_op jit(solution)/shard_map/ppermute | solution.py:463
  9.5 1.4 %copy-start.3 = (bf16[3,1024,256]{2,1,0:T(8,128)(2,1)S(1)}, bf16[3,1024,256]{2,1,0:T(8,128)(2,1)}, u32[]{:S(2)}) copy-start(bf16[3,1024,256]{2,1,0:T(8,128)(2,1)} %refs_1_.6) | copy-start | bytes 4718596
  11.0 1.0 %copy-start.4 = (bf16[256,1024]{1,0:T(8,128)(2,1)S(1)}, bf16[256,1024]{1,0:T(8,128)(2,1)}, u32[]{:S(2)}) copy-start(bf16[256,1024]{1,0:T(8,128)(2,1)} %refs_2_.4) | copy-start | bytes 1572868
  12.0 0.9 copy-start.6
  12.9 0.9 copy-start.5
  13.9 16.0 %collective-permute-start.8 = (bf16[2,256,256]{2,1,0:T(8,128)(2,1)S(1)}, bf16[2,256,256]{2,1,0:T(8,128)(2,1)S(1)}, u32[]{:S(2)}, u32[]{:S(2)}) collective-permute-start(bf16[2,256,256]{2,1,0:T(8,128)(2,1)S(1)} %copy-done.5), channel_id=1, source_target_pairs={{0,24},{4,28},{8,16},{12,20},{16,8},{20,12},{24,0},{28,4},{1,25},{... | collective-permute-start | bytes 786440 | tf_op jit(solution)/shard_map/ppermute | solution.py:463
  21.1 8.9 %copy-start.1 = (bf16[1024,1024]{1,0:T(8,128)(2,1)S(1)}, bf16[1024,1024]{1,0:T(8,128)(2,1)}, u32[]{:S(2)}) copy-start(bf16[1024,1024]{1,0:T(8,128)(2,1)} %refs_1_.7) | copy-start | bytes 6291460
  21.1 8.9 %copy-start.2 = (bf16[3,1024,256]{2,1,0:T(8,128)(2,1)S(1)}, bf16[3,1024,256]{2,1,0:T(8,128)(2,1)}, u32[]{:S(2)}) copy-start(bf16[3,1024,256]{2,1,0:T(8,128)(2,1)} %refs_4_.1) | copy-start | bytes 4718596
  21.9 8.0 %copy-start = (bf16[1024,1024]{1,0:T(8,128)(2,1)S(1)}, bf16[1024,1024]{1,0:T(8,128)(2,1)}, u32[]{:S(2)}) copy-start(bf16[1024,1024]{1,0:T(8,128)(2,1)} %refs_0_.12) | copy-start | bytes 6291460
  21.9 18.2 %collective-permute-start.3 = (bf16[2,384,256]{2,1,0:T(8,128)(2,1)S(1)}, bf16[2,384,256]{2,1,0:T(8,128)(2,1)S(1)}, u32[]{:S(2)}, u32[]{:S(2)}) collective-permute-start(bf16[2,384,256]{2,1,0:T(8,128)(2,1)S(1)} %get-tuple-element.33.refs_0_), channel_id=1, source_target_pairs={{0,8},{4,12},{8,0},{12,4},{16,24},{20,28},{24,16},{28,20},{1,9},{5... | collective-permute-start | bytes 1179656 | tf_op jit(solution)/shard_map/ppermute | solution.py:463
  23.5 16.6 %collective-permute-start.4 = (bf16[2,384,256]{2,1,0:T(8,128)(2,1)S(1)}, bf16[2,384,256]{2,1,0:T(8,128)(2,1)S(1)}, u32[]{:S(2)}, u32[]{:S(2)}) collective-permute-start(bf16[2,384,256]{2,1,0:T(8,128)(2,1)S(1)} %get-tuple-element.33.refs_0_), channel_id=1, source_target_pairs={{0,16},{4,20},{8,24},{12,28},{16,0},{20,4},{24,8},{28,12},{1,17},{... | collective-permute-start | bytes 1179656 | tf_op jit(solution)/shard_map/ppermute | solution.py:463
  25.0 15.1 %collective-permute-start.5 = (bf16[2,384,256]{2,1,0:T(8,128)(2,1)S(1)}, bf16[2,384,256]{2,1,0:T(8,128)(2,1)S(1)}, u32[]{:S(2)}, u32[]{:S(2)}) collective-permute-start(bf16[2,384,256]{2,1,0:T(8,128)(2,1)S(1)} %get-tuple-element.33.refs_0_), channel_id=1, source_target_pairs={{0,24},{4,28},{8,16},{12,20},{16,8},{20,12},{24,0},{28,4},{1,25},{... | collective-permute-start | bytes 1179656 | tf_op jit(solution)/shard_map/ppermute | solution.py:463
  25.5 14.4 %collective-permute-start.10 = (bf16[128,1024]{1,0:T(8,128)(2,1)S(1)}, bf16[128,1024]{1,0:T(8,128)(2,1)S(1)}, u32[]{:S(2)}, u32[]{:S(2)}) collective-permute-start(bf16[128,1024]{1,0:T(8,128)(2,1)S(1)} %get-tuple-element.35.refs_0_), channel_id=1, source_target_pairs={{0,2},{1,3},{2,0},{3,1},{4,6},{5,7},{6,4},{7,5},{8,10},{9,11},{10,... | collective-permute-start | bytes 786440 | tf_op jit(solution)/shard_map/ppermute | solution.py:459
  29.9 10.2 %collective-permute-start.9 = (bf16[128,1024]{1,0:T(8,128)(2,1)S(1)}, bf16[128,1024]{1,0:T(8,128)(2,1)S(1)}, u32[]{:S(2)}, u32[]{:S(2)}) collective-permute-start(bf16[128,1024]{1,0:T(8,128)(2,1)S(1)} %get-tuple-element.35.refs_0_), channel_id=1, source_target_pairs={{0,1},{1,0},{2,3},{3,2},{4,5},{5,4},{6,7},{7,6},{8,9},{9,8},{10,11... | collective-permute-start | bytes 786440 | tf_op jit(solution)/shard_map/ppermute | solution.py:459
  40.1 3.6 %copy-start.7 = (s32[16]{0:T(128)S(1)}, s32[16]{0:T(128)}, u32[]{:S(2)}) copy-start(s32[16]{0:T(128)} %refs_0_.19) | copy-start | bytes 196
  40.2 6.1 %copy-start.8 = (s32[9]{0:T(128)S(1)}, s32[9]{0:T(128)}, u32[]{:S(2)}) copy-start(s32[9]{0:T(128)} %refs_1_.11) | copy-start | bytes 112
  40.2 3.5 %collective-permute-start.11 = (bf16[4,2,384,256]{3,2,1,0:T(8,128)(2,1)S(1)}, bf16[4,2,384,256]{3,2,1,0:T(8,128)(2,1)S(1)}, u32[]{:S(2)}, u32[]{:S(2)}) collective-permute-start(bf16[4,2,384,256]{3,2,1,0:T(8,128)(2,1)S(1)} %bundle.4.refs_1_), channel_id=1, source_target_pairs={{0,4},{4,0},{8,12},{12,8},{16,20},{20,16},{24,28},{28,24},{1,5},{5... | collective-permute-start | bytes 4718600 | tf_op jit(solution)/shard_map/ppermute | solution.py:493
  40.3 10.6 %collective-permute-start.16 = (bf16[128,1024]{1,0:T(8,128)(2,1)S(1)}, bf16[128,1024]{1,0:T(8,128)(2,1)S(1)}, u32[]{:S(2)}, u32[]{:S(2)}) collective-permute-start(bf16[128,1024]{1,0:T(8,128)(2,1)S(1)} %get-tuple-element.35.refs_0_), channel_id=1, source_target_pairs={{0,3},{1,2},{2,1},{3,0},{4,7},{5,6},{6,5},{7,4},{8,11},{9,10},{10,... | collective-permute-start | bytes 786440 | tf_op jit(solution)/shard_map/ppermute | solution.py:459
  42.4 23.1 %collective-permute-start.15 = (bf16[4,2,256,256]{3,2,1,0:T(8,128)(2,1)S(1)}, bf16[4,2,256,256]{3,2,1,0:T(8,128)(2,1)S(1)}, u32[]{:S(2)}, u32[]{:S(2)}) collective-permute-start(bf16[4,2,256,256]{3,2,1,0:T(8,128)(2,1)S(1)} %bundle.3.refs_5_.refs_0_), channel_id=1, source_target_pairs={{0,4},{4,0},{8,12},{12,8},{16,20},{20,16},{24,28},{28,24},{1,5},{5... | collective-permute-start | bytes 3145736 | tf_op jit(solution)/shard_map/ppermute | solution.py:507
  51.0 19.0 %collective-permute-start.17 = (bf16[4,128,1024]{2,1,0:T(8,128)(2,1)S(1)}, bf16[4,128,1024]{2,1,0:T(8,128)(2,1)S(1)}, u32[]{:S(2)}, u32[]{:S(2)}) collective-permute-start(bf16[4,128,1024]{2,1,0:T(8,128)(2,1)S(1)} %bundle.5.refs_2_), channel_id=1, source_target_pairs={{0,4},{4,0},{8,12},{12,8},{16,20},{20,16},{24,28},{28,24},{1,5},{5... | collective-permute-start | bytes 3145736 | tf_op jit(solution)/shard_map/ppermute | solution.py:507
  51.1 15.6 %collective-permute-start.18 = (bf16[192,256]{1,0:T(8,128)(2,1)S(1)}, bf16[192,256]{1,0:T(8,128)(2,1)S(1)}, u32[]{:S(2)}, u32[]{:S(2)}) collective-permute-start(bf16[192,256]{1,0:T(8,128)(2,1)S(1)} %self_attention.2.refs_5_.refs_4_.refs_3_), channel_id=1, source_target_pairs={{0,1},{1,0},{2,3},{3,2},{4,5},{5,4},{6,7},{7,6},{8,9},{9,8},{10,11... | collective-permute-start | bytes 294920 | tf_op jit(solution)/shard_map/ppermute | solution.py:459
  57.2 10.9 %collective-permute-start.19 = (bf16[192,256]{1,0:T(8,128)(2,1)S(1)}, bf16[192,256]{1,0:T(8,128)(2,1)S(1)}, u32[]{:S(2)}, u32[]{:S(2)}) collective-permute-start(bf16[192,256]{1,0:T(8,128)(2,1)S(1)} %self_attention.2.refs_5_.refs_4_.refs_3_), channel_id=1, source_target_pairs={{0,2},{1,3},{2,0},{3,1},{4,6},{5,7},{6,4},{7,5},{8,10},{9,11},{10,... | collective-permute-start | bytes 294920 | tf_op jit(solution)/shard_map/ppermute | solution.py:459
  57.8 12.2 %collective-permute-start.20 = (bf16[192,256]{1,0:T(8,128)(2,1)S(1)}, bf16[192,256]{1,0:T(8,128)(2,1)S(1)}, u32[]{:S(2)}, u32[]{:S(2)}) collective-permute-start(bf16[192,256]{1,0:T(8,128)(2,1)S(1)} %self_attention.2.refs_5_.refs_4_.refs_3_), channel_id=1, source_target_pairs={{0,3},{1,2},{2,1},{3,0},{4,7},{5,6},{6,5},{7,4},{8,11},{9,10},{10,... | collective-permute-start | bytes 294920 | tf_op jit(solution)/shard_map/ppermute | solution.py:459
  65.5 5.5 %copy-start.9 = (s32[9]{0:T(128)S(1)}, s32[9]{0:T(128)}, u32[]{:S(2)}) copy-start(s32[9]{0:T(128)} %refs_2_.7) | copy-start | bytes 112
  65.5 11.1 %collective-permute-start.12 = (bf16[192,256]{1,0:T(8,128)(2,1)S(1)}, bf16[192,256]{1,0:T(8,128)(2,1)S(1)}, u32[]{:S(2)}, u32[]{:S(2)}) collective-permute-start(bf16[192,256]{1,0:T(8,128)(2,1)S(1)} %self_attention.3.refs_4_.refs_3_), channel_id=1, source_target_pairs={{0,1},{1,0},{2,3},{3,2},{4,5},{5,4},{6,7},{7,6},{8,9},{9,8},{10,11... | collective-permute-start | bytes 294920 | tf_op jit(solution)/shard_map/ppermute | solution.py:459
  66.6 11.8 %collective-permute-start.13 = (bf16[192,256]{1,0:T(8,128)(2,1)S(1)}, bf16[192,256]{1,0:T(8,128)(2,1)S(1)}, u32[]{:S(2)}, u32[]{:S(2)}) collective-permute-start(bf16[192,256]{1,0:T(8,128)(2,1)S(1)} %self_attention.3.refs_4_.refs_3_), channel_id=1, source_target_pairs={{0,2},{1,3},{2,0},{3,1},{4,6},{5,7},{6,4},{7,5},{8,10},{9,11},{10,... | collective-permute-start | bytes 294920 | tf_op jit(solution)/shard_map/ppermute | solution.py:459
  68.2 10.3 %collective-permute-start.14 = (bf16[192,256]{1,0:T(8,128)(2,1)S(1)}, bf16[192,256]{1,0:T(8,128)(2,1)S(1)}, u32[]{:S(2)}, u32[]{:S(2)}) collective-permute-start(bf16[192,256]{1,0:T(8,128)(2,1)S(1)} %self_attention.3.refs_4_.refs_3_), channel_id=1, source_target_pairs={{0,3},{1,2},{2,1},{3,0},{4,7},{5,6},{6,5},{7,4},{8,11},{9,10},{10,... | collective-permute-start | bytes 294920 | tf_op jit(solution)/shard_map/ppermute | solution.py:459
  74.0 16.5 %slice-start = ((s8[8388608]{0:T(1024)(128)(4,1)}), s8[4194304]{0:T(1024)(128)(4,1)S(1)}, s32[]{:S(2)}) async-start(s8[8388608]{0:T(1024)(128)(4,1)} %bitcast.1), calls=%async_computation | async-start | bytes 8388608
  74.0 16.5 %slice-start.1 = ((s8[8388608]{0:T(1024)(128)(4,1)}), s8[4194304]{0:T(1024)(128)(4,1)S(1)}, s32[]{:S(2)}) async-start(s8[8388608]{0:T(1024)(128)(4,1)} %bitcast.1), calls=%async_computation.1 | async-start | bytes 8388608
  74.0 14.7 %collective-permute-start.24 = (bf16[192,256]{1,0:T(8,128)(2,1)S(1)}, bf16[192,256]{1,0:T(8,128)(2,1)S(1)}, u32[]{:S(2)}, u32[]{:S(2)}) collective-permute-start(bf16[192,256]{1,0:T(8,128)(2,1)S(1)} %get-tuple-element.48.refs_1_), channel_id=1, source_target_pairs={{0,1},{1,0},{2,3},{3,2},{4,5},{5,4},{6,7},{7,6},{8,9},{9,8},{10,11... | collective-permute-start | bytes 294920 | tf_op jit(solution)/shard_map/ppermute | solution.py:459
  74.2 16.2 %collective-permute-start.25 = (bf16[192,256]{1,0:T(8,128)(2,1)S(1)}, bf16[192,256]{1,0:T(8,128)(2,1)S(1)}, u32[]{:S(2)}, u32[]{:S(2)}) collective-permute-start(bf16[192,256]{1,0:T(8,128)(2,1)S(1)} %get-tuple-element.48.refs_1_), channel_id=1, source_target_pairs={{0,2},{1,3},{2,0},{3,1},{4,6},{5,7},{6,4},{7,5},{8,10},{9,11},{10,... | collective-permute-start | bytes 294920 | tf_op jit(solution)/shard_map/ppermute | solution.py:459
  76.6 13.8 %collective-permute-start.26 = (bf16[192,256]{1,0:T(8,128)(2,1)S(1)}, bf16[192,256]{1,0:T(8,128)(2,1)S(1)}, u32[]{:S(2)}, u32[]{:S(2)}) collective-permute-start(bf16[192,256]{1,0:T(8,128)(2,1)S(1)} %get-tuple-element.48.refs_1_), channel_id=1, source_target_pairs={{0,3},{1,2},{2,1},{3,0},{4,7},{5,6},{6,5},{7,4},{8,11},{9,10},{10,... | collective-permute-start | bytes 294920 | tf_op jit(solution)/shard_map/ppermute | solution.py:459
  82.5 14.3 %collective-permute-start.21 = (bf16[192,256]{1,0:T(8,128)(2,1)S(1)}, bf16[192,256]{1,0:T(8,128)(2,1)S(1)}, u32[]{:S(2)}, u32[]{:S(2)}) collective-permute-start(bf16[192,256]{1,0:T(8,128)(2,1)S(1)} %get-tuple-element.43.refs_1_), channel_id=1, source_target_pairs={{0,1},{1,0},{2,3},{3,2},{4,5},{5,4},{6,7},{7,6},{8,9},{9,8},{10,11... | collective-permute-start | bytes 294920 | tf_op jit(solution)/shard_map/ppermute | solution.py:459
  88.0 8.9 %collective-permute-start.22 = (bf16[192,256]{1,0:T(8,128)(2,1)S(1)}, bf16[192,256]{1,0:T(8,128)(2,1)S(1)}, u32[]{:S(2)}, u32[]{:S(2)}) collective-permute-start(bf16[192,256]{1,0:T(8,128)(2,1)S(1)} %get-tuple-element.43.refs_1_), channel_id=1, source_target_pairs={{0,2},{1,3},{2,0},{3,1},{4,6},{5,7},{6,4},{7,5},{8,10},{9,11},{10,... | collective-permute-start | bytes 294920 | tf_op jit(solution)/shard_map/ppermute | solution.py:459
  88.6 8.2 %collective-permute-start.23 = (bf16[192,256]{1,0:T(8,128)(2,1)S(1)}, bf16[192,256]{1,0:T(8,128)(2,1)S(1)}, u32[]{:S(2)}, u32[]{:S(2)}) collective-permute-start(bf16[192,256]{1,0:T(8,128)(2,1)S(1)} %get-tuple-element.43.refs_1_), channel_id=1, source_target_pairs={{0,3},{1,2},{2,1},{3,0},{4,7},{5,6},{6,5},{7,4},{8,11},{9,10},{10,... | collective-permute-start | bytes 294920 | tf_op jit(solution)/shard_map/ppermute | solution.py:459

commit v6 on v5

--- a/solution.py
+++ b/solution.py
@@ -488,7 +488,8 @@
     near = tuple(range(0, cycle, 2))
     if paired:
         kvs = over_chips(kv, cycle)
-        parts = over_head(part, group)
+        parts = [part] + [lax.ppermute(part, "head", xor(group, j)) for j in (1, 2)]
+        parts.append(lax.ppermute(parts[2], "head", xor(group, 1)))
         (kvs,) = bundle([kvs], [w_up] + parts[1:3])
         kvs = [kvs, lax.ppermute(kvs, "blk", xor(cycle, 1))]
         sources = [(True, near), (True, tuple(s + 1 for s in near))]

time: 103 us -> 99.3 us (0.964)
  Pallas kernels: 42.7 us -> 38.7 us
  waiting for transfers between devices: 10.1 us -> 12.1 us
  starting transfers between devices: 45.6 us -> 43.8 us
    ppermute x18 -> x15, starting transfers between devices: 37.4 us -> 26.4 us  [over_head(): return [x] + [lax.ppermute(x, 'head', xor(size, j)) for j in range(1, size)]]
    ppermute x0 -> x3, starting transfers between devices: none -> 8.98 us  [the longest x1 4.62 us: on_device(): parts.append(lax.ppermute(parts[2], 'head', xor(group, 1)))]
    pallas_call x2, Pallas kernels: 8.62 us -> 4.6 us  [self_attention(): pl.pallas_call(placed(skipping(functools.partial(self_kernel, turn), 6, l...]
    ppermute x0 -> x3, waiting for transfers between devices: none -> 1.96 us  [the longest x1 1.13 us: on_device(): parts.append(lax.ppermute(parts[2], 'head', xor(group, 1)))]
    ppermute x18 -> x15, waiting for transfers between devices: 8.89 us -> 10.1 us  [over_head(): return [x] + [lax.ppermute(x, 'head', xor(size, j)) for j in range(1, size)]]
    ppermute x1, waiting for transfers between devices: 1.17 us -> 0.01 us  [on_device(): kvs = [kvs, lax.ppermute(kvs, 'blk', xor(cycle, 1))]]
  transfers between devices with their start and end apart: 27 -> 27, of which waited for: 5 -> 5; matrix products, arithmetic and copies ran while one was open for 0% -> 0% of each run, Pallas kernels for 35% -> 32%
where the time goes in v6:
time: 99.3 us; the launch traced here: 99.6 us
  starting transfers between devices  43.8 us (44%)
  Pallas kernels  38.7 us (39%)
  waiting for transfers between devices  12.1 us (12%)
  local copies, waits for them, and re-layouts  3.98 us (4%)
  between operations  1.05 us (1%)
    ppermute x15, starting transfers between devices, over_head(): return [x] + [lax.ppermute(x, 'head', xor(size, j)) for j in range(1, size)]  26.4 us
    pallas_call x2, Pallas kernels, mlp(): pl.pallas_call(placed(functools.partial(mlp_kernel, turn)), out_shape=(ja...  12.8 us
    ppermute x15, waiting for transfers between devices, over_head(): return [x] + [lax.ppermute(x, 'head', xor(size, j)) for j in range(1, size)]  10.1 us
    pallas_call x2, Pallas kernels, fetch(): pl.pallas_call(placed(skipping(functools.partial(fetch_kernel, cuts), 1 +...  9.65 us
    ppermute x6, starting transfers between devices, over_chips(): lax.ppermute(x, 'blk', xor(size, s))  7.8 us
    pallas_call x2, Pallas kernels, cross_attention(): pl.pallas_call(placed(functools.partial(cross_kernel, turn)), out_shape=(...  7.02 us
    ppermute x1, starting transfers between devices, on_device(): parts.append(lax.ppermute(parts[2], 'head', xor(group, 1)))  4.62 us
    pallas_call x2, Pallas kernels, self_attention(): pl.pallas_call(placed(skipping(functools.partial(self_kernel, turn), 6, l...  4.6 us
  transfers between devices with their start and end apart: 27, of which 5 were waited for; matrix products, arithmetic and copies ran while one was open for 0% of the time, Pallas kernels for 32%

profile of v6, /device:TPU:0, one launch (start us, length us, event | category | flops | bytes accessed | tf_op | source)
XLA Modules:
  0.0 99.6 jit_solution(2936876664660799322)
XLA Ops:
  0.6 3.1 %collective-permute-start = (bf16[96,1024]{1,0:T(8,128)(2,1)}, bf16[96,1024]{1,0:T(8,128)(2,1)S(1)}, u32[]{:S(2)}, u32[]{:S(2)}) collective-permute-start(bf16[96,1024]{1,0:T(8,128)(2,1)} %refs_0_.10), channel_id=1, source_target_pairs={{0,1},{1,0},{2,3},{3,2},{4,5},{5,4},{6,7},{7,6},{8,9},{9,8},{10,11... | collective-permute-start | bytes 589832 | tf_op jit(solution)/shard_map/ppermute | solution.py:459
  3.7 2.6 %collective-permute-start.1 = (bf16[96,1024]{1,0:T(8,128)(2,1)}, bf16[96,1024]{1,0:T(8,128)(2,1)S(1)}, u32[]{:S(2)}, u32[]{:S(2)}) collective-permute-start(bf16[96,1024]{1,0:T(8,128)(2,1)} %refs_0_.10), channel_id=1, source_target_pairs={{0,2},{1,3},{2,0},{3,1},{4,6},{5,7},{6,4},{7,5},{8,10},{9,11},{10,... | collective-permute-start | bytes 589832 | tf_op jit(solution)/shard_map/ppermute | solution.py:459
  6.3 1.7 %collective-permute-start.6 = (bf16[2,256,256]{2,1,0:T(8,128)(2,1)}, bf16[2,256,256]{2,1,0:T(8,128)(2,1)S(1)}, u32[]{:S(2)}, u32[]{:S(2)}) collective-permute-start(bf16[2,256,256]{2,1,0:T(8,128)(2,1)} %refs_0_.11), channel_id=1, source_target_pairs={{0,8},{4,12},{8,0},{12,4},{16,24},{20,28},{24,16},{28,20},{1,9},{5... | collective-permute-start | bytes 786440 | tf_op jit(solution)/shard_map/ppermute | solution.py:463
  8.0 1.5 %collective-permute-start.7 = (bf16[2,256,256]{2,1,0:T(8,128)(2,1)}, bf16[2,256,256]{2,1,0:T(8,128)(2,1)S(1)}, u32[]{:S(2)}, u32[]{:S(2)}) collective-permute-start(bf16[2,256,256]{2,1,0:T(8,128)(2,1)} %refs_0_.11), channel_id=1, source_target_pairs={{0,16},{4,20},{8,24},{12,28},{16,0},{20,4},{24,8},{28,12},{1,17},{... | collective-permute-start | bytes 786440 | tf_op jit(solution)/shard_map/ppermute | solution.py:463
  9.5 1.4 %copy-done.3 = bf16[3,1024,256]{2,1,0:T(8,128)(2,1)S(1)} copy-done((bf16[3,1024,256]{2,1,0:T(8,128)(2,1)S(1)}, bf16[3,1024,256]{2,1,0:T(8,128)(2,1)}, u32[]{:S(2)}) %copy-start.3) | copy-done | bytes 1572888
  11.0 1.0 %copy-done.4 = bf16[256,1024]{1,0:T(8,128)(2,1)S(1)} copy-done((bf16[256,1024]{1,0:T(8,128)(2,1)S(1)}, bf16[256,1024]{1,0:T(8,128)(2,1)}, u32[]{:S(2)}) %copy-start.4) | copy-done | bytes 524312
  12.0 0.9 copy-done.6
  12.9 0.4 fetch.2
  13.3 0.6 copy-done.5
  13.9 1.0 %collective-permute-start.8 = (bf16[2,256,256]{2,1,0:T(8,128)(2,1)S(1)}, bf16[2,256,256]{2,1,0:T(8,128)(2,1)S(1)}, u32[]{:S(2)}, u32[]{:S(2)}) collective-permute-start(bf16[2,256,256]{2,1,0:T(8,128)(2,1)S(1)} %copy-done.5), channel_id=1, source_target_pairs={{0,24},{4,28},{8,16},{12,20},{16,8},{20,12},{24,0},{28,4},{1,25},{... | collective-permute-start | bytes 786440 | tf_op jit(solution)/shard_map/ppermute | solution.py:463
  14.9 6.2 %collective-permute-done.1.refs_2_ = bf16[96,1024]{1,0:T(8,128)(2,1)S(1)} collective-permute-done((bf16[96,1024]{1,0:T(8,128)(2,1)}, bf16[96,1024]{1,0:T(8,128)(2,1)S(1)}, u32[]{:S(2)}, u32[]{:S(2)}) %collective-permute-start.1) | collective-permute-done | bytes 196640 | tf_op jit(solution)/shard_map/ppermute | solution.py:459
  21.1 0.8 project.1
  21.9 1.6 %collective-permute-start.3 = (bf16[2,384,256]{2,1,0:T(8,128)(2,1)S(1)}, bf16[2,384,256]{2,1,0:T(8,128)(2,1)S(1)}, u32[]{:S(2)}, u32[]{:S(2)}) collective-permute-start(bf16[2,384,256]{2,1,0:T(8,128)(2,1)S(1)} %get-tuple-element.33.refs_0_), channel_id=1, source_target_pairs={{0,8},{4,12},{8,0},{12,4},{16,24},{20,28},{24,16},{28,20},{1,9},{5... | collective-permute-start | bytes 1179656 | tf_op jit(solution)/shard_map/ppermute | solution.py:463
  23.5 1.5 %collective-permute-start.4 = (bf16[2,384,256]{2,1,0:T(8,128)(2,1)S(1)}, bf16[2,384,256]{2,1,0:T(8,128)(2,1)S(1)}, u32[]{:S(2)}, u32[]{:S(2)}) collective-permute-start(bf16[2,384,256]{2,1,0:T(8,128)(2,1)S(1)} %get-tuple-element.33.refs_0_), channel_id=1, source_target_pairs={{0,16},{4,20},{8,24},{12,28},{16,0},{20,4},{24,8},{28,12},{1,17},{... | collective-permute-start | bytes 1179656 | tf_op jit(solution)/shard_map/ppermute | solution.py:463
  25.0 0.5 collective-permute-start.5
  25.5 4.4 %collective-permute-start.10 = (bf16[128,1024]{1,0:T(8,128)(2,1)S(1)}, bf16[128,1024]{1,0:T(8,128)(2,1)S(1)}, u32[]{:S(2)}, u32[]{:S(2)}) collective-permute-start(bf16[128,1024]{1,0:T(8,128)(2,1)S(1)} %get-tuple-element.35.refs_0_), channel_id=1, source_target_pairs={{0,2},{1,3},{2,0},{3,1},{4,6},{5,7},{6,4},{7,5},{8,10},{9,11},{10,... | collective-permute-start | bytes 786440 | tf_op jit(solution)/shard_map/ppermute | solution.py:491
  29.9 0.1 bundle.3.refs_5_.refs_0_
  30.0 9.3 %fetch.3 = (bf16[1024,256]{1,0:T(8,128)(2,1)S(1)}, bf16[1024,1024]{1,0:T(8,128)(2,1)S(1)}, bf16[1024,4096]{1,0:T(8,128)(2,1)S(1)}, bf16[4096,1024]{1,0:T(8,128)(2,1)}, bf16[3,1024,256]{2,1,0:T(8,128)(2,1)S(1)}) custom-call(bf16[1024,1024]{1,0:T(8,128)(2,1)S(1)} %copy-done, bf16[1024,1024]{1,0:T(8,128)(2,1)S(1)} %copy-done.1, bf16[1024,4096]{1,0:T(8,128)(2,1)} %refs_2_.5, ...), custom_call_target="tpu_custom_call" | custom-call | bytes 1048576 | tf_op jit(solution)/shard_map/fetch/pallas_call | solution.py:125
  39.3 0.6 collective-permute-done.10.refs_6_.refs_2_
  39.9 0.2 collective-permute-done.9.refs_5_.refs_1_
  40.1 0.1 bundle.4.refs_1_
  40.2 0.1 collective-permute-start.11
  40.3 0.5 collective-permute-start.15
  40.8 4.6 %collective-permute-start.16 = (bf16[128,1024]{1,0:T(8,128)(2,1)S(1)}, bf16[128,1024]{1,0:T(8,128)(2,1)S(1)}, u32[]{:S(2)}, u32[]{:S(2)}) collective-permute-start(bf16[128,1024]{1,0:T(8,128)(2,1)S(1)} %collective-permute-done.10.refs_6_.refs_2_), channel_id=1, source_target_pairs={{0,1},{1,0},{2,3},{3,2},{4,5},{5,4},{6,7},{7,6},{8,9},{9,8},{10,11... | collective-permute-start | bytes 786440 | tf_op jit(solution)/shard_map/ppermute | solution.py:492
  45.4 2.6 %order.1 = (bf16[3072,256]{1,0:T(8,128)(2,1)S(1)}, bf16[2,144,3072]{2,1,0:T(8,128)(2,1)S(1)}, bf16[2,384,256]{2,1,0:T(8,128)(2,1)}) custom-call(s32[16]{0:T(128)S(1)} %copy-done.7, bf16[4,2,384,256]{3,2,1,0:T(8,128)(2,1)S(1)} %bundle.4.refs_1_, bf16[4,2,384,256]{3,2,1,0:T(8,128)(2,1)S(1)} %collective-permute-done.11.refs_2_), custom_call_target="tpu_custom_call" | custom-call | bytes 393216 | tf_op jit(solution)/shard_map/order/pallas_call | solution.py:189
  48.0 2.8 %self_attention.2.refs_5_.refs_4_.refs_3_ = bf16[192,256]{1,0:T(8,128)(2,1)S(1)} custom-call(s32[16]{0:T(128)S(1)} %copy-done.7, s32[9]{0:T(128)S(1)} %copy-done.8, bf16[384,256]{1,0:T(8,128)(2,1)S(1)} %get-tuple-element.32.refs_4_.refs_2_, bf16[3072,256]{1,0:T(8,128)(2,1)S(1)} %get-tuple-element.36.refs_3_, bf16[2,144,3072]{2,1,0:T(8,128)(2,1)S(1)} %get-tuple-element.37.refs_4_), custom_call_target="tpu_custom_call" | custom-call | flops 10000000000 | tf_op jit(solution)/shard_map/self_attention/pallas_call | solution.py:322
  50.8 1.1 %collective-permute-done.16.refs_3_ = bf16[128,1024]{1,0:T(8,128)(2,1)S(1)} collective-permute-done((bf16[128,1024]{1,0:T(8,128)(2,1)S(1)}, bf16[128,1024]{1,0:T(8,128)(2,1)S(1)}, u32[]{:S(2)}, u32[]{:S(2)}) %collective-permute-start.16) | collective-permute-done | bytes 262176 | tf_op jit(solution)/shard_map/ppermute | solution.py:492
  52.0 0.1 bundle.5.refs_2_
  52.1 0.1 collective-permute-start.17
  52.1 2.9 %collective-permute-start.18 = (bf16[192,256]{1,0:T(8,128)(2,1)S(1)}, bf16[192,256]{1,0:T(8,128)(2,1)S(1)}, u32[]{:S(2)}, u32[]{:S(2)}) collective-permute-start(bf16[192,256]{1,0:T(8,128)(2,1)S(1)} %self_attention.2.refs_5_.refs_4_.refs_3_), channel_id=1, source_target_pairs={{0,1},{1,0},{2,3},{3,2},{4,5},{5,4},{6,7},{7,6},{8,9},{9,8},{10,11... | collective-permute-start | bytes 294920 | tf_op jit(solution)/shard_map/ppermute | solution.py:459
  55.0 1.0 collective-permute-start.19
  56.0 1.5 %collective-permute-start.20 = (bf16[192,256]{1,0:T(8,128)(2,1)S(1)}, bf16[192,256]{1,0:T(8,128)(2,1)S(1)}, u32[]{:S(2)}, u32[]{:S(2)}) collective-permute-start(bf16[192,256]{1,0:T(8,128)(2,1)S(1)} %self_attention.2.refs_5_.refs_4_.refs_3_), channel_id=1, source_target_pairs={{0,3},{1,2},{2,1},{3,0},{4,7},{5,6},{6,5},{7,4},{8,11},{9,10},{10,... | collective-permute-start | bytes 294920 | tf_op jit(solution)/shard_map/ppermute | solution.py:459
  57.5 1.8 %self_attention.3.refs_4_.refs_3_ = bf16[192,256]{1,0:T(8,128)(2,1)S(1)} custom-call(s32[16]{0:T(128)S(1)} %copy-done.7, s32[9]{0:T(128)S(1)} %copy-done.8, bf16[384,256]{1,0:T(8,128)(2,1)S(1)} %get-tuple-element.32.refs_4_.refs_2_, bf16[3072,256]{1,0:T(8,128)(2,1)S(1)} %get-tuple-element.36.refs_3_, bf16[2,144,3072]{2,1,0:T(8,128)(2,1)S(1)} %get-tuple-element.37.refs_4_, ...), custom_call_target="tpu_custom_call" | custom-call | flops 10000000000 | tf_op jit(solution)/shard_map/self_attention/pallas_call | solution.py:322
  59.3 1.1 %collective-permute-start.12 = (bf16[192,256]{1,0:T(8,128)(2,1)S(1)}, bf16[192,256]{1,0:T(8,128)(2,1)S(1)}, u32[]{:S(2)}, u32[]{:S(2)}) collective-permute-start(bf16[192,256]{1,0:T(8,128)(2,1)S(1)} %self_attention.3.refs_4_.refs_3_), channel_id=1, source_target_pairs={{0,1},{1,0},{2,3},{3,2},{4,5},{5,4},{6,7},{7,6},{8,9},{9,8},{10,11... | collective-permute-start | bytes 294920 | tf_op jit(solution)/shard_map/ppermute | solution.py:459
  60.4 1.9 %collective-permute-start.13 = (bf16[192,256]{1,0:T(8,128)(2,1)S(1)}, bf16[192,256]{1,0:T(8,128)(2,1)S(1)}, u32[]{:S(2)}, u32[]{:S(2)}) collective-permute-start(bf16[192,256]{1,0:T(8,128)(2,1)S(1)} %self_attention.3.refs_4_.refs_3_), channel_id=1, source_target_pairs={{0,2},{1,3},{2,0},{3,1},{4,6},{5,7},{6,4},{7,5},{8,10},{9,11},{10,... | collective-permute-start | bytes 294920 | tf_op jit(solution)/shard_map/ppermute | solution.py:459
  62.3 3.9 %collective-permute-done.19.refs_6_.refs_5_ = bf16[192,256]{1,0:T(8,128)(2,1)S(1)} collective-permute-done((bf16[192,256]{1,0:T(8,128)(2,1)S(1)}, bf16[192,256]{1,0:T(8,128)(2,1)S(1)}, u32[]{:S(2)}, u32[]{:S(2)}) %collective-permute-start.19) | collective-permute-done | bytes 98336 | tf_op jit(solution)/shard_map/ppermute | solution.py:459
  66.1 1.5 %collective-permute-start.14 = (bf16[192,256]{1,0:T(8,128)(2,1)S(1)}, bf16[192,256]{1,0:T(8,128)(2,1)S(1)}, u32[]{:S(2)}, u32[]{:S(2)}) collective-permute-start(bf16[192,256]{1,0:T(8,128)(2,1)S(1)} %self_attention.3.refs_4_.refs_3_), channel_id=1, source_target_pairs={{0,3},{1,2},{2,1},{3,0},{4,7},{5,6},{6,5},{7,4},{8,11},{9,10},{10,... | collective-permute-start | bytes 294920 | tf_op jit(solution)/shard_map/ppermute | solution.py:459
  67.7 1.0 prepare.1
  68.7 2.9 %cross_attention.3 = (f32[192,1024]{1,0:T(8,128)S(1)}, bf16[192,256]{1,0:T(8,128)(2,1)S(1)}) custom-call(s32[16]{0:T(128)S(1)} %copy-done.7, s32[9]{0:T(128)S(1)} %copy-done.8, s32[9]{0:T(128)S(1)} %copy-done.9, bf16[192,256]{1,0:T(8,128)(2,1)S(1)} %self_attention.2.refs_5_.refs_4_.refs_3_, bf16[192,256]{1,0:T(8,128)(2,1)S(1)} %collective-permute-done.18.refs_5_.refs_4_, ...), custom_call_target="tpu_custom_call" | custom-call | flops 10000000000 | tf_op jit(solution)/shard_map/cross_attention/pallas_call | solution.py:370
  71.7 3.9 %collective-permute-start.24 = (bf16[192,256]{1,0:T(8,128)(2,1)S(1)}, bf16[192,256]{1,0:T(8,128)(2,1)S(1)}, u32[]{:S(2)}, u32[]{:S(2)}) collective-permute-start(bf16[192,256]{1,0:T(8,128)(2,1)S(1)} %get-tuple-element.48.refs_1_), channel_id=1, source_target_pairs={{0,1},{1,0},{2,3},{3,2},{4,5},{5,4},{6,7},{7,6},{8,9},{9,8},{10,11... | collective-permute-start | bytes 294920 | tf_op jit(solution)/shard_map/ppermute | solution.py:459
  75.6 0.6 collective-permute-start.25
  76.2 1.9 %collective-permute-start.26 = (bf16[192,256]{1,0:T(8,128)(2,1)S(1)}, bf16[192,256]{1,0:T(8,128)(2,1)S(1)}, u32[]{:S(2)}, u32[]{:S(2)}) collective-permute-start(bf16[192,256]{1,0:T(8,128)(2,1)S(1)} %get-tuple-element.48.refs_1_), channel_id=1, source_target_pairs={{0,3},{1,2},{2,1},{3,0},{4,7},{5,6},{6,5},{7,4},{8,11},{9,10},{10,... | collective-permute-start | bytes 294920 | tf_op jit(solution)/shard_map/ppermute | solution.py:459
  78.1 4.1 %cross_attention.2 = (f32[192,1024]{1,0:T(8,128)S(1)}, bf16[192,256]{1,0:T(8,128)(2,1)S(1)}) custom-call(s32[16]{0:T(128)S(1)} %copy-done.7, s32[9]{0:T(128)S(1)} %copy-done.8, s32[9]{0:T(128)S(1)} %copy-done.9, bf16[192,256]{1,0:T(8,128)(2,1)S(1)} %self_attention.3.refs_4_.refs_3_, bf16[192,256]{1,0:T(8,128)(2,1)S(1)} %collective-permute-done.12.refs_4_, ...), custom_call_target="tpu_custom_call" | custom-call | flops 10000000000 | tf_op jit(solution)/shard_map/cross_attention/pallas_call | solution.py:370
  82.2 1.1 %collective-permute-start.21 = (bf16[192,256]{1,0:T(8,128)(2,1)S(1)}, bf16[192,256]{1,0:T(8,128)(2,1)S(1)}, u32[]{:S(2)}, u32[]{:S(2)}) collective-permute-start(bf16[192,256]{1,0:T(8,128)(2,1)S(1)} %get-tuple-element.43.refs_1_), channel_id=1, source_target_pairs={{0,1},{1,0},{2,3},{3,2},{4,5},{5,4},{6,7},{7,6},{8,9},{9,8},{10,11... | collective-permute-start | bytes 294920 | tf_op jit(solution)/shard_map/ppermute | solution.py:459
  83.3 1.4 %collective-permute-start.22 = (bf16[192,256]{1,0:T(8,128)(2,1)S(1)}, bf16[192,256]{1,0:T(8,128)(2,1)S(1)}, u32[]{:S(2)}, u32[]{:S(2)}) collective-permute-start(bf16[192,256]{1,0:T(8,128)(2,1)S(1)} %get-tuple-element.43.refs_1_), channel_id=1, source_target_pairs={{0,2},{1,3},{2,0},{3,1},{4,6},{5,7},{6,4},{7,5},{8,10},{9,11},{10,... | collective-permute-start | bytes 294920 | tf_op jit(solution)/shard_map/ppermute | solution.py:459
  84.7 1.9 %collective-permute-start.23 = (bf16[192,256]{1,0:T(8,128)(2,1)S(1)}, bf16[192,256]{1,0:T(8,128)(2,1)S(1)}, u32[]{:S(2)}, u32[]{:S(2)}) collective-permute-start(bf16[192,256]{1,0:T(8,128)(2,1)S(1)} %get-tuple-element.43.refs_1_), channel_id=1, source_target_pairs={{0,3},{1,2},{2,1},{3,0},{4,7},{5,6},{6,5},{7,4},{8,11},{9,10},{10,... | collective-permute-start | bytes 294920 | tf_op jit(solution)/shard_map/ppermute | solution.py:459
  86.6 6.4 %mlp.2 = (f32[96,1024]{1,0:T(8,128)}, f32[3,384,256]{2,1,0:T(8,128)}) custom-call(s32[16]{0:T(128)S(1)} %copy-done.7, bf16[192,256]{1,0:T(8,128)(2,1)S(1)} %get-tuple-element.48.refs_1_, bf16[192,256]{1,0:T(8,128)(2,1)S(1)} %collective-permute-done.24.refs_2_, bf16[192,256]{1,0:T(8,128)(2,1)S(1)} %collective-permute-done.25.refs_3_, ...), custom_call_target="tpu_custom_call" | custom-call | flops 300000000 | tf_op jit(solution)/shard_map/mlp/pallas_call | solution.py:437
  93.1 6.4 %mlp.3 = (f32[96,1024]{1,0:T(8,128)}, f32[3,384,256]{2,1,0:T(8,128)}) custom-call(s32[16]{0:T(128)S(1)} %copy-done.7, bf16[192,256]{1,0:T(8,128)(2,1)S(1)} %get-tuple-element.43.refs_1_, bf16[192,256]{1,0:T(8,128)(2,1)S(1)} %collective-permute-done.21.refs_2_, ...), custom_call_target="tpu_custom_call", output_to_operand_aliasing={{0}: (10, {}), {1}: (11, {})} | custom-call | flops 300000000 | tf_op jit(solution)/shard_map/mlp/pallas_call | solution.py:437
  (45 shorter events, 0.1 us)
Async XLA Ops:
  0.6 12.7 %collective-permute-start = (bf16[96,1024]{1,0:T(8,128)(2,1)}, bf16[96,1024]{1,0:T(8,128)(2,1)S(1)}, u32[]{:S(2)}, u32[]{:S(2)}) collective-permute-start(bf16[96,1024]{1,0:T(8,128)(2,1)} %refs_0_.10), channel_id=1, source_target_pairs={{0,1},{1,0},{2,3},{3,2},{4,5},{5,4},{6,7},{7,6},{8,9},{9,8},{10,11... | collective-permute-start | bytes 589832 | tf_op jit(solution)/shard_map/ppermute | solution.py:459
  3.7 17.4 %collective-permute-start.1 = (bf16[96,1024]{1,0:T(8,128)(2,1)}, bf16[96,1024]{1,0:T(8,128)(2,1)S(1)}, u32[]{:S(2)}, u32[]{:S(2)}) collective-permute-start(bf16[96,1024]{1,0:T(8,128)(2,1)} %refs_0_.10), channel_id=1, source_target_pairs={{0,2},{1,3},{2,0},{3,1},{4,6},{5,7},{6,4},{7,5},{8,10},{9,11},{10,... | collective-permute-start | bytes 589832 | tf_op jit(solution)/shard_map/ppermute | solution.py:459
  6.3 14.8 %collective-permute-start.2 = (bf16[96,1024]{1,0:T(8,128)(2,1)}, bf16[96,1024]{1,0:T(8,128)(2,1)S(1)}, u32[]{:S(2)}, u32[]{:S(2)}) collective-permute-start(bf16[96,1024]{1,0:T(8,128)(2,1)} %refs_0_.10), channel_id=1, source_target_pairs={{0,3},{1,2},{2,1},{3,0},{4,7},{5,6},{6,5},{7,4},{8,11},{9,10},{10,... | collective-permute-start | bytes 589832 | tf_op jit(solution)/shard_map/ppermute | solution.py:459
  6.3 18.7 %collective-permute-start.6 = (bf16[2,256,256]{2,1,0:T(8,128)(2,1)}, bf16[2,256,256]{2,1,0:T(8,128)(2,1)S(1)}, u32[]{:S(2)}, u32[]{:S(2)}) collective-permute-start(bf16[2,256,256]{2,1,0:T(8,128)(2,1)} %refs_0_.11), channel_id=1, source_target_pairs={{0,8},{4,12},{8,0},{12,4},{16,24},{20,28},{24,16},{28,20},{1,9},{5... | collective-permute-start | bytes 786440 | tf_op jit(solution)/shard_map/ppermute | solution.py:463
  8.0 17.5 %collective-permute-start.7 = (bf16[2,256,256]{2,1,0:T(8,128)(2,1)}, bf16[2,256,256]{2,1,0:T(8,128)(2,1)S(1)}, u32[]{:S(2)}, u32[]{:S(2)}) collective-permute-start(bf16[2,256,256]{2,1,0:T(8,128)(2,1)} %refs_0_.11), channel_id=1, source_target_pairs={{0,16},{4,20},{8,24},{12,28},{16,0},{20,4},{24,8},{28,12},{1,17},{... | collective-permute-start | bytes 786440 | tf_op jit(solution)/shard_map/ppermute | solution.py:463
  9.5 1.4 %copy-start.3 = (bf16[3,1024,256]{2,1,0:T(8,128)(2,1)S(1)}, bf16[3,1024,256]{2,1,0:T(8,128)(2,1)}, u32[]{:S(2)}) copy-start(bf16[3,1024,256]{2,1,0:T(8,128)(2,1)} %refs_1_.6) | copy-start | bytes 4718596
  11.0 1.0 %copy-start.4 = (bf16[256,1024]{1,0:T(8,128)(2,1)S(1)}, bf16[256,1024]{1,0:T(8,128)(2,1)}, u32[]{:S(2)}) copy-start(bf16[256,1024]{1,0:T(8,128)(2,1)} %refs_2_.4) | copy-start | bytes 1572868
  12.0 0.9 copy-start.6
  12.9 0.9 copy-start.5
  13.9 16.0 %collective-permute-start.8 = (bf16[2,256,256]{2,1,0:T(8,128)(2,1)S(1)}, bf16[2,256,256]{2,1,0:T(8,128)(2,1)S(1)}, u32[]{:S(2)}, u32[]{:S(2)}) collective-permute-start(bf16[2,256,256]{2,1,0:T(8,128)(2,1)S(1)} %copy-done.5), channel_id=1, source_target_pairs={{0,24},{4,28},{8,16},{12,20},{16,8},{20,12},{24,0},{28,4},{1,25},{... | collective-permute-start | bytes 786440 | tf_op jit(solution)/shard_map/ppermute | solution.py:463
  21.1 8.9 %copy-start.1 = (bf16[1024,1024]{1,0:T(8,128)(2,1)S(1)}, bf16[1024,1024]{1,0:T(8,128)(2,1)}, u32[]{:S(2)}) copy-start(bf16[1024,1024]{1,0:T(8,128)(2,1)} %refs_1_.7) | copy-start | bytes 6291460
  21.1 8.9 %copy-start.2 = (bf16[3,1024,256]{2,1,0:T(8,128)(2,1)S(1)}, bf16[3,1024,256]{2,1,0:T(8,128)(2,1)}, u32[]{:S(2)}) copy-start(bf16[3,1024,256]{2,1,0:T(8,128)(2,1)} %refs_4_.1) | copy-start | bytes 4718596
  21.9 8.0 %copy-start = (bf16[1024,1024]{1,0:T(8,128)(2,1)S(1)}, bf16[1024,1024]{1,0:T(8,128)(2,1)}, u32[]{:S(2)}) copy-start(bf16[1024,1024]{1,0:T(8,128)(2,1)} %refs_0_.12) | copy-start | bytes 6291460
  21.9 18.2 %collective-permute-start.3 = (bf16[2,384,256]{2,1,0:T(8,128)(2,1)S(1)}, bf16[2,384,256]{2,1,0:T(8,128)(2,1)S(1)}, u32[]{:S(2)}, u32[]{:S(2)}) collective-permute-start(bf16[2,384,256]{2,1,0:T(8,128)(2,1)S(1)} %get-tuple-element.33.refs_0_), channel_id=1, source_target_pairs={{0,8},{4,12},{8,0},{12,4},{16,24},{20,28},{24,16},{28,20},{1,9},{5... | collective-permute-start | bytes 1179656 | tf_op jit(solution)/shard_map/ppermute | solution.py:463
  23.5 16.6 %collective-permute-start.4 = (bf16[2,384,256]{2,1,0:T(8,128)(2,1)S(1)}, bf16[2,384,256]{2,1,0:T(8,128)(2,1)S(1)}, u32[]{:S(2)}, u32[]{:S(2)}) collective-permute-start(bf16[2,384,256]{2,1,0:T(8,128)(2,1)S(1)} %get-tuple-element.33.refs_0_), channel_id=1, source_target_pairs={{0,16},{4,20},{8,24},{12,28},{16,0},{20,4},{24,8},{28,12},{1,17},{... | collective-permute-start | bytes 1179656 | tf_op jit(solution)/shard_map/ppermute | solution.py:463
  25.0 15.1 %collective-permute-start.5 = (bf16[2,384,256]{2,1,0:T(8,128)(2,1)S(1)}, bf16[2,384,256]{2,1,0:T(8,128)(2,1)S(1)}, u32[]{:S(2)}, u32[]{:S(2)}) collective-permute-start(bf16[2,384,256]{2,1,0:T(8,128)(2,1)S(1)} %get-tuple-element.33.refs_0_), channel_id=1, source_target_pairs={{0,24},{4,28},{8,16},{12,20},{16,8},{20,12},{24,0},{28,4},{1,25},{... | collective-permute-start | bytes 1179656 | tf_op jit(solution)/shard_map/ppermute | solution.py:463
  25.5 14.4 %collective-permute-start.10 = (bf16[128,1024]{1,0:T(8,128)(2,1)S(1)}, bf16[128,1024]{1,0:T(8,128)(2,1)S(1)}, u32[]{:S(2)}, u32[]{:S(2)}) collective-permute-start(bf16[128,1024]{1,0:T(8,128)(2,1)S(1)} %get-tuple-element.35.refs_0_), channel_id=1, source_target_pairs={{0,2},{1,3},{2,0},{3,1},{4,6},{5,7},{6,4},{7,5},{8,10},{9,11},{10,... | collective-permute-start | bytes 786440 | tf_op jit(solution)/shard_map/ppermute | solution.py:491
  29.9 10.2 %collective-permute-start.9 = (bf16[128,1024]{1,0:T(8,128)(2,1)S(1)}, bf16[128,1024]{1,0:T(8,128)(2,1)S(1)}, u32[]{:S(2)}, u32[]{:S(2)}) collective-permute-start(bf16[128,1024]{1,0:T(8,128)(2,1)S(1)} %get-tuple-element.35.refs_0_), channel_id=1, source_target_pairs={{0,1},{1,0},{2,3},{3,2},{4,5},{5,4},{6,7},{7,6},{8,9},{9,8},{10,11... | collective-permute-start | bytes 786440 | tf_op jit(solution)/shard_map/ppermute | solution.py:491
  40.1 5.3 %copy-start.7 = (s32[16]{0:T(128)S(1)}, s32[16]{0:T(128)}, u32[]{:S(2)}) copy-start(s32[16]{0:T(128)} %refs_0_.19) | copy-start | bytes 196
  40.2 7.8 %copy-start.8 = (s32[9]{0:T(128)S(1)}, s32[9]{0:T(128)}, u32[]{:S(2)}) copy-start(s32[9]{0:T(128)} %refs_1_.11) | copy-start | bytes 112
  40.2 5.2 %collective-permute-start.11 = (bf16[4,2,384,256]{3,2,1,0:T(8,128)(2,1)S(1)}, bf16[4,2,384,256]{3,2,1,0:T(8,128)(2,1)S(1)}, u32[]{:S(2)}, u32[]{:S(2)}) collective-permute-start(bf16[4,2,384,256]{3,2,1,0:T(8,128)(2,1)S(1)} %bundle.4.refs_1_), channel_id=1, source_target_pairs={{0,4},{4,0},{8,12},{12,8},{16,20},{20,16},{24,28},{28,24},{1,5},{5... | collective-permute-start | bytes 4718600 | tf_op jit(solution)/shard_map/ppermute | solution.py:494
  40.3 19.0 %collective-permute-start.15 = (bf16[4,2,256,256]{3,2,1,0:T(8,128)(2,1)S(1)}, bf16[4,2,256,256]{3,2,1,0:T(8,128)(2,1)S(1)}, u32[]{:S(2)}, u32[]{:S(2)}) collective-permute-start(bf16[4,2,256,256]{3,2,1,0:T(8,128)(2,1)S(1)} %bundle.3.refs_5_.refs_0_), channel_id=1, source_target_pairs={{0,4},{4,0},{8,12},{12,8},{16,20},{20,16},{24,28},{28,24},{1,5},{5... | collective-permute-start | bytes 3145736 | tf_op jit(solution)/shard_map/ppermute | solution.py:508
  40.8 11.2 %collective-permute-start.16 = (bf16[128,1024]{1,0:T(8,128)(2,1)S(1)}, bf16[128,1024]{1,0:T(8,128)(2,1)S(1)}, u32[]{:S(2)}, u32[]{:S(2)}) collective-permute-start(bf16[128,1024]{1,0:T(8,128)(2,1)S(1)} %collective-permute-done.10.refs_6_.refs_2_), channel_id=1, source_target_pairs={{0,1},{1,0},{2,3},{3,2},{4,5},{5,4},{6,7},{7,6},{8,9},{9,8},{10,11... | collective-permute-start | bytes 786440 | tf_op jit(solution)/shard_map/ppermute | solution.py:492
  52.1 15.6 %collective-permute-start.17 = (bf16[4,128,1024]{2,1,0:T(8,128)(2,1)S(1)}, bf16[4,128,1024]{2,1,0:T(8,128)(2,1)S(1)}, u32[]{:S(2)}, u32[]{:S(2)}) collective-permute-start(bf16[4,128,1024]{2,1,0:T(8,128)(2,1)S(1)} %bundle.5.refs_2_), channel_id=1, source_target_pairs={{0,4},{4,0},{8,12},{12,8},{16,20},{20,16},{24,28},{28,24},{1,5},{5... | collective-permute-start | bytes 3145736 | tf_op jit(solution)/shard_map/ppermute | solution.py:508
  52.1 8.3 %collective-permute-start.18 = (bf16[192,256]{1,0:T(8,128)(2,1)S(1)}, bf16[192,256]{1,0:T(8,128)(2,1)S(1)}, u32[]{:S(2)}, u32[]{:S(2)}) collective-permute-start(bf16[192,256]{1,0:T(8,128)(2,1)S(1)} %self_attention.2.refs_5_.refs_4_.refs_3_), channel_id=1, source_target_pairs={{0,1},{1,0},{2,3},{3,2},{4,5},{5,4},{6,7},{7,6},{8,9},{9,8},{10,11... | collective-permute-start | bytes 294920 | tf_op jit(solution)/shard_map/ppermute | solution.py:459
  55.0 11.1 %collective-permute-start.19 = (bf16[192,256]{1,0:T(8,128)(2,1)S(1)}, bf16[192,256]{1,0:T(8,128)(2,1)S(1)}, u32[]{:S(2)}, u32[]{:S(2)}) collective-permute-start(bf16[192,256]{1,0:T(8,128)(2,1)S(1)} %self_attention.2.refs_5_.refs_4_.refs_3_), channel_id=1, source_target_pairs={{0,2},{1,3},{2,0},{3,1},{4,6},{5,7},{6,4},{7,5},{8,10},{9,11},{10,... | collective-permute-start | bytes 294920 | tf_op jit(solution)/shard_map/ppermute | solution.py:459
  56.0 11.7 %collective-permute-start.20 = (bf16[192,256]{1,0:T(8,128)(2,1)S(1)}, bf16[192,256]{1,0:T(8,128)(2,1)S(1)}, u32[]{:S(2)}, u32[]{:S(2)}) collective-permute-start(bf16[192,256]{1,0:T(8,128)(2,1)S(1)} %self_attention.2.refs_5_.refs_4_.refs_3_), channel_id=1, source_target_pairs={{0,3},{1,2},{2,1},{3,0},{4,7},{5,6},{6,5},{7,4},{8,11},{9,10},{10,... | collective-permute-start | bytes 294920 | tf_op jit(solution)/shard_map/ppermute | solution.py:459
  59.3 9.4 %copy-start.9 = (s32[9]{0:T(128)S(1)}, s32[9]{0:T(128)}, u32[]{:S(2)}) copy-start(s32[9]{0:T(128)} %refs_2_.7) | copy-start | bytes 112
  59.3 16.9 %collective-permute-start.12 = (bf16[192,256]{1,0:T(8,128)(2,1)S(1)}, bf16[192,256]{1,0:T(8,128)(2,1)S(1)}, u32[]{:S(2)}, u32[]{:S(2)}) collective-permute-start(bf16[192,256]{1,0:T(8,128)(2,1)S(1)} %self_attention.3.refs_4_.refs_3_), channel_id=1, source_target_pairs={{0,1},{1,0},{2,3},{3,2},{4,5},{5,4},{6,7},{7,6},{8,9},{9,8},{10,11... | collective-permute-start | bytes 294920 | tf_op jit(solution)/shard_map/ppermute | solution.py:459
  60.4 17.6 %collective-permute-start.13 = (bf16[192,256]{1,0:T(8,128)(2,1)S(1)}, bf16[192,256]{1,0:T(8,128)(2,1)S(1)}, u32[]{:S(2)}, u32[]{:S(2)}) collective-permute-start(bf16[192,256]{1,0:T(8,128)(2,1)S(1)} %self_attention.3.refs_4_.refs_3_), channel_id=1, source_target_pairs={{0,2},{1,3},{2,0},{3,1},{4,6},{5,7},{6,4},{7,5},{8,10},{9,11},{10,... | collective-permute-start | bytes 294920 | tf_op jit(solution)/shard_map/ppermute | solution.py:459
  66.1 11.9 %collective-permute-start.14 = (bf16[192,256]{1,0:T(8,128)(2,1)S(1)}, bf16[192,256]{1,0:T(8,128)(2,1)S(1)}, u32[]{:S(2)}, u32[]{:S(2)}) collective-permute-start(bf16[192,256]{1,0:T(8,128)(2,1)S(1)} %self_attention.3.refs_4_.refs_3_), channel_id=1, source_target_pairs={{0,3},{1,2},{2,1},{3,0},{4,7},{5,6},{6,5},{7,4},{8,11},{9,10},{10,... | collective-permute-start | bytes 294920 | tf_op jit(solution)/shard_map/ppermute | solution.py:459
  71.6 15.0 %slice-start = ((s8[8388608]{0:T(1024)(128)(4,1)}), s8[4194304]{0:T(1024)(128)(4,1)S(1)}, s32[]{:S(2)}) async-start(s8[8388608]{0:T(1024)(128)(4,1)} %bitcast.1), calls=%async_computation | async-start | bytes 8388608
  71.7 15.0 %slice-start.1 = ((s8[8388608]{0:T(1024)(128)(4,1)}), s8[4194304]{0:T(1024)(128)(4,1)S(1)}, s32[]{:S(2)}) async-start(s8[8388608]{0:T(1024)(128)(4,1)} %bitcast.1), calls=%async_computation.1 | async-start | bytes 8388608
  71.7 13.1 %collective-permute-start.24 = (bf16[192,256]{1,0:T(8,128)(2,1)S(1)}, bf16[192,256]{1,0:T(8,128)(2,1)S(1)}, u32[]{:S(2)}, u32[]{:S(2)}) collective-permute-start(bf16[192,256]{1,0:T(8,128)(2,1)S(1)} %get-tuple-element.48.refs_1_), channel_id=1, source_target_pairs={{0,1},{1,0},{2,3},{3,2},{4,5},{5,4},{6,7},{7,6},{8,9},{9,8},{10,11... | collective-permute-start | bytes 294920 | tf_op jit(solution)/shard_map/ppermute | solution.py:459
  75.6 11.0 %collective-permute-start.25 = (bf16[192,256]{1,0:T(8,128)(2,1)S(1)}, bf16[192,256]{1,0:T(8,128)(2,1)S(1)}, u32[]{:S(2)}, u32[]{:S(2)}) collective-permute-start(bf16[192,256]{1,0:T(8,128)(2,1)S(1)} %get-tuple-element.48.refs_1_), channel_id=1, source_target_pairs={{0,2},{1,3},{2,0},{3,1},{4,6},{5,7},{6,4},{7,5},{8,10},{9,11},{10,... | collective-permute-start | bytes 294920 | tf_op jit(solution)/shard_map/ppermute | solution.py:459
  76.2 10.5 %collective-permute-start.26 = (bf16[192,256]{1,0:T(8,128)(2,1)S(1)}, bf16[192,256]{1,0:T(8,128)(2,1)S(1)}, u32[]{:S(2)}, u32[]{:S(2)}) collective-permute-start(bf16[192,256]{1,0:T(8,128)(2,1)S(1)} %get-tuple-element.48.refs_1_), channel_id=1, source_target_pairs={{0,3},{1,2},{2,1},{3,0},{4,7},{5,6},{6,5},{7,4},{8,11},{9,10},{10,... | collective-permute-start | bytes 294920 | tf_op jit(solution)/shard_map/ppermute | solution.py:459
  82.2 10.9 %collective-permute-start.21 = (bf16[192,256]{1,0:T(8,128)(2,1)S(1)}, bf16[192,256]{1,0:T(8,128)(2,1)S(1)}, u32[]{:S(2)}, u32[]{:S(2)}) collective-permute-start(bf16[192,256]{1,0:T(8,128)(2,1)S(1)} %get-tuple-element.43.refs_1_), channel_id=1, source_target_pairs={{0,1},{1,0},{2,3},{3,2},{4,5},{5,4},{6,7},{7,6},{8,9},{9,8},{10,11... | collective-permute-start | bytes 294920 | tf_op jit(solution)/shard_map/ppermute | solution.py:459
  83.3 9.8 %collective-permute-start.22 = (bf16[192,256]{1,0:T(8,128)(2,1)S(1)}, bf16[192,256]{1,0:T(8,128)(2,1)S(1)}, u32[]{:S(2)}, u32[]{:S(2)}) collective-permute-start(bf16[192,256]{1,0:T(8,128)(2,1)S(1)} %get-tuple-element.43.refs_1_), channel_id=1, source_target_pairs={{0,2},{1,3},{2,0},{3,1},{4,6},{5,7},{6,4},{7,5},{8,10},{9,11},{10,... | collective-permute-start | bytes 294920 | tf_op jit(solution)/shard_map/ppermute | solution.py:459
  84.7 8.3 %collective-permute-start.23 = (bf16[192,256]{1,0:T(8,128)(2,1)S(1)}, bf16[192,256]{1,0:T(8,128)(2,1)S(1)}, u32[]{:S(2)}, u32[]{:S(2)}) collective-permute-start(bf16[192,256]{1,0:T(8,128)(2,1)S(1)} %get-tuple-element.43.refs_1_), channel_id=1, source_target_pairs={{0,3},{1,2},{2,1},{3,0},{4,7},{5,6},{6,5},{7,4},{8,11},{9,10},{10,... | collective-permute-start | bytes 294920 | tf_op jit(solution)/shard_map/ppermute | solution.py:459
